TPU v7x, 32 devices: a whole 2x2x4 slice. The times are simulated.
32 devices in a mesh: layer: 8 (over z, y), lat: 4 (over x, core).
Axes of the slice: x: 2, y: 2, z: 4, core: 2. Of those that a mesh axis runs over, the one named last changes fastest.
Arguments:
- inputs: bfloat16 [128, 2, 2048], P(None, None, 'layer'), may hold values from -6 to 6
- encoder: bfloat16 [2, 2048, 4096], P(None, 'layer', 'lat'), may hold values from -0.125 to 0.125
- enc_bias: float32 [2, 4096], P(None, 'lat'), may hold values from -3 to 3
- decoder: bfloat16 [8, 3, 4096, 256], P('layer', None, 'lat'), may hold values from -0.5 to 0.5
- dec_bias: float32 [8, 2, 256], P('layer'), may hold values from -3 to 3
- targets: bfloat16 [8, 128, 2, 256], P('layer'), may hold values from -6 to 6
- top_index: int32 [128, 2, 64], replicated, may hold values from 0 to 4095, as said below
Outputs:
- decoder_grad: float32 [8, 3, 4096, 256], P('layer', None, 'lat')
- encoder_grad: float32 [2, 2048, 4096], P(None, 'layer', 'lat')
- bias_grad: float32 [2, 4096], P(None, 'lat')
Inputs may be any that keep to these rules, and one draw needn't show every extreme that they name: `top_index`: the 64 entries of one token and layer are distinct; at most 32 of them have the same value of n // 1024, and every value of n // 1024 is taken by exactly 32 entries of some token and layer.
All inputs are finite; a program needn't handle non-finite values.
Results may differ from a plain program's by a relative error of at most 0.0045.
Values may be sent and summed in bfloat16 or wider, within the bound.
No kernel may reach another device: no remote copies, remote signals or barrier semaphores. Data moves between devices by JAX's collectives and lax.ppermute only.
A program may use at most 64 MiB of HBM per device.

v0:
```python
import jax
import jax.numpy as jnp
from jax import lax
from jax.sharding import PartitionSpec as P

FEAT_SPLIT = 8


def pick_rows(weight_table, row_index):
    return jnp.take(weight_table, row_index, axis=0)


def body(inputs, encoder, enc_bias, decoder, dec_bias, targets, top_index):
    tokens, layers, top_count = top_index.shape
    slab_width = encoder.shape[2]
    slab_most = 2 * top_count // lax.axis_size("lat")
    pair_index = lax.axis_index("layer") // FEAT_SPLIT
    slab_index = lax.axis_index("lat")
    blocks = decoder.shape[1]
    decoder_own = decoder[0]
    local_index = top_index - slab_index * slab_width
    inside = (local_index >= 0) & (local_index < slab_width)
    position_ids = lax.broadcasted_iota(jnp.int32, top_index.shape, 2)
    order_key = jnp.where(inside, 2 * top_count, top_count) - position_ids
    slot_key, position = lax.top_k(order_key, slab_most)
    valid_slot = slot_key > top_count
    picked = jnp.take_along_axis(jnp.where(inside, local_index, 0), position, axis=2)
    encoder_rows = jnp.swapaxes(encoder, 1, 2)
    columns = jax.vmap(pick_rows, in_axes=(0, 1), out_axes=1)(encoder_rows, picked)
    partial_value = jnp.einsum("tld,tlsd->tls", inputs, columns, preferred_element_type=jnp.float32)
    pre_total = lax.psum(partial_value, "layer")
    bias_picked = jax.vmap(pick_rows, in_axes=(0, 1), out_axes=1)(enc_bias, picked)
    pre_value = (pre_total + bias_picked).astype(jnp.bfloat16)
    act_slots = lax.optimization_barrier(
        jnp.where(valid_slot, pre_value, jnp.zeros_like(pre_value))
    )
    token_ids = lax.broadcasted_iota(jnp.int32, picked.shape, 0)
    layer_ids = lax.broadcasted_iota(jnp.int32, picked.shape, 1)
    act_dense = (
        jnp.zeros((tokens, layers, slab_width), jnp.bfloat16)
        .at[token_ids, layer_ids, picked]
        .add(act_slots)
    )
    block_ids = jnp.arange(blocks, dtype=jnp.int32)
    first_target = block_ids <= pair_index
    source = jnp.where(first_target, block_ids, block_ids - pair_index - 1)
    slot_ids = jnp.where(first_target, 0, 1).astype(jnp.int32)
    slot_weight = jnp.stack([first_target, jnp.logical_not(first_target)], axis=1).astype(
        jnp.float32
    )
    source_onehot = (source[:, None] == jnp.arange(layers, dtype=jnp.int32)[None, :]).astype(
        jnp.float32
    )
    act_source = jnp.take(act_dense, source, axis=1)
    picked_source = jnp.take(picked, source, axis=1)
    per_block = jnp.einsum(
        "tks,ksf->tkf", act_source, decoder_own, preferred_element_type=jnp.float32
    )
    rebuilt = lax.psum(
        jnp.einsum("tkf,kc->tcf", per_block, slot_weight, precision=lax.Precision.HIGHEST), "lat"
    )
    residue = (rebuilt + dec_bias[0][None, :, :] - targets[0].astype(jnp.float32)).astype(
        jnp.bfloat16
    )
    residue = lax.optimization_barrier(residue)
    residue_block = jnp.take(residue, slot_ids, axis=1)
    block_grad = jnp.einsum(
        "tks,tkf->ksf", act_source, residue_block, preferred_element_type=jnp.float32
    )
    dense_grad = jnp.einsum(
        "tkf,ksf->tks", residue_block, decoder_own, preferred_element_type=jnp.float32
    )
    per_block = jnp.take_along_axis(dense_grad, picked_source, axis=2)
    grad_slots = lax.psum(
        jnp.einsum("tks,kl->tls", per_block, source_onehot, precision=lax.Precision.HIGHEST),
        "layer",
    ).astype(jnp.bfloat16)
    pre_grad = lax.optimization_barrier(
        jnp.where(valid_slot, grad_slots, jnp.zeros_like(grad_slots))
    )
    grad_dense = (
        jnp.zeros((tokens, layers, slab_width), jnp.bfloat16)
        .at[token_ids, layer_ids, picked]
        .add(pre_grad)
    )
    encoder_grad = jnp.einsum(
        "tld,tln->ldn", inputs, grad_dense, preferred_element_type=jnp.float32
    )
    bias_grad = jnp.sum(grad_dense, axis=0, dtype=jnp.float32)
    return (block_grad[None], encoder_grad, bias_grad)


def solution(mesh):
    return jax.shard_map(
        body,
        mesh=mesh,
        in_specs=(
            P(None, None, "layer"),
            P(None, "layer", "lat"),
            P(None, "lat"),
            P("layer", None, "lat", None),
            P("layer", None, None),
            P("layer", None, None, None),
            P(),
        ),
        out_specs=(P("layer", None, "lat", None), P(None, "layer", "lat"), P(None, "lat")),
        check_vma=False,
    )
```

profile of v0, /device:TPU:0, one launch (start us, length us, event | category | flops | bytes accessed | tf_op | source)
XLA Modules:
  0.0 594.4 jit_solution(13618870835661795366)
XLA Ops:
  7.3 1.0 iota_subtract_fusion
  8.3 0.9 top_k.12
  9.4 65.9 %gather_fusion.3 = s32[8192]{0:T(1024)S(1)} fusion(s32[128,2,64]{0,2,1:T(8,128)S(1)} %get-tuple-element.29, s32[8192]{0:T(1024)S(1)} %reshape.136), kind=kCustom, calls=%fused_computation.3 | custom fusion | bytes 163840 | tf_op jit(solution)/shard_map/jit(take_along_axis)/gather | solution.py:27
  76.2 69.2 %gather_fusion.5 = f32[8192]{0:T(1024)S(1)} fusion(f32[2,1024]{1,0:T(2,128)S(1)} %copy-done.1, s32[8192]{0:T(1024)S(1)} %reshape.142), kind=kCustom, calls=%fused_computation.5 | custom fusion | bytes 131072 | tf_op jit(solution)/shard_map/vmap(jit(_take))/gather | solution.py:10
  145.9 1.5 copy.84
  147.4 80.9 %gather_fusion.4 = bf16[8192,256]{1,0:T(8,128)(2,1)} fusion(bf16[2,1024,256]{2,1,0:T(8,128)(2,1)S(1)} %bitcast.87, s32[8192]{0:T(1024)S(1)} %reshape.142), kind=kCustom, calls=%fused_computation.4 | custom fusion | bytes 8454144 | tf_op jit(solution)/shard_map/vmap(jit(_take))/gather | solution.py:10
  228.3 3.8 fusion
  232.1 38.9 %psum.21 = f32[128,2,32]{0,2,1:T(8,128)S(1)} all-reduce(f32[128,2,32]{0,2,1:T(8,128)S(1)} %bitcast.89), channel_id=1, replica_groups=mesh['layer'=8,'lat'=4] {'layer'}, use_global_device_ids=true, to_apply=%region_1.2 | all-reduce | flops 8192 | bytes 65536 | tf_op jit(solution)/shard_map/psum | solution.py:31
  271.2 57.4 %scatter_custom_fusion = bf16[262144]{0:T(1024)(128)(2,1)S(1)} fusion(s32[8192]{0:T(1024)S(1)} %reshape.160, bf16[8192]{0:T(1024)(128)(2,1)S(1)} %reshape.162, bf16[]{:T(256)} %constant.132.clone.1), kind=kCustom, calls=%fused_computation.32 | custom fusion | flops 8192 | bytes 524290
  328.9 0.6 gather_fusion
  330.0 1.5 convolution_bitcast_fusion.2
  331.5 0.6 gather_fusion.2
  332.5 28.4 %all-reduce.2.cloned.1.call-done = f32[128,2,256]{2,1,0:T(2,128)} async-done(((f32[128,2,256]{2,1,0:T(2,128)}), f32[128,2,256]{2,1,0:T(2,128)}) %all-reduce.2.cloned.1.call-update) | async-done | bytes 262160 | tf_op jit(solution)/shard_map/psum | solution.py:59
  360.9 1.1 fusion.16
  362.0 0.6 gather_fusion.1
  362.6 0.6 fusion.6
  363.2 118.1 %gather_fusion.6 = f32[12288]{0:T(1024)S(1)} fusion(f32[128,3,1024]{2,0,1:T(8,128)S(1)} %fusion.6, s32[12288]{0:T(1024)S(1)} %reshape.154), kind=kCustom, calls=%fused_computation.6 | custom fusion | bytes 245760 | tf_op jit(solution)/shard_map/jit(take_along_axis)/gather | solution.py:73
  481.9 37.1 %psum.23 = bf16[128,2,32]{0,2,1:T(8,128)(2,1)S(1)} all-reduce(f32[128,2,32]{0,2,1:T(8,128)S(1)} %bitcast.90), channel_id=1, replica_groups=mesh['layer'=8,'lat'=4] {'layer'}, use_global_device_ids=true, to_apply=%region_4.5 | all-reduce | flops 8192 | bytes 49152 | tf_op jit(solution)/shard_map/psum | solution.py:74
  519.3 58.0 %scatter_custom_fusion.1 = bf16[262144]{0:T(1024)(128)(2,1)} fusion(s32[8192]{0:T(1024)S(1)} %reshape.160, bf16[8192]{0:T(1024)(128)(2,1)S(1)} %reshape.168, bf16[]{:T(256)} %constant.132.clone.1), kind=kCustom, calls=%fused_computation.30 | custom fusion | flops 8192 | bytes 524290
  577.3 1.2 reshape.110
  578.5 1.1 convert_reduce_fusion
  579.6 2.7 convolution_bitcast_fusion.1
  582.3 2.4 convolution_bitcast_fusion
  584.7 2.9 copy.99
  (68 shorter events, 3.9 us)
Async XLA Ops:
  7.2 322.3 %copy-start = (bf16[1,3,1024,256]{3,2,1,0:T(8,128)(2,1)S(1)}, bf16[1,3,1024,256]{3,2,1,0:T(8,128)(2,1)}, u32[]{:S(2)}) copy-start(bf16[1,3,1024,256]{3,2,1,0:T(8,128)(2,1)} %param.10) | copy-start | bytes 4718596
  7.2 353.7 %all-reduce.2.cloned.1.call-start = ((), (), s32[]{:S(2)}) async-start(), calls=%async_computation | async-start | bytes 524288 | tf_op jit(solution)/shard_map/psum | solution.py:59
  9.4 66.2 %copy-start.8 = (s32[3]{0:T(128)S(1)}, s32[3]{0:T(128)}, u32[]{:S(2)}) copy-start(s32[3]{0:T(128)} %constant.149) | copy-start | bytes 40
  9.4 66.3 %copy-start.7 = (s32[3]{0:T(128)S(1)}, s32[3]{0:T(128)}, u32[]{:S(2)}) copy-start(s32[3]{0:T(128)} %constant.146) | copy-start | bytes 40
  75.3 0.9 copy-start.1
  147.4 80.9 %copy-start.5 = (bf16[128,2,256]{2,1,0:T(2,128)(2,1)S(1)}, bf16[128,2,256]{2,1,0:T(2,128)(2,1)}, u32[]{:S(2)}) copy-start(bf16[128,2,256]{2,1,0:T(2,128)(2,1)} %param.7) | copy-start | bytes 393220
  328.8 32.1 %copy-start.4 = (bf16[1,128,2,256]{3,2,1,0:T(2,128)(2,1)S(1)}, bf16[1,128,2,256]{3,2,1,0:T(2,128)(2,1)}, u32[]{:S(2)}) copy-start(bf16[1,128,2,256]{3,2,1,0:T(2,128)(2,1)} %param.12) | copy-start | bytes 393220
  328.8 32.1 %copy-start.6 = (f32[1,2,256]{2,1,0:T(2,128)S(1)}, f32[1,2,256]{2,1,0:T(2,128)}, u32[]{:S(2)}) copy-start(f32[1,2,256]{2,1,0:T(2,128)} %param.11) | copy-start | bytes 6148
  329.5 32.5 %copy-start.2 = (bf16[3,128,1024]{2,1,0:T(8,128)(2,1)}, bf16[3,128,1024]{2,1,0:T(8,128)(2,1)S(1)}, u32[]{:S(2)}) copy-start(bf16[3,128,1024]{2,1,0:T(8,128)(2,1)S(1)} %gather_fusion) | copy-start | bytes 2359300
  481.3 101.0 %copy-start.3 = (bf16[3,128,1024]{2,1,0:T(8,128)(2,1)S(1)}, bf16[3,128,1024]{2,1,0:T(8,128)(2,1)}, u32[]{:S(2)}) copy-start(bf16[3,128,1024]{2,1,0:T(8,128)(2,1)} %copy-done.2) | copy-start | bytes 2359300
Sparse Core Ops, SparseCore 0:
  331.6 29.2 all-reduce.1
where the time goes:
time: 595 us; the launch traced here: 594 us
  local copies, waits for them, and re-layouts  344 us (58%)
  other arithmetic  120 us (20%)
  blocking collectives  76 us (13%)
  waiting for transfers between devices  28.4 us (5%)
  between operations  14.5 us (2%)
  matrix products  11.7 us (2%)
    gather x6, local copies, waits for them, and re-layouts, pick_rows(): return jnp.take(weight_table, row_index, axis=0)  150 us
    gather x5, local copies, waits for them, and re-layouts, body(): per_block = jnp.take_along_axis(dense_grad, picked_source, axis=2)  119 us
    unnamed x5, other arithmetic  116 us
    gather x5, local copies, waits for them, and re-layouts, body(): jnp.take_along_axis(jnp.where(inside, local_index, 0), position, axis=2)  66.4 us
    psum x1, blocking collectives, body(): pre_total = lax.psum(partial_value, 'layer')  38.9 us
    psum x1, blocking collectives, body(): lax.psum(jnp.einsum('tks,kl->tls', per_block, source_onehot, precision=la...  37.1 us
    psum x1, waiting for transfers between devices, body(): lax.psum(jnp.einsum('tkf,kc->tcf', per_block, slot_weight, precision=lax....  28.4 us
  transfers between devices with their start and end apart: 1, of which 1 were waited for; matrix products, arithmetic and copies ran while one was open for 0% of the time, Pallas kernels for 0%

commit v1 on v0

v1 whole, which is shorter than its diff:
```python
import functools

import jax
import jax.numpy as jnp
from jax import lax
from jax.experimental import pallas as pl
from jax.experimental.pallas import tpu as pltpu
from jax.sharding import PartitionSpec as P

FEAT_SPLIT = 8
LANES = 128
CELL = 256

BF = jnp.bfloat16
F32 = jnp.float32
NT = (((1,), (1,)), ((), ()))
TN = (((0,), (0,)), ((), ()))


def matmul(left, right, dims=(((1,), (0,)), ((), ()))):
    return lax.dot_general(left, right, dims, preferred_element_type=F32)


def flag(condition):
    return jnp.where(condition, 1.0, 0.0).astype(BF)


def iota(shape, dimension):
    return lax.broadcasted_iota(jnp.int32, shape, dimension)


def cell_masks(cell_index, rows):
    row = lax.shift_right_arithmetic(cell_index, 7)
    lane = jnp.bitwise_and(cell_index, LANES - 1)
    row_hit = iota((rows, CELL), 0) == row
    lane_hot = flag(iota((LANES, CELL), 0) == lane)
    return row_hit, lane_hot


def gather_slots(dense, zidx_ref, out_ref, layer, cells, tokens_cell, width):
    blocks = width // LANES
    for cell in range(cells):
        view = jnp.concatenate(
            [
                dense[cell * tokens_cell : (cell + 1) * tokens_cell, b * LANES : (b + 1) * LANES]
                for b in range(blocks)
            ],
            axis=0,
        ).astype(BF)
        at = layer * cells + cell
        row_hit, lane_hot = cell_masks(zidx_ref[at : at + 1, :], blocks * tokens_cell)
        spread = matmul(view, lane_hot)
        out_ref[at : at + 1, :] = jnp.sum(jnp.where(row_hit, spread, 0.0), axis=0, keepdims=True)


def scatter_slots(values, zidx_ref, dense_ref, layer, cells, tokens_cell, width):
    blocks = width // LANES
    group = max(1, 16 // tokens_cell)
    for first in range(0, cells, group):
        views = []
        for cell in range(first, first + group):
            at = layer * cells + cell
            row_hit, lane_hot = cell_masks(zidx_ref[at : at + 1, :], blocks * tokens_cell)
            placed = jnp.where(row_hit, values[at : at + 1, :], 0.0).astype(BF)
            views.append(matmul(placed, lane_hot, NT))
        for b in range(blocks):
            piece = [v[b * tokens_cell : (b + 1) * tokens_cell] for v in views]
            piece = piece[0] if group == 1 else jnp.concatenate(piece, axis=0)
            dense_ref[
                layer,
                first * tokens_cell : (first + group) * tokens_cell,
                b * LANES : (b + 1) * LANES,
            ] = piece.astype(BF)


def slot_index(top, slab, width, layers, top_count, slab_most, tokens_cell):
    tokens, lanes = top.shape
    cells = tokens // tokens_cell
    lane = iota(top.shape, 1)
    place = jnp.bitwise_and(lane, top_count - 1)
    local = top - slab * width
    inside = (local >= 0) & (local < width)
    before = iota((lanes, lanes), 0)
    after = iota((lanes, lanes), 1)
    earlier = flag((before // top_count == after // top_count) & (before < after))
    rank = matmul(flag(inside), earlier).astype(jnp.int32)
    word = jnp.where(inside, (1 << 30) + ((place - rank) << 16) + local, 0)
    step = 0
    while (1 << step) < top_count:
        moved = pltpu.roll(word, lanes - (1 << step), 1)
        bit = 1 << (16 + step)
        word = jnp.where(
            (moved & bit) != 0, moved, jnp.where((word & bit) != 0, 0, word)
        )
        step += 1
    local = word & 0xFFFF
    low = (local & (LANES - 1)).astype(F32).astype(BF)
    high = jnp.where(word != 0, (local >> 7) + 1, 0).astype(F32).astype(BF)
    both = jnp.concatenate([low, high], axis=0)
    column = iota((tokens, CELL), 1) // slab_most
    own = column == jnp.bitwise_and(iota((tokens, CELL), 0), tokens_cell - 1)
    pool = flag(iota((cells, tokens), 1) // tokens_cell == iota((cells, tokens), 0))
    out = []
    for layer in range(layers):
        pick = flag(
            iota((lanes, CELL), 0)
            == layer * top_count + jnp.bitwise_and(iota((lanes, CELL), 1), slab_most - 1)
        )
        tiled = matmul(both, pick)
        low_t = jnp.where(own, tiled[:tokens], 0.0).astype(BF)
        high_t = jnp.where(own, tiled[tokens:], 0.0).astype(BF)
        low_z = matmul(pool, low_t).astype(jnp.int32)
        high_z = matmul(pool, high_t).astype(jnp.int32)
        token = iota((cells, CELL), 1) // slab_most
        row = (high_z - 1) * tokens_cell + token
        out.append(jnp.where(high_z > 0, row * LANES + low_z, -1))
    return jnp.concatenate(out, axis=0)


def encode_kernel(plan, where_ref, x_ref, encoder_ref, bias_ref, top_ref, z_ref, zidx_ref, slots):
    layers, cells, tokens_cell, width, top_count, slab_most = plan
    depth = encoder_ref.shape[1]
    zidx_ref[...] = slot_index(
        top_ref[...], where_ref[1], width, layers, top_count, slab_most, tokens_cell
    )
    with_bias = jnp.where(where_ref[0] == 0, 1.0, 0.0)
    for layer in range(layers):
        dense = matmul(x_ref[:, layer * depth : (layer + 1) * depth], encoder_ref[layer])
        dense = dense + bias_ref[layer : layer + 1, :] * with_bias
        gather_slots(dense, zidx_ref, slots, layer, cells, tokens_cell, width)
    z_ref[...] = slots[...].astype(BF)


def decode_kernel(plan, pair, parts_ref, zidx_ref, decoder_ref, act_ref, partial_ref):
    layers, cells, tokens_cell, width, top_count, slab_most = plan
    total = jnp.sum(parts_ref[...].astype(F32), axis=0)
    total = total.astype(BF).astype(F32)
    for layer in range(layers):
        scatter_slots(total, zidx_ref, act_ref, layer, cells, tokens_cell, width)
    sums = [None, None]
    for k in range(layers + 1):
        source, slot = (k, 0) if k <= pair else (k - pair - 1, 1)
        term = matmul(act_ref[source], decoder_ref[k])
        sums[slot] = term if sums[slot] is None else sums[slot] + term
    for slot in range(2):
        partial_ref[slot] = sums[slot].astype(BF)


def residue_kernel(
    plan, pair, parts_ref, dec_bias_ref, targets_ref, zidx_ref, decoder_ref, act_ref,
    z_ref, grad_ref, slots, residue
):
    layers, cells, tokens_cell, width, top_count, slab_most = plan
    for slot in range(2):
        rebuilt = jnp.sum(parts_ref[:, slot].astype(F32), axis=0)
        rebuilt = rebuilt + dec_bias_ref[slot : slot + 1, :]
        residue[slot] = (rebuilt - targets_ref[slot].astype(F32)).astype(BF)
    places = [(k, 0) if k <= pair else (k - pair - 1, 1) for k in range(layers + 1)]
    for layer in range(layers):
        dense = None
        for k in range(layers + 1):
            if places[k][0] == layer:
                term = matmul(residue[places[k][1]], decoder_ref[k], NT)
                dense = term if dense is None else dense + term
        if dense is None:
            slots[layer * cells : (layer + 1) * cells, :] = jnp.zeros((cells, CELL), F32)
        else:
            gather_slots(dense, zidx_ref, slots, layer, cells, tokens_cell, width)
    z_ref[...] = slots[...].astype(BF)
    for k in range(layers + 1):
        grad_ref[k] = matmul(act_ref[places[k][0]], residue[places[k][1]], TN)


def encoder_grad_kernel(plan, parts_ref, zidx_ref, x_ref, grad_ref, bias_ref, dense):
    layers, cells, tokens_cell, width, top_count, slab_most = plan
    depth = grad_ref.shape[1]
    tokens = x_ref.shape[0]
    total = jnp.sum(parts_ref[...].astype(F32), axis=0)
    total = total.astype(BF).astype(F32)
    for layer in range(layers):
        scatter_slots(total, zidx_ref, dense, layer, cells, tokens_cell, width)
        grad_ref[layer] = matmul(
            x_ref[:, layer * depth : (layer + 1) * depth], dense[layer], TN
        )
        ones = jnp.ones((8, tokens), BF)
        bias_ref[layer : layer + 1, :] = matmul(ones, dense[layer])[:1]


def call(kernel, out_shape, scratch, *args, smem=0):
    vmem = pl.BlockSpec(memory_space=pltpu.VMEM)
    return pl.pallas_call(
        kernel,
        out_shape=out_shape,
        in_specs=[pl.BlockSpec(memory_space=pltpu.SMEM)] * smem + [vmem] * (len(args) - smem),
        out_specs=jax.tree.map(lambda _: vmem, out_shape),
        scratch_shapes=scratch,
        compiler_params=pltpu.CompilerParams(vmem_limit_bytes=40 * 1024 * 1024),
    )(*args)


def share(value, axis):
    count = lax.axis_size(axis)
    copies = jnp.broadcast_to(value[None], (count,) + value.shape)
    return lax.all_to_all(copies, axis, 0, 0, tiled=True)


def by_pair(pairs, build, *args):
    branches = [functools.partial(build, pair) for pair in range(pairs)]
    if pairs == 1:
        return branches[0](*args)
    return lax.switch(lax.axis_index("layer") // FEAT_SPLIT, branches, *args)


def body(inputs, encoder, enc_bias, decoder, dec_bias, targets, top_index):
    tokens, layers, top_count = top_index.shape
    width = encoder.shape[2]
    feat = decoder.shape[3]
    slab_most = 2 * top_count // lax.axis_size("lat")
    tokens_cell = CELL // slab_most
    cells = tokens // tokens_cell
    rows = layers * cells
    pairs = lax.axis_size("layer") // FEAT_SPLIT
    plan = (layers, cells, tokens_cell, width, top_count, slab_most)
    where = jnp.stack([lax.axis_index("layer"), lax.axis_index("lat")]).astype(jnp.int32)
    x = inputs.reshape(tokens, -1)
    top = top_index.reshape(tokens, -1)
    shape = jax.ShapeDtypeStruct
    z, zidx = call(
        functools.partial(encode_kernel, plan),
        (shape((rows, CELL), BF), shape((rows, CELL), jnp.int32)),
        [pltpu.VMEM((rows, CELL), F32)],
        where, x, encoder, enc_bias, top, smem=1,
    )
    parts = share(z, "layer")

    def decode(pair, *args):
        return call(
            functools.partial(decode_kernel, plan, pair),
            (shape((layers, tokens, width), BF), shape((2, tokens, feat), BF)),
            [],
            *args,
        )

    act, partial = by_pair(pairs, decode, parts, zidx, decoder[0])
    partials = lax.all_gather(partial, "lat")

    def residues(pair, *args):
        return call(
            functools.partial(residue_kernel, plan, pair),
            (shape((rows, CELL), BF), shape((layers + 1, width, feat), F32)),
            [pltpu.VMEM((rows, CELL), F32), pltpu.VMEM((2, tokens, feat), BF)],
            *args,
        )

    z, decoder_grad = by_pair(
        pairs, residues, partials, dec_bias[0], jnp.swapaxes(targets[0], 0, 1), zidx, decoder[0], act
    )
    parts = share(z, "layer")
    encoder_grad, bias_grad = call(
        functools.partial(encoder_grad_kernel, plan),
        (shape(encoder.shape, F32), shape(enc_bias.shape, F32)),
        [pltpu.VMEM((layers, tokens, width), BF)],
        parts, zidx, x,
    )
    return decoder_grad[None], encoder_grad, bias_grad


def solution(mesh):
    return jax.shard_map(
        body,
        mesh=mesh,
        in_specs=(
            P(None, None, "layer"),
            P(None, "layer", "lat"),
            P(None, "lat"),
            P("layer", None, "lat", None),
            P("layer", None, None),
            P("layer", None, None, None),
            P(),
        ),
        out_specs=(P("layer", None, "lat", None), P(None, "layer", "lat"), P(None, "lat")),
        check_vma=False,
    )
```

time: 595 us -> 47.5 us (0.08)
  local copies, waits for them, and re-layouts: 344 us -> 5.5 us
  other arithmetic: 120 us -> 0.08 us
  blocking collectives: 76 us -> 17.3 us
  waiting for transfers between devices: 28.4 us -> 6.42 us
  between operations: 14.5 us -> 0.68 us
  matrix products: 11.7 us -> 0 us
  Pallas kernels: 0 us -> 9.78 us
  starting transfers between devices: 0.04 us -> 7.28 us
    gather x19 -> x0, local copies, waits for them, and re-layouts: 337 us -> none  [the longest x6 150 us: pick_rows(): return jnp.take(weight_table, row_index, axis=0)]
    unnamed x5 -> x0, other arithmetic: 116 us -> none
    psum x2 -> x0, blocking collectives: 76 us -> none  [the longest x1 38.9 us: body(): pre_total = lax.psum(partial_value, 'layer')]
    psum x1 -> x0, waiting for transfers between devices: 28.4 us -> none  [body(): lax.psum(jnp.einsum('tkf,kc->tcf', per_block, slot_weight, precision=lax....]
    dot_general x7 -> x0, matrix products: 11.7 us -> none  [the longest x1 3.79 us: body(): jnp.einsum('tld,tlsd->tls', inputs, columns, preferred_element_type=jnp.f...]
    all_to_all x0 -> x1, blocking collectives: none -> 10.2 us  [share(): return lax.all_to_all(copies, axis, 0, 0, tiled=True)]
    pallas_call x0 -> x4, Pallas kernels: none -> 9.78 us  [call(): pl.pallas_call(kernel, out_shape=out_shape, in_specs=[pl.BlockSpec(memory...]
    all_to_all x0 -> x1, starting transfers between devices: none -> 7.28 us  [share(): return lax.all_to_all(copies, axis, 0, 0, tiled=True)]
  transfers between devices with their start and end apart: 1 -> 1, of which waited for: 1 -> 1; matrix products, arithmetic and copies ran while one was open for 0% -> 2% of each run, Pallas kernels for 0% -> 0%
where the time goes in v1:
time: 47.5 us; the launch traced here: 47.1 us
  blocking collectives  17.3 us (36%)
  Pallas kernels  9.78 us (21%)
  starting transfers between devices  7.28 us (15%)
  waiting for transfers between devices  6.42 us (14%)
  local copies, waits for them, and re-layouts  5.5 us (12%)
  between operations  0.68 us (1%)
    all_to_all x1, blocking collectives, share(): return lax.all_to_all(copies, axis, 0, 0, tiled=True)  10.2 us
    pallas_call x4, Pallas kernels, call(): pl.pallas_call(kernel, out_shape=out_shape, in_specs=[pl.BlockSpec(memory...  9.78 us
    all_to_all x1, starting transfers between devices, share(): return lax.all_to_all(copies, axis, 0, 0, tiled=True)  7.28 us
    all_gather x1, blocking collectives, body(): partials = lax.all_gather(partial, 'lat')  7.17 us
    all_to_all x1, waiting for transfers between devices, share(): return lax.all_to_all(copies, axis, 0, 0, tiled=True)  6.42 us
    unnamed x10, local copies, waits for them, and re-layouts  3.77 us
    reshape x1, local copies, waits for them, and re-layouts, body(): top = top_index.reshape(tokens, -1)  1.04 us
  transfers between devices with their start and end apart: 1, of which 1 were waited for; matrix products, arithmetic and copies ran while one was open for 2% of the time, Pallas kernels for 0%

profile of v1, /device:TPU:0, one launch (start us, length us, event | category | flops | bytes accessed | tf_op | source)
XLA Modules:
  0.0 47.1 jit_solution(15294215442424662569)
XLA Ops:
  0.6 0.0 copy-start
  0.6 1.0 %copy.14.top_ref = s32[128,128]{1,0:T(8,128)S(1)} copy(s32[128,128]{0,1:T(8,128)} %bitcast.22) | data formatting | bytes 131072 | tf_op jit(solution)/shard_map/reshape | solution.py:226
  1.7 0.9 %copy.16 = bf16[16,8,2,256]{3,1,2,0:T(8,128)(2,1)S(1)} copy(bf16[16,8,2,256]{3,2,1,0:T(2,128)(2,1)} %bitcast.21) | data formatting | bytes 262144
  2.6 0.1 pad_add_fusion.where_ref
  2.7 0.0 copy-start.1
  2.7 1.2 %copy-done.1 = bf16[2,256,1024]{2,1,0:T(8,128)(2,1)S(1)} copy-done((bf16[2,256,1024]{2,1,0:T(8,128)(2,1)S(1)}, bf16[2,256,1024]{2,1,0:T(8,128)(2,1)}, u32[]{:S(2)}) %copy-start.1) | copy-done | bytes 1048600
  3.9 0.0 copy-start.2
  3.9 0.7 %copy-done.2 = f32[2,1024]{1,0:T(2,128)S(1)} copy-done((f32[2,1024]{1,0:T(2,128)S(1)}, f32[2,1024]{1,0:T(2,128)}, u32[]{:S(2)}) %copy-start.2) | copy-done | bytes 8216
  4.6 0.0 copy-start.3
  4.6 2.5 %shard_map.94 = (bf16[32,256]{1,0:T(8,128)(2,1)S(1)}, s32[32,256]{1,0:T(8,128)S(1)}) custom-call(s32[2]{0:T(128)S(1)} %pad_add_fusion.where_ref, bf16[128,512]{1,0:T(8,128)(2,1)S(1)} %bitcast.17, bf16[2,256,1024]{2,1,0:T(8,128)(2,1)S(1)} %copy-done.1, f32[2,1024]{1,0:T(2,128)S(1)} %copy-done.2, s32[128,128]{1,0:T(8,128)S(1)} %copy.14.top_ref), custom_call_target="tpu_custom_call" | custom-call | tf_op jit(solution)/shard_map/pallas_call | solution.py:191
  7.1 0.7 %broadcast_in_dim.6 = bf16[8,32,256]{2,1,0:T(8,128)(2,1)} broadcast(bf16[32,256]{1,0:T(8,128)(2,1)S(1)} %get-tuple-element.11), dimensions={1,2} | broadcast | bytes 147456 | tf_op jit(solution)/shard_map/broadcast_in_dim | solution.py:203
  7.8 7.3 %all-to-all-start = ((bf16[8,32,256]{2,1,0:T(8,128)(2,1)}), bf16[8,32,256]{2,1,0:T(8,128)(2,1)S(1)}, u32[]{:S(2)}, u32[]{:S(2)}) async-start(bf16[8,32,256]{2,1,0:T(8,128)(2,1)} %broadcast_in_dim.6), calls=%async_computation | async-start | bytes 262144 | tf_op jit(solution)/shard_map/all_to_all | solution.py:204
  15.0 0.9 %copy.18 = bf16[1,128,2,256]{3,1,2,0:T(8,128)(2,1)S(1)} copy(bf16[1,128,2,256]{3,2,1,0:T(2,128)(2,1)} %param.12) | data formatting | bytes 262144 | tf_op args[5]
  16.0 6.4 %all-to-all-done.parts_ref = bf16[8,32,256]{2,1,0:T(8,128)(2,1)S(1)} async-done(((bf16[8,32,256]{2,1,0:T(8,128)(2,1)}), bf16[8,32,256]{2,1,0:T(8,128)(2,1)S(1)}, u32[]{:S(2)}, u32[]{:S(2)}) %all-to-all-start) | async-done | bytes 131104 | tf_op jit(solution)/shard_map/all_to_all | solution.py:204
  22.4 0.0 copy-done
  22.4 1.3 %shard_map.95 = (bf16[2,128,1024]{2,1,0:T(8,128)(2,1)S(1)}, bf16[2,128,256]{2,1,0:T(8,128)(2,1)S(1)}) custom-call(bf16[8,32,256]{2,1,0:T(8,128)(2,1)S(1)} %all-to-all-done.parts_ref, s32[32,256]{1,0:T(8,128)S(1)} %get-tuple-element.12.zidx_ref, bf16[3,1024,256]{2,1,0:T(8,128)(2,1)S(1)} %bitcast.14), custom_call_target="tpu_custom_call" | custom-call | tf_op jit(solution)/shard_map/pallas_call | solution.py:191
  23.7 7.2 %all-gather = bf16[8,128,256]{2,1,0:T(8,128)(2,1)S(1)} all-gather(bf16[2,128,256]{2,1,0:T(8,128)(2,1)S(1)} %get-tuple-element.13), channel_id=2, replica_groups=mesh['layer'=8,'lat'=4] {'lat'}, dimensions={0}, use_global_device_ids=true | all-gather | bytes 655360 | tf_op jit(solution)/shard_map/all_gather | solution.py:245
  30.8 0.0 copy-done.3
  30.8 3.3 %shard_map.96 = (bf16[32,256]{1,0:T(8,128)(2,1)S(1)}, f32[3,1024,256]{2,1,0:T(8,128)}) custom-call(bf16[4,2,128,256]{3,2,1,0:T(8,128)(2,1)S(1)} %bitcast.16, f32[2,256]{1,0:T(2,128)S(1)} %bitcast.20, bf16[2,128,256]{2,1,0:T(8,128)(2,1)S(1)} %bitcast.19, s32[32,256]{1,0:T(8,128)S(1)} %get-tuple-element.12.zidx_ref, bf16[3,1024,256]{2,1,0:T(8,128)(2,1)S(1)} %bitcast.15, ...), custom_call_target="tpu_custom_call" | custom-call | tf_op jit(solution)/shard_map/pallas_call | solution.py:191
  34.2 10.2 %all_to_all.10.parts_ref = bf16[8,32,256]{2,1,0:T(8,128)(2,1)S(1)} all-to-all(bf16[8,32,256]{2,1,0:T(8,128)(2,1)S(1)} %broadcast_in_dim.8), channel_id=1, replica_groups=mesh['layer'=8,'lat'=4] {'layer'}, dimensions={0} | all-to-all | bytes 262144 | tf_op jit(solution)/shard_map/all_to_all | solution.py:204
  44.3 2.7 %shard_map.97 = (f32[2,256,1024]{2,1,0:T(8,128)}, f32[2,1024]{1,0:T(2,128)}) custom-call(bf16[8,32,256]{2,1,0:T(8,128)(2,1)S(1)} %all_to_all.10.parts_ref, s32[32,256]{1,0:T(8,128)S(1)} %get-tuple-element.12.zidx_ref, bf16[128,512]{1,0:T(8,128)(2,1)S(1)} %bitcast.18), custom_call_target="tpu_custom_call" | custom-call | tf_op jit(solution)/shard_map/pallas_call | solution.py:191
  (1 shorter events, 0.0 us)
Async XLA Ops:
  0.6 21.8 %copy-start = (bf16[1,3,1024,256]{3,2,1,0:T(8,128)(2,1)S(1)}, bf16[1,3,1024,256]{3,2,1,0:T(8,128)(2,1)}, u32[]{:S(2)}) copy-start(bf16[1,3,1024,256]{3,2,1,0:T(8,128)(2,1)} %param.10) | copy-start | bytes 4718596
  2.7 1.2 %copy-start.1 = (bf16[2,256,1024]{2,1,0:T(8,128)(2,1)S(1)}, bf16[2,256,1024]{2,1,0:T(8,128)(2,1)}, u32[]{:S(2)}) copy-start(bf16[2,256,1024]{2,1,0:T(8,128)(2,1)} %encoder_ref.1) | copy-start | bytes 3145732
  3.9 0.7 %copy-start.2 = (f32[2,1024]{1,0:T(2,128)S(1)}, f32[2,1024]{1,0:T(2,128)}, u32[]{:S(2)}) copy-start(f32[2,1024]{1,0:T(2,128)} %bias_ref.1) | copy-start | bytes 24580
  4.6 26.2 %copy-start.3 = (f32[1,2,256]{2,1,0:T(2,128)S(1)}, f32[1,2,256]{2,1,0:T(2,128)}, u32[]{:S(2)}) copy-start(f32[1,2,256]{2,1,0:T(2,128)} %param.11) | copy-start | bytes 6148
  7.8 14.6 %all-to-all-start = ((bf16[8,32,256]{2,1,0:T(8,128)(2,1)}), bf16[8,32,256]{2,1,0:T(8,128)(2,1)S(1)}, u32[]{:S(2)}, u32[]{:S(2)}) async-start(bf16[8,32,256]{2,1,0:T(8,128)(2,1)} %broadcast_in_dim.6), calls=%async_computation | async-start | bytes 262144 | tf_op jit(solution)/shard_map/all_to_all | solution.py:204

commit v2 on v1

v2 whole, which is shorter than its diff:
```python
import functools

import jax
import jax.numpy as jnp
from jax import lax
from jax.experimental import pallas as pl
from jax.experimental.pallas import tpu as pltpu
from jax.sharding import PartitionSpec as P

FEAT_SPLIT = 8
LANES = 128
CELL = 256
PARTS = 4

BF = jnp.bfloat16
F32 = jnp.float32
NT = (((1,), (1,)), ((), ()))
TN = (((0,), (0,)), ((), ()))


def matmul(left, right, dims=(((1,), (0,)), ((), ()))):
    return lax.dot_general(left, right, dims, preferred_element_type=F32)


def flag(condition):
    return jnp.where(condition, 1.0, 0.0).astype(BF)


def iota(shape, dimension):
    return lax.broadcasted_iota(jnp.int32, shape, dimension)


def pick_lanes(table, lanes):
    return jnp.take_along_axis(table, lanes, axis=1, mode="promise_in_bounds")


def choose(options, code):
    bit = 1
    while len(options) > 1:
        odd = (code & bit) != 0
        options = [
            jnp.where(odd, options[i + 1], options[i]) if i + 1 < len(options) else options[i]
            for i in range(0, len(options), 2)
        ]
        bit *= 2
    return options[0]


def stride(width):
    return 1 << (width // LANES - 1).bit_length()


def gather_slots(dense, index):
    lane = jnp.bitwise_and(index, LANES - 1)
    picked = [
        pick_lanes(dense[:, b * LANES : (b + 1) * LANES], lane)
        for b in range(dense.shape[1] // LANES)
    ]
    return choose(picked, lax.shift_right_logical(index, 7))


def join_layers(picked, index, width):
    total = choose(picked, lax.shift_right_logical(index, 7) // stride(width))
    return jnp.where(index < 0, 0.0, total)


def fold_slots(values, used):
    folds = LANES // used
    rows = values.shape[0] // folds
    total = values[:rows]
    for f in range(1, folds):
        total = total + pltpu.roll(values[f * rows : (f + 1) * rows], f * used, 1)
    return total


def unfold_slots(values, used):
    folds = LANES // used
    parts = [values] + [pltpu.roll(values, LANES - f * used, 1) for f in range(1, folds)]
    return jnp.concatenate(parts, axis=0)


def sum_parts(parts_ref, used):
    total = jnp.sum(parts_ref[...].astype(F32), axis=0)
    total = unfold_slots(total.astype(BF).astype(F32), used)
    return jnp.where(iota(total.shape, 1) < used, total, 0.0)


def place_slots(values, lane):
    blocks = lane.shape[1] // LANES
    return jnp.concatenate(
        [pick_lanes(values, lane[:, b * LANES : (b + 1) * LANES]).astype(BF) for b in range(blocks)],
        axis=1,
    )


def slot_index(top, slab, width, layers, top_count, slab_most):
    rows, tokens = top.shape
    place = jnp.bitwise_and(iota(top.shape, 0), top_count - 1)
    local = top - slab * width
    inside = (local >= 0) & (local < width)
    after = iota((rows, rows), 0)
    before = iota((rows, rows), 1)
    earlier = flag((before // top_count == after // top_count) & (before < after))
    rank = matmul(earlier, flag(inside)).astype(jnp.int32)
    local = local + (iota(top.shape, 0) // top_count) * (stride(width) * LANES)
    word = jnp.where(inside, (1 << 30) + ((place - rank) << 16) + local, 0)
    step = 0
    while (1 << step) < top_count:
        moved = pltpu.roll(word, rows - (1 << step), 0)
        bit = 1 << (16 + step)
        word = jnp.where((moved & bit) != 0, moved, jnp.where((word & bit) != 0, 0, word))
        step += 1
    index = jnp.where(word != 0, word & 0xFFFF, -1)
    kept = [index[layer * top_count : layer * top_count + slab_most] for layer in range(layers)]
    spare = LANES - layers * slab_most
    if spare:
        kept.append(jnp.full((spare, tokens), -1, jnp.int32))
    return jnp.transpose(jnp.concatenate(kept, axis=0), (1, 0))


def encode_kernel(
    plan, x_hbm, encoder_hbm, bias_hbm, top_hbm, z_ref, index_ref,
    x_ref, encoder_ref, bias_ref, top_ref, x_layer, sems
):
    layers, width, top_count, slab_most = plan
    copies = [
        pltpu.make_async_copy(source, target, sems.at[i])
        for i, (source, target) in enumerate(
            [(top_hbm, top_ref), (x_hbm, x_ref), (bias_hbm, bias_ref), (encoder_hbm, encoder_ref)]
        )
    ]
    for copy in copies:
        copy.start()
    for copy in copies[:2]:
        copy.wait()
    for layer in range(layers):
        x_layer[layer] = x_ref[:, layer, :]
    index = slot_index(top_ref[...], lax.axis_index("lat"), width, layers, top_count, slab_most)
    index_ref[...] = index
    for copy in copies[2:]:
        copy.wait()
    with_bias = jnp.where(lax.axis_index("layer") == 0, 1.0, 0.0)
    picked = []
    for layer in range(layers):
        dense = matmul(x_layer[layer], encoder_ref[layer])
        dense = dense + bias_ref[layer : layer + 1, :] * with_bias
        picked.append(gather_slots(dense, index))
    z_ref[...] = fold_slots(join_layers(picked, index, width), layers * slab_most).astype(BF)


def inverse_kernel(plan, index_ref, inverse_ref):
    layers, width, top_count, slab_most = plan
    index = index_ref[...]
    tokens = index.shape[0]
    tokens_cell = CELL // slab_most
    cells = tokens // tokens_cell
    blocks = width // LANES
    rows = blocks * tokens_cell
    low = jnp.bitwise_and(index, LANES - 1).astype(F32).astype(BF)
    high = (lax.shift_right_arithmetic(index, 7) + 1).astype(F32).astype(BF)
    both = jnp.concatenate([low, high], axis=0)
    own = iota((tokens, CELL), 1) // slab_most == jnp.bitwise_and(
        iota((tokens, CELL), 0), tokens_cell - 1
    )
    pool = flag(iota((cells, tokens), 1) // tokens_cell == iota((cells, tokens), 0))
    token = iota((cells, CELL), 1) // slab_most
    slot = jnp.bitwise_and(iota((rows, CELL), 1), slab_most - 1)
    for layer in range(layers):
        pick = flag(
            iota((LANES, CELL), 0)
            == layer * slab_most + jnp.bitwise_and(iota((LANES, CELL), 1), slab_most - 1)
        )
        tiled = matmul(both, pick)
        low_c = matmul(pool, jnp.where(own, tiled[:tokens], 0.0).astype(BF)).astype(jnp.int32)
        high_c = matmul(pool, jnp.where(own, tiled[tokens:], 0.0).astype(BF)).astype(jnp.int32)
        row_c = jnp.where(high_c > 0, (high_c - 1 - layer * stride(width)) * tokens_cell + token, -1)
        lane_id = (slot + (layer * slab_most - (LANES - 1))).astype(F32)
        for cell in range(cells):
            row_hit = iota((rows, CELL), 0) == row_c[cell : cell + 1]
            lane_hot = flag(iota((LANES, CELL), 0) == low_c[cell : cell + 1])
            placed = jnp.where(row_hit, lane_id, 0.0).astype(BF)
            view = matmul(placed, lane_hot, NT).astype(jnp.int32) + (LANES - 1)
            for b in range(blocks):
                inverse_ref[
                    layer,
                    cell * tokens_cell : (cell + 1) * tokens_cell,
                    b * LANES : (b + 1) * LANES,
                ] = view[b * tokens_cell : (b + 1) * tokens_cell]


def decode_kernel(
    plan, pair, parts_ref, inverse_ref, decoder_ref, index_ref, act_ref, partial_ref, index_out
):
    index_out[...] = index_ref[...]
    layers, width, top_count, slab_most = plan
    total = sum_parts(parts_ref, layers * slab_most)
    for layer in range(layers):
        act_ref[layer] = place_slots(total, inverse_ref[layer])
    sums = [None, None]
    for k in range(layers + 1):
        source, slot = (k, 0) if k <= pair else (k - pair - 1, 1)
        term = matmul(act_ref[source], decoder_ref[k])
        sums[slot] = term if sums[slot] is None else sums[slot] + term
    for slot in range(2):
        partial_ref[slot] = sums[slot].astype(BF)


def residue_kernel(
    plan, pair, parts_ref, dec_bias_ref, targets_ref, index_ref, decoder_ref, z_ref, residue
):
    layers, width, top_count, slab_most = plan
    for slot in range(2):
        rebuilt = jnp.sum(parts_ref[:, slot].astype(F32), axis=0)
        rebuilt = rebuilt + dec_bias_ref[slot : slot + 1, :]
        residue[slot] = (rebuilt - targets_ref[slot].astype(F32)).astype(BF)
    places = [(k, 0) if k <= pair else (k - pair - 1, 1) for k in range(layers + 1)]
    index = index_ref[...]
    picked = []
    for layer in range(layers):
        dense = None
        for k in range(layers + 1):
            if places[k][0] == layer:
                term = matmul(residue[places[k][1]], decoder_ref[k], NT)
                dense = term if dense is None else dense + term
        picked.append(jnp.zeros(index.shape, F32) if dense is None else gather_slots(dense, index))
    z_ref[...] = fold_slots(join_layers(picked, index, width), layers * slab_most).astype(BF)


def decoder_grad_kernel(plan, pair, act_ref, residue_ref, x_ref, grad_hbm, xt_ref, grad, sems):
    layers = plan[0]
    copies = []
    for k in range(layers + 1):
        source, slot = (k, 0) if k <= pair else (k - pair - 1, 1)
        grad[k] = matmul(act_ref[source], residue_ref[slot], TN)
        copy = pltpu.make_async_copy(grad.at[k], grad_hbm.at[k], sems.at[k])
        copy.start()
        copies.append(copy)
    for layer in range(layers):
        xt_ref[layer] = jnp.transpose(x_ref[:, layer, :], (1, 0))
    for copy in copies:
        copy.wait()


def encoder_grad_kernel(
    plan, parts_ref, inverse_ref, xt_ref, grad_hbm, bias_hbm, values, grad, bias, sems, bias_sem
):
    layers, width, top_count, slab_most = plan
    tokens = xt_ref.shape[2]
    part = width // PARTS
    values[...] = sum_parts(parts_ref, layers * slab_most)
    ones = jnp.ones((8, tokens), BF)
    copies = []
    for layer in range(layers):
        for i in range(PARTS):
            at = (layer, slice(None), pl.ds(i * part, part))
            dense = place_slots(values[...], inverse_ref[at])
            grad[at] = matmul(xt_ref[layer], dense)
            copies.append(
                pltpu.make_async_copy(grad.at[at], grad_hbm.at[at], sems.at[layer * PARTS + i])
            )
            copies[-1].start()
            bias[layer : layer + 1, i * part : (i + 1) * part] = matmul(ones, dense)[:1]
    copies.append(pltpu.make_async_copy(bias, bias_hbm, bias_sem))
    copies[-1].start()
    for copy in copies:
        copy.wait()


VMEM = pl.BlockSpec(memory_space=pltpu.VMEM)
HBM = pl.BlockSpec(memory_space=pltpu.HBM)
MIB = 1024 * 1024


def call(kernel, ins, outs, scratch, *args, cost=None, room=24):
    args = [
        pltpu.with_memory_space_constraint(arg, pltpu.HBM) if spec is HBM else arg
        for spec, arg in zip(ins, args, strict=True)
    ]
    return pl.pallas_call(
        kernel,
        out_shape=tuple(
            (pltpu.HBM if spec is HBM else pltpu.VMEM)(shape, dtype) for shape, dtype, spec in outs
        ),
        in_specs=ins,
        out_specs=tuple(spec for _, _, spec in outs),
        scratch_shapes=scratch,
        cost_estimate=cost,
        compiler_params=pltpu.CompilerParams(vmem_limit_bytes=room * MIB),
    )(*args)


def share(value, axis):
    copies = jnp.broadcast_to(value[None], (lax.axis_size(axis),) + value.shape)
    return lax.all_to_all(copies, axis, 0, 0, tiled=True)


def by_pair(pairs, build, *args):
    branches = [functools.partial(build, pair) for pair in range(pairs)]
    if pairs == 1:
        return branches[0](*args)
    return lax.switch(lax.axis_index("layer") // FEAT_SPLIT, branches, *args)


def body(inputs, encoder, enc_bias, decoder, dec_bias, targets, top_index):
    tokens, layers, top_count = top_index.shape
    depth, width = encoder.shape[1:]
    feat = decoder.shape[3]
    slab_most = 2 * top_count // lax.axis_size("lat")
    packed = tokens * layers * slab_most // LANES
    pairs = lax.axis_size("layer") // FEAT_SPLIT
    plan = (layers, width, top_count, slab_most)
    top = jnp.transpose(top_index, (1, 2, 0)).reshape(layers * top_count, tokens)
    dma = pltpu.SemaphoreType.DMA
    i32 = jnp.int32
    z, index = call(
        functools.partial(encode_kernel, plan),
        [HBM] * 4,
        [((packed, LANES), BF, VMEM), ((tokens, LANES), i32, VMEM)],
        [
            pltpu.VMEM(inputs.shape, BF),
            pltpu.VMEM(encoder.shape, BF),
            pltpu.VMEM(enc_bias.shape, F32),
            pltpu.VMEM(top.shape, i32),
            pltpu.VMEM((layers, tokens, depth), BF),
            dma((4,)),
        ],
        inputs, encoder, enc_bias, top,
    )
    parts = share(z, "layer")
    (inverse,) = call(
        functools.partial(inverse_kernel, plan),
        [VMEM],
        [((layers, tokens, width), i32, VMEM)],
        [],
        index,
        cost=pl.CostEstimate(flops=10**8, bytes_accessed=10**6, transcendentals=0),
    )

    def decode(pair, *args):
        return call(
            functools.partial(decode_kernel, plan, pair),
            [VMEM] * 4,
            [
                ((layers, tokens, width), BF, VMEM),
                ((2, tokens, feat), BF, VMEM),
                ((tokens, LANES), i32, VMEM),
            ],
            [],
            *args,
        )

    act, partial, index = by_pair(pairs, decode, parts, inverse, decoder[0], index)
    partials = lax.all_gather(partial, "lat")

    def residues(pair, *args):
        return call(
            functools.partial(residue_kernel, plan, pair),
            [VMEM] * 5,
            [((packed, LANES), BF, VMEM), ((2, tokens, feat), BF, VMEM)],
            [],
            *args,
        )

    z, residue = by_pair(
        pairs, residues, partials, dec_bias[0], jnp.swapaxes(targets[0], 0, 1), index, decoder[0]
    )
    parts = share(z, "layer")

    def decoder_grads(pair, *args):
        return call(
            functools.partial(decoder_grad_kernel, plan, pair),
            [VMEM] * 3,
            [((layers + 1, width, feat), F32, HBM), ((layers, depth, tokens), BF, VMEM)],
            [pltpu.VMEM((layers + 1, width, feat), F32), dma((layers + 1,))],
            *args,
            cost=pl.CostEstimate(
                flops=2 * (layers + 1) * tokens * width * feat,
                bytes_accessed=4 * (layers + 1) * width * feat,
                transcendentals=0,
            ),
        )

    decoder_grad, xt = by_pair(pairs, decoder_grads, act, residue, inputs)
    encoder_grad, bias_grad = call(
        functools.partial(encoder_grad_kernel, plan),
        [VMEM] * 3,
        [(encoder.shape, F32, HBM), (enc_bias.shape, F32, HBM)],
        [
            pltpu.VMEM((tokens, LANES), F32),
            pltpu.VMEM(encoder.shape, F32),
            pltpu.VMEM(enc_bias.shape, F32),
            dma((PARTS * layers,)),
            dma,
        ],
        parts, inverse, xt,
    )
    return decoder_grad[None], encoder_grad, bias_grad


def solution(mesh):
    return jax.shard_map(
        body,
        mesh=mesh,
        in_specs=(
            P(None, None, "layer"),
            P(None, "layer", "lat"),
            P(None, "lat"),
            P("layer", None, "lat", None),
            P("layer", None, None),
            P("layer", None, None, None),
            P(),
        ),
        out_specs=(P("layer", None, "lat", None), P(None, "layer", "lat"), P(None, "lat")),
        check_vma=False,
    )
```

time: 47.5 us -> 42.1 us (0.89)
  blocking collectives: 17.3 us -> 7.31 us
  waiting for transfers between devices: 6.42 us -> 10.6 us
  starting transfers between devices: 7.28 us -> 10.7 us
  local copies, waits for them, and re-layouts: 5.5 us -> 2.28 us
    all_to_all x1 -> x0, blocking collectives: 10.2 us -> none  [share(): return lax.all_to_all(copies, axis, 0, 0, tiled=True)]
    all_to_all x1 -> x2, waiting for transfers between devices: 6.42 us -> 10.6 us  [share(): return lax.all_to_all(copies, axis, 0, 0, tiled=True)]
    all_to_all x1 -> x2, starting transfers between devices: 7.28 us -> 10.7 us  [share(): return lax.all_to_all(copies, axis, 0, 0, tiled=True)]
    unnamed x10 -> x7, local copies, waits for them, and re-layouts: 3.77 us -> 0.93 us
    reshape x1 -> x0, local copies, waits for them, and re-layouts: 1.04 us -> none  [body(): top = top_index.reshape(tokens, -1)]
    broadcast_in_dim x2, local copies, waits for them, and re-layouts: 0.68 us -> 1.35 us  [share(): copies = jnp.broadcast_to(value[None], (lax.axis_size(axis),) + value.shape)]
    pallas_call x4 -> x6, Pallas kernels: 9.78 us -> 10.1 us  [call(): pl.pallas_call(kernel, out_shape=tuple(((pltpu.HBM if spec is HBM else pl...]
  transfers between devices with their start and end apart: 1 -> 2, of which waited for: 1 -> 2; matrix products, arithmetic and copies ran while one was open for 2% -> 2% of each run, Pallas kernels for 0% -> 8%
where the time goes in v2:
time: 42.1 us; the launch traced here: 41.6 us
  starting transfers between devices  10.7 us (25%)
  waiting for transfers between devices  10.6 us (25%)
  Pallas kernels  10.1 us (24%)
  blocking collectives  7.31 us (17%)
  local copies, waits for them, and re-layouts  2.28 us (5%)
  between operations  0.7 us (2%)
    all_to_all x2, starting transfers between devices, share(): return lax.all_to_all(copies, axis, 0, 0, tiled=True)  10.7 us
    all_to_all x2, waiting for transfers between devices, share(): return lax.all_to_all(copies, axis, 0, 0, tiled=True)  10.6 us
    pallas_call x6, Pallas kernels, call(): pl.pallas_call(kernel, out_shape=tuple(((pltpu.HBM if spec is HBM else pl...  10.1 us
    all_gather x1, blocking collectives, body(): partials = lax.all_gather(partial, 'lat')  7.31 us
    broadcast_in_dim x2, local copies, waits for them, and re-layouts, share(): copies = jnp.broadcast_to(value[None], (lax.axis_size(axis),) + value.shape)  1.35 us
    unnamed x7, local copies, waits for them, and re-layouts  0.93 us
  transfers between devices with their start and end apart: 2, of which 2 were waited for; matrix products, arithmetic and copies ran while one was open for 2% of the time, Pallas kernels for 8%

profile of v2, /device:TPU:0, one launch (start us, length us, event | category | flops | bytes accessed | tf_op | source)
XLA Modules:
  0.0 41.6 jit_solution(10403939214686799136)
XLA Ops:
  0.6 0.0 copy-start
  0.6 2.6 %shard_map.94 = (bf16[64,128]{1,0:T(8,128)(2,1)S(1)}, s32[128,128]{1,0:T(8,128)S(1)}) custom-call(bf16[128,2,256]{2,1,0:T(2,128)(2,1)} %x_ref.1, bf16[2,256,1024]{2,1,0:T(8,128)(2,1)} %encoder_hbm.1, f32[2,1024]{1,0:T(2,128)} %bias_hbm.1, s32[128,128]{1,0:T(8,128)} %bitcast.17), custom_call_target="tpu_custom_call" | custom-call | tf_op jit(solution)/shard_map/pallas_call | solution.py:279
  3.3 0.7 %broadcast_in_dim.6 = bf16[8,64,128]{2,1,0:T(8,128)(2,1)} broadcast(bf16[64,128]{1,0:T(8,128)(2,1)S(1)} %get-tuple-element.14), dimensions={1,2} | broadcast | bytes 147456 | tf_op jit(solution)/shard_map/broadcast_in_dim | solution.py:293
  4.0 7.3 %all-to-all-start = ((bf16[8,64,128]{2,1,0:T(8,128)(2,1)}), bf16[8,64,128]{2,1,0:T(8,128)(2,1)S(1)}, u32[]{:S(2)}, u32[]{:S(2)}) async-start(bf16[8,64,128]{2,1,0:T(8,128)(2,1)} %broadcast_in_dim.6), calls=%async_computation | async-start | bytes 262144 | tf_op jit(solution)/shard_map/all_to_all | solution.py:294
  11.2 0.9 %copy.13 = bf16[1,128,2,256]{3,1,2,0:T(8,128)(2,1)S(1)} copy(bf16[1,128,2,256]{3,2,1,0:T(2,128)(2,1)} %param.12) | data formatting | bytes 262144 | tf_op args[5]
  12.2 0.0 copy-start.2
  12.2 1.4 %shard_map.95.inverse_ref = s32[2,128,1024]{2,1,0:T(8,128)S(1)} custom-call(s32[128,128]{1,0:T(8,128)S(1)} %get-tuple-element.15.index_ref), custom_call_target="tpu_custom_call" | custom-call | flops 100000000 | bytes 1000000 | tf_op jit(solution)/shard_map/pallas_call | solution.py:279
  13.6 5.0 %all-to-all-done.parts_ref = bf16[8,64,128]{2,1,0:T(8,128)(2,1)S(1)} async-done(((bf16[8,64,128]{2,1,0:T(8,128)(2,1)}), bf16[8,64,128]{2,1,0:T(8,128)(2,1)S(1)}, u32[]{:S(2)}, u32[]{:S(2)}) %all-to-all-start) | async-done | bytes 131104 | tf_op jit(solution)/shard_map/all_to_all | solution.py:294
  18.6 0.0 copy-done
  18.6 0.9 %shard_map.96 = (bf16[2,128,1024]{2,1,0:T(8,128)(2,1)S(1)}, bf16[2,128,256]{2,1,0:T(8,128)(2,1)S(1)}, s32[128,128]{1,0:T(8,128)S(1)}) custom-call(bf16[8,64,128]{2,1,0:T(8,128)(2,1)S(1)} %all-to-all-done.parts_ref, s32[2,128,1024]{2,1,0:T(8,128)S(1)} %shard_map.95.inverse_ref, bf16[3,1024,256]{2,1,0:T(8,128)(2,1)S(1)} %bitcast.12, ...), custom_call_target="tpu_custom_call" | custom-call | tf_op jit(solution)/shard_map/pallas_call | solution.py:279
  19.5 0.0 copy-start.1
  19.5 7.3 %all-gather = bf16[8,128,256]{2,1,0:T(8,128)(2,1)S(1)} all-gather(bf16[2,128,256]{2,1,0:T(8,128)(2,1)S(1)} %get-tuple-element.17), channel_id=2, replica_groups=mesh['layer'=8,'lat'=4] {'lat'}, dimensions={0}, use_global_device_ids=true | all-gather | bytes 655360 | tf_op jit(solution)/shard_map/all_gather | solution.py:353
  26.8 0.0 copy-done.2
  26.8 1.0 %shard_map.97 = (bf16[64,128]{1,0:T(8,128)(2,1)S(1)}, bf16[2,128,256]{2,1,0:T(8,128)(2,1)S(1)}) custom-call(bf16[4,2,128,256]{3,2,1,0:T(8,128)(2,1)S(1)} %bitcast.14, f32[2,256]{1,0:T(2,128)S(1)} %bitcast.16, bf16[2,128,256]{2,1,0:T(8,128)(2,1)S(1)} %bitcast.15, s32[128,128]{1,0:T(8,128)S(1)} %get-tuple-element.18.index_ref, bf16[3,1024,256]{2,1,0:T(8,128)(2,1)S(1)} %bitcast.13), custom_call_target="tpu_custom_call" | custom-call | tf_op jit(solution)/shard_map/pallas_call | solution.py:279
  27.9 0.7 %broadcast_in_dim.8 = bf16[8,64,128]{2,1,0:T(8,128)(2,1)} broadcast(bf16[64,128]{1,0:T(8,128)(2,1)S(1)} %get-tuple-element.21), dimensions={1,2} | broadcast | bytes 147456 | tf_op jit(solution)/shard_map/broadcast_in_dim | solution.py:293
  28.5 3.4 %all-to-all-start.1 = ((bf16[8,64,128]{2,1,0:T(8,128)(2,1)}), bf16[8,64,128]{2,1,0:T(8,128)(2,1)S(1)}, u32[]{:S(2)}, u32[]{:S(2)}) async-start(bf16[8,64,128]{2,1,0:T(8,128)(2,1)} %broadcast_in_dim.8), calls=%async_computation.1 | async-start | bytes 262144 | tf_op jit(solution)/shard_map/all_to_all | solution.py:294
  31.9 0.0 copy-done.1
  31.9 2.1 %shard_map.98 = (f32[3,1024,256]{2,1,0:T(8,128)}, bf16[2,256,128]{2,1,0:T(8,128)(2,1)S(1)}) custom-call(bf16[2,128,1024]{2,1,0:T(8,128)(2,1)S(1)} %get-tuple-element.16.act_ref, bf16[2,128,256]{2,1,0:T(8,128)(2,1)S(1)} %get-tuple-element.19.residue_ref, bf16[128,2,256]{2,1,0:T(2,128)(2,1)S(1)} %copy-done.1), custom_call_target="tpu_custom_call" | custom-call | flops 201326592 | bytes 3145728 | tf_op jit(solution)/shard_map/pallas_call | solution.py:279
  34.0 5.6 %all-to-all-done.1.parts_ref = bf16[8,64,128]{2,1,0:T(8,128)(2,1)S(1)} async-done(((bf16[8,64,128]{2,1,0:T(8,128)(2,1)}), bf16[8,64,128]{2,1,0:T(8,128)(2,1)S(1)}, u32[]{:S(2)}, u32[]{:S(2)}) %all-to-all-start.1) | async-done | bytes 131104 | tf_op jit(solution)/shard_map/all_to_all | solution.py:294
  39.6 2.0 %shard_map.99 = (f32[2,256,1024]{2,1,0:T(8,128)}, f32[2,1024]{1,0:T(2,128)}) custom-call(bf16[8,64,128]{2,1,0:T(8,128)(2,1)S(1)} %all-to-all-done.1.parts_ref, s32[2,128,1024]{2,1,0:T(8,128)S(1)} %shard_map.95.inverse_ref, bf16[2,256,128]{2,1,0:T(8,128)(2,1)S(1)} %get-tuple-element.22.xt_ref), custom_call_target="tpu_custom_call" | custom-call | tf_op jit(solution)/shard_map/pallas_call | solution.py:279
Async XLA Ops:
  0.6 18.0 %copy-start = (bf16[1,3,1024,256]{3,2,1,0:T(8,128)(2,1)S(1)}, bf16[1,3,1024,256]{3,2,1,0:T(8,128)(2,1)}, u32[]{:S(2)}) copy-start(bf16[1,3,1024,256]{3,2,1,0:T(8,128)(2,1)} %param.10) | copy-start | bytes 4718596
  4.0 14.6 %all-to-all-start = ((bf16[8,64,128]{2,1,0:T(8,128)(2,1)}), bf16[8,64,128]{2,1,0:T(8,128)(2,1)S(1)}, u32[]{:S(2)}, u32[]{:S(2)}) async-start(bf16[8,64,128]{2,1,0:T(8,128)(2,1)} %broadcast_in_dim.6), calls=%async_computation | async-start | bytes 262144 | tf_op jit(solution)/shard_map/all_to_all | solution.py:294
  12.2 14.7 %copy-start.2 = (f32[1,2,256]{2,1,0:T(2,128)S(1)}, f32[1,2,256]{2,1,0:T(2,128)}, u32[]{:S(2)}) copy-start(f32[1,2,256]{2,1,0:T(2,128)} %param.11) | copy-start | bytes 6148
  19.5 12.4 %copy-start.1 = (bf16[128,2,256]{2,1,0:T(2,128)(2,1)S(1)}, bf16[128,2,256]{2,1,0:T(2,128)(2,1)}, u32[]{:S(2)}) copy-start(bf16[128,2,256]{2,1,0:T(2,128)(2,1)} %x_ref.1) | copy-start | bytes 393220
  28.5 11.1 %all-to-all-start.1 = ((bf16[8,64,128]{2,1,0:T(8,128)(2,1)}), bf16[8,64,128]{2,1,0:T(8,128)(2,1)S(1)}, u32[]{:S(2)}, u32[]{:S(2)}) async-start(bf16[8,64,128]{2,1,0:T(8,128)(2,1)} %broadcast_in_dim.8), calls=%async_computation.1 | async-start | bytes 262144 | tf_op jit(solution)/shard_map/all_to_all | solution.py:294

commit v3 on v2

v3 whole, which is shorter than its diff:
```python
import functools

import jax
import jax.numpy as jnp
from jax import lax
from jax.experimental import pallas as pl
from jax.experimental.pallas import tpu as pltpu
from jax.sharding import PartitionSpec as P

FEAT_SPLIT = 8
LANES = 128
PARTS = 4
CHUNK = 32
NUMBER_BITS = 7
WORD_BLOCKS = 31 // NUMBER_BITS

BF = jnp.bfloat16
F32 = jnp.float32
NT = (((1,), (1,)), ((), ()))
TN = (((0,), (0,)), ((), ()))


def matmul(left, right, dims=(((1,), (0,)), ((), ()))):
    return lax.dot_general(left, right, dims, preferred_element_type=F32)


def flag(condition):
    return jnp.where(condition, 1.0, 0.0).astype(BF)


def iota(shape, dimension):
    return lax.broadcasted_iota(jnp.int32, shape, dimension)


def pick_lanes(table, lanes):
    return jnp.take_along_axis(table, lanes, axis=1, mode="promise_in_bounds")


def choose(options, code):
    bit = 1
    while len(options) > 1:
        odd = (code & bit) != 0
        options = [
            jnp.where(odd, options[i + 1], options[i]) if i + 1 < len(options) else options[i]
            for i in range(0, len(options), 2)
        ]
        bit *= 2
    return options[0]


def stride(width):
    return 1 << (width // LANES - 1).bit_length()


def gather_slots(dense, index):
    lane = jnp.bitwise_and(index, LANES - 1)
    picked = [
        pick_lanes(dense[:, b * LANES : (b + 1) * LANES], lane)
        for b in range(dense.shape[1] // LANES)
    ]
    return choose(picked, lax.shift_right_logical(index, 7))


def join_layers(picked, index, width):
    total = choose(picked, lax.shift_right_logical(index, 7) // stride(width))
    return jnp.where(index < 0, 0.0, total)


def fold_slots(values, used):
    folds = LANES // used
    rows = values.shape[0] // folds
    total = values[:rows]
    for f in range(1, folds):
        total = total + pltpu.roll(values[f * rows : (f + 1) * rows], f * used, 1)
    return total


def sum_parts(parts_ref, used):
    total = jnp.sum(parts_ref[...].astype(F32), axis=0).astype(BF).astype(F32)
    folds = LANES // used
    total = jnp.concatenate(
        [pltpu.roll(total, (1 - f * used) % LANES, 1) for f in range(folds)], axis=0
    )
    lane = iota(total.shape, 1)
    return jnp.where((lane > 0) & (lane <= used), total, 0.0)


def place_slots(values, lane):
    blocks = lane.shape[1] // LANES
    return jnp.concatenate(
        [pick_lanes(values, lane[:, b * LANES : (b + 1) * LANES]).astype(BF) for b in range(blocks)],
        axis=1,
    )


def slot_index(top, slab, width, layers, top_count, slab_most):
    rows, tokens = top.shape
    place = jnp.bitwise_and(iota(top.shape, 0), top_count - 1)
    local = top - slab * width
    inside = (local >= 0) & (local < width)
    after = iota((rows, rows), 0)
    before = iota((rows, rows), 1)
    earlier = flag((before // top_count == after // top_count) & (before < after))
    rank = matmul(earlier, flag(inside)).astype(jnp.int32)
    local = local + (iota(top.shape, 0) // top_count) * (stride(width) * LANES)
    word = jnp.where(inside, (1 << 30) + ((place - rank) << 16) + local, 0)
    step = 0
    while (1 << step) < top_count:
        moved = pltpu.roll(word, rows - (1 << step), 0)
        bit = 1 << (16 + step)
        word = jnp.where((moved & bit) != 0, moved, jnp.where((word & bit) != 0, 0, word))
        step += 1
    index = jnp.where(word != 0, word & 0xFFFF, -1)
    return jnp.concatenate(
        [index[layer * top_count : layer * top_count + slab_most] for layer in range(layers)], axis=0
    )


def by_token(kept):
    spare = jnp.full((LANES - kept.shape[0], kept.shape[1]), -1, jnp.int32)
    return jnp.transpose(jnp.concatenate([kept, spare], axis=0), (1, 0))


def inverse_kernel(plan, kept_ref, inverse_ref, rows_ref):
    layers, width, top_count, slab_most = plan
    tokens = kept_ref.shape[1]
    blocks = width // LANES
    words = -(-blocks // WORD_BLOCKS)
    for layer in range(layers):
        own = kept_ref[layer * slab_most : (layer + 1) * slab_most, :]
        block = lax.shift_right_arithmetic(own, 7) - layer * stride(width)
        number = iota(own.shape, 0) + (1 + layer * slab_most)
        value = lax.shift_left(number, NUMBER_BITS * (block % WORD_BLOCKS))
        rows_ref[layer, 0] = jnp.bitwise_and(own, LANES - 1)
        for w in range(words):
            rows_ref[layer, 1 + w] = jnp.where((own >= 0) & (block // WORD_BLOCKS == w), value, 0)
        pieces = [[] for w in range(words)]
        for first in range(0, LANES, CHUNK):
            lane = iota((CHUNK, tokens), 0) + first
            totals = [jnp.zeros((CHUNK, tokens), jnp.int32) for w in range(words)]
            for s in range(slab_most):
                match = lane == rows_ref[layer, 0, s : s + 1, :]
                for w in range(words):
                    totals[w] = totals[w] + jnp.where(match, rows_ref[layer, 1 + w, s : s + 1, :], 0)
            for w in range(words):
                pieces[w].append(totals[w])
        for w in range(words):
            word = jnp.transpose(jnp.concatenate(pieces[w], axis=0), (1, 0))
            for b in range(w * WORD_BLOCKS, min((w + 1) * WORD_BLOCKS, blocks)):
                numbers = lax.shift_right_logical(word, NUMBER_BITS * (b % WORD_BLOCKS))
                inverse_ref[layer, :, b * LANES : (b + 1) * LANES] = jnp.bitwise_and(
                    numbers, LANES - 1
                )


def encode_kernel(
    plan, x_hbm, encoder_hbm, bias_hbm, top_hbm, z_ref, index_ref, kept_ref,
    x_ref, encoder_ref, bias_ref, top_ref, x_layer, sems
):
    layers, width, top_count, slab_most = plan
    copies = [
        pltpu.make_async_copy(source, target, sems.at[i])
        for i, (source, target) in enumerate(
            [(top_hbm, top_ref), (x_hbm, x_ref), (bias_hbm, bias_ref), (encoder_hbm, encoder_ref)]
        )
    ]
    for copy in copies:
        copy.start()
    for copy in copies[:2]:
        copy.wait()
    for layer in range(layers):
        x_layer[layer] = x_ref[:, layer, :]
    kept = slot_index(top_ref[...], lax.axis_index("lat"), width, layers, top_count, slab_most)
    kept_ref[...] = kept
    index = by_token(kept)
    index_ref[...] = index
    for copy in copies[2:]:
        copy.wait()
    with_bias = jnp.where(lax.axis_index("layer") == 0, 1.0, 0.0)
    picked = []
    for layer in range(layers):
        dense = matmul(x_layer[layer], encoder_ref[layer])
        dense = dense + bias_ref[layer : layer + 1, :] * with_bias
        picked.append(gather_slots(dense, index))
    z_ref[...] = fold_slots(join_layers(picked, index, width), layers * slab_most).astype(BF)


def block_places(layers, pair):
    return [(k, 0) if k <= pair else (k - pair - 1, 1) for k in range(layers + 1)]


def decode_kernel(
    plan, pair, parts_ref, inverse_ref, decoder_ref, index_ref, act_ref, partial_ref, index_out
):
    layers, width, top_count, slab_most = plan
    index_out[...] = index_ref[...]
    total = sum_parts(parts_ref, layers * slab_most)
    for layer in range(layers):
        act_ref[layer] = place_slots(total, inverse_ref[layer])
    sums = [None, None]
    for k, (source, slot) in enumerate(block_places(layers, pair)):
        term = matmul(act_ref[source], decoder_ref[k])
        sums[slot] = term if sums[slot] is None else sums[slot] + term
    for slot in range(2):
        partial_ref[slot] = sums[slot].astype(BF)


def turn_kernel(act_ref, x_ref, targets_ref, decoder_ref, act_t, x_t, targets_out, decoder_t):
    for layer in range(act_ref.shape[0]):
        act_t[layer] = jnp.transpose(act_ref[layer], (1, 0))
        x_t[layer] = jnp.transpose(x_ref[:, layer, :], (1, 0))
    for slot in range(2):
        targets_out[slot] = targets_ref[:, slot, :]
    for k in range(decoder_ref.shape[0]):
        decoder_t[k] = jnp.transpose(decoder_ref[k], (1, 0))


def residue_kernel(
    plan, pair, mine_ref, theirs_ref, dec_bias_ref, targets_ref, index_ref, decoder_t,
    z_ref, residue
):
    layers, width, top_count, slab_most = plan
    for slot in range(2):
        rebuilt = mine_ref[slot].astype(F32) + theirs_ref[slot].astype(F32)
        rebuilt = rebuilt + dec_bias_ref[slot : slot + 1, :]
        residue[slot] = (rebuilt - targets_ref[slot].astype(F32)).astype(BF)
    places = block_places(layers, pair)
    index = index_ref[...]
    picked = []
    for layer in range(layers):
        dense = None
        for k, (source, slot) in enumerate(places):
            if source == layer:
                term = matmul(residue[slot], decoder_t[k])
                dense = term if dense is None else dense + term
        picked.append(jnp.zeros(index.shape, F32) if dense is None else gather_slots(dense, index))
    z_ref[...] = fold_slots(join_layers(picked, index, width), layers * slab_most).astype(BF)


def grads_kernel(
    plan, pair, parts_ref, inverse_ref, x_t, act_t, residue_ref,
    decoder_hbm, encoder_hbm, bias_hbm, values, decoder_grad, encoder_grad, bias, sems
):
    layers, width, top_count, slab_most = plan
    tokens = x_t.shape[2]
    part = width // PARTS
    copies = []

    def send(source, target):
        copies.append(pltpu.make_async_copy(source, target, sems.at[len(copies)]))
        copies[-1].start()

    for k, (source, slot) in enumerate(block_places(layers, pair)):
        decoder_grad[k] = matmul(act_t[source], residue_ref[slot])
        send(decoder_grad.at[k], decoder_hbm.at[k])
    values[...] = sum_parts(parts_ref, layers * slab_most)
    ones = jnp.ones((8, tokens), BF)
    for layer in range(layers):
        for i in range(PARTS):
            at = (layer, slice(None), pl.ds(i * part, part))
            dense = place_slots(values[...], inverse_ref[at])
            encoder_grad[at] = matmul(x_t[layer], dense)
            send(encoder_grad.at[at], encoder_hbm.at[at])
            bias[layer : layer + 1, i * part : (i + 1) * part] = matmul(ones, dense)[:1]
    send(bias, bias_hbm)
    for copy in copies:
        copy.wait()


VMEM = pl.BlockSpec(memory_space=pltpu.VMEM)
HBM = pl.BlockSpec(memory_space=pltpu.HBM)
MIB = 1024 * 1024


def call(kernel, ins, outs, scratch, *args, cost=None, room=24):
    args = [
        pltpu.with_memory_space_constraint(arg, pltpu.HBM) if spec is HBM else arg
        for spec, arg in zip(ins, args, strict=True)
    ]
    return pl.pallas_call(
        kernel,
        out_shape=tuple(
            (pltpu.HBM if spec is HBM else pltpu.VMEM)(shape, dtype) for shape, dtype, spec in outs
        ),
        in_specs=ins,
        out_specs=tuple(spec for _, _, spec in outs),
        scratch_shapes=scratch,
        cost_estimate=cost,
        compiler_params=pltpu.CompilerParams(vmem_limit_bytes=room * MIB),
    )(*args)


def share(value, axis):
    copies = jnp.broadcast_to(value[None], (lax.axis_size(axis),) + value.shape)
    return lax.all_to_all(copies, axis, 0, 0, tiled=True)


def by_pair(pairs, build, *args):
    branches = [functools.partial(build, pair) for pair in range(pairs)]
    if pairs == 1:
        return branches[0](*args)
    return lax.switch(lax.axis_index("layer") // FEAT_SPLIT, branches, *args)


def across(value, axis, step):
    pairs = [(i, i ^ step) for i in range(lax.axis_size(axis))]
    return lax.ppermute(value, axis, pairs)


def body(inputs, encoder, enc_bias, decoder, dec_bias, targets, top_index):
    tokens, layers, top_count = top_index.shape
    depth, width = encoder.shape[1:]
    feat = decoder.shape[3]
    slabs = lax.axis_size("lat")
    slab_most = 2 * top_count // slabs
    packed = tokens * layers * slab_most // LANES
    pairs = lax.axis_size("layer") // FEAT_SPLIT
    plan = (layers, width, top_count, slab_most)
    top = jnp.transpose(top_index, (1, 2, 0)).reshape(layers * top_count, tokens)
    dma = pltpu.SemaphoreType.DMA
    i32 = jnp.int32
    z, index, kept = call(
        functools.partial(encode_kernel, plan),
        [HBM] * 4,
        [
            ((packed, LANES), BF, VMEM),
            ((tokens, LANES), i32, VMEM),
            ((layers * slab_most, tokens), i32, VMEM),
        ],
        [
            pltpu.VMEM(inputs.shape, BF),
            pltpu.VMEM(encoder.shape, BF),
            pltpu.VMEM(enc_bias.shape, F32),
            pltpu.VMEM(top.shape, i32),
            pltpu.VMEM((layers, tokens, depth), BF),
            dma((4,)),
        ],
        inputs, encoder, enc_bias, top,
    )
    parts = share(z, "layer")
    (inverse,) = call(
        functools.partial(inverse_kernel, plan),
        [VMEM],
        [((layers, tokens, width), i32, VMEM)],
        [pltpu.VMEM((layers, 1 - (-width // (LANES * WORD_BLOCKS)), slab_most, tokens), i32)],
        kept,
        cost=pl.CostEstimate(flops=10**8, bytes_accessed=10**6, transcendentals=0),
    )

    def decode(pair, *args):
        return call(
            functools.partial(decode_kernel, plan, pair),
            [VMEM] * 4,
            [
                ((layers, tokens, width), BF, VMEM),
                ((2, tokens, feat), BF, VMEM),
                ((tokens, LANES), i32, VMEM),
            ],
            [],
            *args,
        )

    act, partial, index = by_pair(pairs, decode, parts, inverse, decoder[0], index)
    step = 1
    while 2 * step < slabs:
        partial = (partial.astype(F32) + across(partial, "lat", step).astype(F32)).astype(BF)
        step *= 2
    partial, act = lax.optimization_barrier((partial, act))
    theirs = across(partial, "lat", step)
    act_t, x_t, targets_by_slot, decoder_t = call(
        turn_kernel,
        [VMEM] * 4,
        [
            ((layers, width, tokens), BF, VMEM),
            ((layers, depth, tokens), BF, VMEM),
            ((2, tokens, feat), BF, VMEM),
            ((layers + 1, feat, width), BF, VMEM),
        ],
        [],
        act, inputs, targets[0], decoder[0],
        cost=pl.CostEstimate(flops=10**8, bytes_accessed=10**7, transcendentals=0),
    )

    def residues(pair, *args):
        return call(
            functools.partial(residue_kernel, plan, pair),
            [VMEM] * 6,
            [((packed, LANES), BF, VMEM), ((2, tokens, feat), BF, VMEM)],
            [],
            *args,
        )

    z, residue = by_pair(
        pairs, residues, partial, theirs, dec_bias[0], targets_by_slot, index, decoder_t
    )
    parts = share(z, "layer")

    def grads(pair, *args):
        return call(
            functools.partial(grads_kernel, plan, pair),
            [VMEM] * 5,
            [
                ((layers + 1, width, feat), F32, HBM),
                (encoder.shape, F32, HBM),
                (enc_bias.shape, F32, HBM),
            ],
            [
                pltpu.VMEM((tokens, LANES), F32),
                pltpu.VMEM((layers + 1, width, feat), F32),
                pltpu.VMEM(encoder.shape, F32),
                pltpu.VMEM(enc_bias.shape, F32),
                dma((PARTS * layers + layers + 2,)),
            ],
            *args,
        )

    decoder_grad, encoder_grad, bias_grad = by_pair(
        pairs, grads, parts, inverse, x_t, act_t, residue
    )
    return decoder_grad[None], encoder_grad, bias_grad


def solution(mesh):
    return jax.shard_map(
        body,
        mesh=mesh,
        in_specs=(
            P(None, None, "layer"),
            P(None, "layer", "lat"),
            P(None, "lat"),
            P("layer", None, "lat", None),
            P("layer", None, None),
            P("layer", None, None, None),
            P(),
        ),
        out_specs=(P("layer", None, "lat", None), P(None, "layer", "lat"), P(None, "lat")),
        check_vma=False,
    )
```

time: 42.1 us -> 40.4 us (0.960)
  blocking collectives: 7.31 us -> 9.74 us
  starting transfers between devices: 10.7 us -> 8.9 us
  local copies, waits for them, and re-layouts: 2.28 us -> 0.71 us
  Pallas kernels: 10.1 us -> 9.54 us
    all_to_all x0 -> x1, blocking collectives: none -> 9.74 us  [share(): return lax.all_to_all(copies, axis, 0, 0, tiled=True)]
    all_gather x1 -> x0, blocking collectives: 7.31 us -> none  [body(): partials = lax.all_gather(partial, 'lat')]
    all_to_all x2 -> x1, waiting for transfers between devices: 10.6 us -> 6.23 us  [share(): return lax.all_to_all(copies, axis, 0, 0, tiled=True)]
    ppermute x0 -> x2, waiting for transfers between devices: none -> 4.25 us  [across(): return lax.ppermute(value, axis, pairs)]
    all_to_all x2 -> x1, starting transfers between devices: 10.7 us -> 7.28 us  [share(): return lax.all_to_all(copies, axis, 0, 0, tiled=True)]
    ppermute x0 -> x2, starting transfers between devices: none -> 1.62 us  [across(): return lax.ppermute(value, axis, pairs)]
    unnamed x7 -> x8, local copies, waits for them, and re-layouts: 0.93 us -> 0.02 us
    broadcast_in_dim x2, local copies, waits for them, and re-layouts: 1.35 us -> 0.69 us  [share(): copies = jnp.broadcast_to(value[None], (lax.axis_size(axis),) + value.shape)]
  transfers between devices with their start and end apart: 2 -> 3, of which waited for: 2 -> 3; matrix products, arithmetic and copies ran while one was open for 2% -> 0% of each run, Pallas kernels for 8% -> 6%
where the time goes in v3:
time: 40.4 us; the launch traced here: 40.1 us
  waiting for transfers between devices  10.5 us (26%)
  blocking collectives  9.74 us (24%)
  Pallas kernels  9.54 us (24%)
  starting transfers between devices  8.9 us (22%)
  local copies, waits for them, and re-layouts  0.71 us (2%)
  between operations  0.7 us (2%)
    all_to_all x1, blocking collectives, share(): return lax.all_to_all(copies, axis, 0, 0, tiled=True)  9.74 us
    pallas_call x6, Pallas kernels, call(): pl.pallas_call(kernel, out_shape=tuple(((pltpu.HBM if spec is HBM else pl...  9.54 us
    all_to_all x1, starting transfers between devices, share(): return lax.all_to_all(copies, axis, 0, 0, tiled=True)  7.28 us
    all_to_all x1, waiting for transfers between devices, share(): return lax.all_to_all(copies, axis, 0, 0, tiled=True)  6.23 us
    ppermute x2, waiting for transfers between devices, across(): return lax.ppermute(value, axis, pairs)  4.25 us
    ppermute x2, starting transfers between devices, across(): return lax.ppermute(value, axis, pairs)  1.62 us
  transfers between devices with their start and end apart: 3, of which 3 were waited for; matrix products, arithmetic and copies ran while one was open for 0% of the time, Pallas kernels for 6%

profile of v3, /device:TPU:0, one launch (start us, length us, event | category | flops | bytes accessed | tf_op | source)
XLA Modules:
  0.0 40.1 jit_solution(5622301055582499648)
XLA Ops:
  0.6 0.0 copy-start
  0.6 2.6 %shard_map.94 = (bf16[64,128]{1,0:T(8,128)(2,1)S(1)}, s32[128,128]{1,0:T(8,128)S(1)}, s32[64,128]{1,0:T(8,128)S(1)}) custom-call(bf16[128,2,256]{2,1,0:T(2,128)(2,1)} %x_ref.1, bf16[2,256,1024]{2,1,0:T(8,128)(2,1)} %encoder_hbm.1, f32[2,1024]{1,0:T(2,128)} %bias_hbm.1, s32[128,128]{1,0:T(8,128)} %bitcast.11), custom_call_target="tpu_custom_call" | custom-call | tf_op jit(solution)/shard_map/pallas_call | solution.py:280
  3.3 0.7 %broadcast_in_dim.6 = bf16[8,64,128]{2,1,0:T(8,128)(2,1)} broadcast(bf16[64,128]{1,0:T(8,128)(2,1)S(1)} %get-tuple-element.20), dimensions={1,2} | broadcast | bytes 147456 | tf_op jit(solution)/shard_map/broadcast_in_dim | solution.py:294
  4.0 7.3 %all-to-all-start = ((bf16[8,64,128]{2,1,0:T(8,128)(2,1)}), bf16[8,64,128]{2,1,0:T(8,128)(2,1)S(1)}, u32[]{:S(2)}, u32[]{:S(2)}) async-start(bf16[8,64,128]{2,1,0:T(8,128)(2,1)} %broadcast_in_dim.6), calls=%async_computation | async-start | bytes 262144 | tf_op jit(solution)/shard_map/all_to_all | solution.py:295
  11.2 0.0 copy-start.1
  11.2 0.0 copy-start.2
  11.3 1.1 %shard_map.95.inverse_ref = s32[2,128,1024]{2,1,0:T(8,128)S(1)} custom-call(s32[64,128]{1,0:T(8,128)S(1)} %get-tuple-element.21.kept_ref), custom_call_target="tpu_custom_call" | custom-call | flops 100000000 | bytes 1000000 | tf_op jit(solution)/shard_map/pallas_call | solution.py:280
  12.3 6.2 %all-to-all-done.parts_ref = bf16[8,64,128]{2,1,0:T(8,128)(2,1)S(1)} async-done(((bf16[8,64,128]{2,1,0:T(8,128)(2,1)}), bf16[8,64,128]{2,1,0:T(8,128)(2,1)S(1)}, u32[]{:S(2)}, u32[]{:S(2)}) %all-to-all-start) | async-done | bytes 131104 | tf_op jit(solution)/shard_map/all_to_all | solution.py:295
  18.6 0.0 copy-done
  18.6 0.0 copy-start.3
  18.6 1.0 %shard_map.96 = (bf16[2,128,1024]{2,1,0:T(8,128)(2,1)S(1)}, bf16[2,128,256]{2,1,0:T(8,128)(2,1)S(1)}, s32[128,128]{1,0:T(8,128)S(1)}) custom-call(bf16[8,64,128]{2,1,0:T(8,128)(2,1)S(1)} %all-to-all-done.parts_ref, s32[2,128,1024]{2,1,0:T(8,128)S(1)} %shard_map.95.inverse_ref, bf16[3,1024,256]{2,1,0:T(8,128)(2,1)S(1)} %bitcast.7, ...), custom_call_target="tpu_custom_call" | custom-call | tf_op jit(solution)/shard_map/pallas_call | solution.py:280
  19.6 0.1 collective-permute-start
  19.6 1.3 %collective-permute-done = bf16[2,128,256]{2,1,0:T(8,128)(2,1)S(1)} collective-permute-done((bf16[2,128,256]{2,1,0:T(8,128)(2,1)S(1)}, bf16[2,128,256]{2,1,0:T(8,128)(2,1)S(1)}, u32[]{:S(2)}, u32[]{:S(2)}) %collective-permute-start) | collective-permute-done | bytes 131104 | tf_op jit(solution)/shard_map/ppermute | solution.py:307
  21.0 1.6 %collective-permute-start.1 = (bf16[2,128,256]{2,1,0:T(8,128)(2,1)S(1)}, bf16[2,128,256]{2,1,0:T(8,128)(2,1)S(1)}, u32[]{:S(2)}, u32[]{:S(2)}) collective-permute-start(bf16[2,128,256]{2,1,0:T(8,128)(2,1)S(1)} %add_convert_fusion.mine_ref), channel_id=1, source_target_pairs={{0,2},{1,3},{2,0},{3,1},{4,6},{5,7},{6,4},{7,5},{8,10},{9,11},{10,... | collective-permute-start | bytes 393224 | tf_op jit(solution)/shard_map/ppermute | solution.py:307
  22.6 0.0 copy-done.1
  22.6 0.0 copy-done.2
  22.6 1.1 %shard_map.97 = (bf16[2,1024,128]{2,1,0:T(8,128)(2,1)S(1)}, bf16[2,256,128]{2,1,0:T(8,128)(2,1)S(1)}, bf16[2,128,256]{2,1,0:T(8,128)(2,1)S(1)}, bf16[3,256,1024]{2,1,0:T(8,128)(2,1)S(1)}) custom-call(bf16[2,128,1024]{2,1,0:T(8,128)(2,1)S(1)} %get-tuple-element.26.act_ref, bf16[128,2,256]{2,1,0:T(2,128)(2,1)S(1)} %copy-done.1, ...), custom_call_target="tpu_custom_call" | custom-call | flops 100000000 | bytes 10000000 | tf_op jit(solution)/shard_map/pallas_call | solution.py:280
  23.7 2.9 %collective-permute-done.1.theirs_ref = bf16[2,128,256]{2,1,0:T(8,128)(2,1)S(1)} collective-permute-done((bf16[2,128,256]{2,1,0:T(8,128)(2,1)S(1)}, bf16[2,128,256]{2,1,0:T(8,128)(2,1)S(1)}, u32[]{:S(2)}, u32[]{:S(2)}) %collective-permute-start.1) | collective-permute-done | bytes 131104 | tf_op jit(solution)/shard_map/ppermute | solution.py:307
  26.6 0.0 copy-done.3
  26.6 0.9 %shard_map.98 = (bf16[64,128]{1,0:T(8,128)(2,1)S(1)}, bf16[2,128,256]{2,1,0:T(8,128)(2,1)S(1)}) custom-call(bf16[2,128,256]{2,1,0:T(8,128)(2,1)S(1)} %add_convert_fusion.mine_ref, bf16[2,128,256]{2,1,0:T(8,128)(2,1)S(1)} %collective-permute-done.1.theirs_ref, f32[2,256]{1,0:T(2,128)S(1)} %bitcast.10, bf16[2,128,256]{2,1,0:T(8,128)(2,1)S(1)} %get-tuple-element.27.targets_ref, ...), custom_call_target="tpu_custom_call" | custom-call | tf_op jit(solution)/shard_map/pallas_call | solution.py:280
  27.5 9.7 %all_to_all.10.parts_ref = bf16[8,64,128]{2,1,0:T(8,128)(2,1)S(1)} all-to-all(bf16[8,64,128]{2,1,0:T(8,128)(2,1)S(1)} %broadcast_in_dim.7), channel_id=1, replica_groups=mesh['layer'=8,'lat'=4] {'layer'}, dimensions={0} | all-to-all | bytes 262144 | tf_op jit(solution)/shard_map/all_to_all | solution.py:295
  37.3 2.8 %shard_map.99 = (f32[3,1024,256]{2,1,0:T(8,128)}, f32[2,256,1024]{2,1,0:T(8,128)}, f32[2,1024]{1,0:T(2,128)}) custom-call(bf16[8,64,128]{2,1,0:T(8,128)(2,1)S(1)} %all_to_all.10.parts_ref, s32[2,128,1024]{2,1,0:T(8,128)S(1)} %shard_map.95.inverse_ref, bf16[2,256,128]{2,1,0:T(8,128)(2,1)S(1)} %get-tuple-element.31.x_t, ...), custom_call_target="tpu_custom_call" | custom-call | tf_op jit(solution)/shard_map/pallas_call | solution.py:280
  (2 shorter events, 0.1 us)
Async XLA Ops:
  0.6 18.0 %copy-start = (bf16[1,3,1024,256]{3,2,1,0:T(8,128)(2,1)S(1)}, bf16[1,3,1024,256]{3,2,1,0:T(8,128)(2,1)}, u32[]{:S(2)}) copy-start(bf16[1,3,1024,256]{3,2,1,0:T(8,128)(2,1)} %param.10) | copy-start | bytes 4718596
  4.0 14.6 %all-to-all-start = ((bf16[8,64,128]{2,1,0:T(8,128)(2,1)}), bf16[8,64,128]{2,1,0:T(8,128)(2,1)S(1)}, u32[]{:S(2)}, u32[]{:S(2)}) async-start(bf16[8,64,128]{2,1,0:T(8,128)(2,1)} %broadcast_in_dim.6), calls=%async_computation | async-start | bytes 262144 | tf_op jit(solution)/shard_map/all_to_all | solution.py:295
  11.2 11.3 %copy-start.1 = (bf16[128,2,256]{2,1,0:T(2,128)(2,1)S(1)}, bf16[128,2,256]{2,1,0:T(2,128)(2,1)}, u32[]{:S(2)}) copy-start(bf16[128,2,256]{2,1,0:T(2,128)(2,1)} %x_ref.1) | copy-start | bytes 393220
  11.2 11.3 %copy-start.2 = (bf16[1,128,2,256]{3,2,1,0:T(2,128)(2,1)S(1)}, bf16[1,128,2,256]{3,2,1,0:T(2,128)(2,1)}, u32[]{:S(2)}) copy-start(bf16[1,128,2,256]{3,2,1,0:T(2,128)(2,1)} %param.12) | copy-start | bytes 393220
  18.6 8.1 %copy-start.3 = (f32[1,2,256]{2,1,0:T(2,128)S(1)}, f32[1,2,256]{2,1,0:T(2,128)}, u32[]{:S(2)}) copy-start(f32[1,2,256]{2,1,0:T(2,128)} %param.11) | copy-start | bytes 6148
  19.6 1.4 %collective-permute-start = (bf16[2,128,256]{2,1,0:T(8,128)(2,1)S(1)}, bf16[2,128,256]{2,1,0:T(8,128)(2,1)S(1)}, u32[]{:S(2)}, u32[]{:S(2)}) collective-permute-start(bf16[2,128,256]{2,1,0:T(8,128)(2,1)S(1)} %get-tuple-element.23), channel_id=1, source_target_pairs={{0,1},{1,0},{2,3},{3,2},{4,5},{5,4},{6,7},{7,6},{8,9},{9,8},{10,11... | collective-permute-start | bytes 393224 | tf_op jit(solution)/shard_map/ppermute | solution.py:307
  21.0 5.6 %collective-permute-start.1 = (bf16[2,128,256]{2,1,0:T(8,128)(2,1)S(1)}, bf16[2,128,256]{2,1,0:T(8,128)(2,1)S(1)}, u32[]{:S(2)}, u32[]{:S(2)}) collective-permute-start(bf16[2,128,256]{2,1,0:T(8,128)(2,1)S(1)} %add_convert_fusion.mine_ref), channel_id=1, source_target_pairs={{0,2},{1,3},{2,0},{3,1},{4,6},{5,7},{6,4},{7,5},{8,10},{9,11},{10,... | collective-permute-start | bytes 393224 | tf_op jit(solution)/shard_map/ppermute | solution.py:307

commit v4 on v3

--- a/solution.py
+++ b/solution.py
@@ -33,13 +33,24 @@
 
 
 def pick_lanes(table, lanes):
-    return jnp.take_along_axis(table, lanes, axis=1, mode="promise_in_bounds")
-
-
-def choose(options, code):
-    bit = 1
+    return lax.gather(
+        table,
+        lanes[..., None],
+        lax.GatherDimensionNumbers(
+            offset_dims=(),
+            collapsed_slice_dims=(1,),
+            start_index_map=(1,),
+            operand_batching_dims=(0,),
+            start_indices_batching_dims=(0,),
+        ),
+        slice_sizes=(1, 1),
+        mode=lax.GatherScatterMode.PROMISE_IN_BOUNDS,
+    )
+
+
+def choose(options, index, bit):
     while len(options) > 1:
-        odd = (code & bit) != 0
+        odd = jnp.bitwise_and(index, jnp.int16(bit)) != 0
         options = [
             jnp.where(odd, options[i + 1], options[i]) if i + 1 < len(options) else options[i]
             for i in range(0, len(options), 2)
@@ -53,17 +64,17 @@
 
 
 def gather_slots(dense, index):
-    lane = jnp.bitwise_and(index, LANES - 1)
+    lane = jnp.bitwise_and(index, jnp.int16(LANES - 1))
     picked = [
-        pick_lanes(dense[:, b * LANES : (b + 1) * LANES], lane)
+        pick_lanes(dense[:, b * LANES : (b + 1) * LANES].astype(BF), lane)
         for b in range(dense.shape[1] // LANES)
     ]
-    return choose(picked, lax.shift_right_logical(index, 7))
+    return choose(picked, index, LANES)
 
 
 def join_layers(picked, index, width):
-    total = choose(picked, lax.shift_right_logical(index, 7) // stride(width))
-    return jnp.where(index < 0, 0.0, total)
+    total = choose(picked, index, LANES * stride(width))
+    return jnp.where(index < 0, jnp.zeros_like(total), total).astype(F32)
 
 
 def fold_slots(values, used):
@@ -76,19 +87,19 @@
 
 
 def sum_parts(parts_ref, used):
-    total = jnp.sum(parts_ref[...].astype(F32), axis=0).astype(BF).astype(F32)
+    total = jnp.sum(parts_ref[...].astype(F32), axis=0)
     folds = LANES // used
     total = jnp.concatenate(
         [pltpu.roll(total, (1 - f * used) % LANES, 1) for f in range(folds)], axis=0
     )
     lane = iota(total.shape, 1)
-    return jnp.where((lane > 0) & (lane <= used), total, 0.0)
+    return jnp.where((lane > 0) & (lane <= used), total, 0.0).astype(BF)
 
 
 def place_slots(values, lane):
     blocks = lane.shape[1] // LANES
     return jnp.concatenate(
-        [pick_lanes(values, lane[:, b * LANES : (b + 1) * LANES]).astype(BF) for b in range(blocks)],
+        [pick_lanes(values, lane[:, b * LANES : (b + 1) * LANES]) for b in range(blocks)],
         axis=1,
     )
 
@@ -150,7 +161,7 @@
                 numbers = lax.shift_right_logical(word, NUMBER_BITS * (b % WORD_BLOCKS))
                 inverse_ref[layer, :, b * LANES : (b + 1) * LANES] = jnp.bitwise_and(
                     numbers, LANES - 1
-                )
+                ).astype(jnp.int16)
 
 
 def encode_kernel(
@@ -168,11 +179,14 @@
         copy.start()
     for copy in copies[:2]:
         copy.wait()
-    for layer in range(layers):
-        x_layer[layer] = x_ref[:, layer, :]
+    tokens, depth = x_ref.shape[0], x_ref.shape[2]
+    x_rows = x_ref[...].reshape(tokens * layers, depth)
+    token, row = iota((tokens, tokens * layers), 0), iota((tokens, tokens * layers), 1)
+    for layer in range(layers):
+        x_layer[layer] = matmul(flag(row == layers * token + layer), x_rows).astype(BF)
     kept = slot_index(top_ref[...], lax.axis_index("lat"), width, layers, top_count, slab_most)
     kept_ref[...] = kept
-    index = by_token(kept)
+    index = by_token(kept).astype(jnp.int16)
     index_ref[...] = index
     for copy in copies[2:]:
         copy.wait()
@@ -190,7 +204,8 @@
 
 
 def decode_kernel(
-    plan, pair, parts_ref, inverse_ref, decoder_ref, index_ref, act_ref, partial_ref, index_out
+    plan, pair, parts_ref, inverse_ref, decoder_ref, index_ref,
+    act_ref, partial_ref, rounded_ref, index_out
 ):
     layers, width, top_count, slab_most = plan
     index_out[...] = index_ref[...]
@@ -202,7 +217,8 @@
         term = matmul(act_ref[source], decoder_ref[k])
         sums[slot] = term if sums[slot] is None else sums[slot] + term
     for slot in range(2):
-        partial_ref[slot] = sums[slot].astype(BF)
+        partial_ref[slot] = sums[slot]
+        rounded_ref[slot] = sums[slot].astype(BF)
 
 
 def turn_kernel(act_ref, x_ref, targets_ref, decoder_ref, act_t, x_t, targets_out, decoder_t):
@@ -221,7 +237,7 @@
 ):
     layers, width, top_count, slab_most = plan
     for slot in range(2):
-        rebuilt = mine_ref[slot].astype(F32) + theirs_ref[slot].astype(F32)
+        rebuilt = mine_ref[slot] + theirs_ref[slot].astype(F32)
         rebuilt = rebuilt + dec_bias_ref[slot : slot + 1, :]
         residue[slot] = (rebuilt - targets_ref[slot].astype(F32)).astype(BF)
     places = block_places(layers, pair)
@@ -233,7 +249,7 @@
             if source == layer:
                 term = matmul(residue[slot], decoder_t[k])
                 dense = term if dense is None else dense + term
-        picked.append(jnp.zeros(index.shape, F32) if dense is None else gather_slots(dense, index))
+        picked.append(jnp.zeros(index.shape, BF) if dense is None else gather_slots(dense, index))
     z_ref[...] = fold_slots(join_layers(picked, index, width), layers * slab_most).astype(BF)
 
 
@@ -251,8 +267,10 @@
         copies[-1].start()
 
     for k, (source, slot) in enumerate(block_places(layers, pair)):
-        decoder_grad[k] = matmul(act_t[source], residue_ref[slot])
-        send(decoder_grad.at[k], decoder_hbm.at[k])
+        for i in range(PARTS):
+            rows = pl.ds(i * part, part)
+            decoder_grad[k, rows] = matmul(act_t[source, rows], residue_ref[slot])
+            send(decoder_grad.at[k, rows], decoder_hbm.at[k, rows])
     values[...] = sum_parts(parts_ref, layers * slab_most)
     ones = jnp.ones((8, tokens), BF)
     for layer in range(layers):
@@ -318,13 +336,13 @@
     plan = (layers, width, top_count, slab_most)
     top = jnp.transpose(top_index, (1, 2, 0)).reshape(layers * top_count, tokens)
     dma = pltpu.SemaphoreType.DMA
-    i32 = jnp.int32
+    i16, i32 = jnp.int16, jnp.int32
     z, index, kept = call(
         functools.partial(encode_kernel, plan),
         [HBM] * 4,
         [
             ((packed, LANES), BF, VMEM),
-            ((tokens, LANES), i32, VMEM),
+            ((tokens, LANES), i16, VMEM),
             ((layers * slab_most, tokens), i32, VMEM),
         ],
         [
@@ -341,7 +359,7 @@
     (inverse,) = call(
         functools.partial(inverse_kernel, plan),
         [VMEM],
-        [((layers, tokens, width), i32, VMEM)],
+        [((layers, tokens, width), i16, VMEM)],
         [pltpu.VMEM((layers, 1 - (-width // (LANES * WORD_BLOCKS)), slab_most, tokens), i32)],
         kept,
         cost=pl.CostEstimate(flops=10**8, bytes_accessed=10**6, transcendentals=0),
@@ -353,20 +371,22 @@
             [VMEM] * 4,
             [
                 ((layers, tokens, width), BF, VMEM),
+                ((2, tokens, feat), F32, VMEM),
                 ((2, tokens, feat), BF, VMEM),
-                ((tokens, LANES), i32, VMEM),
+                ((tokens, LANES), i16, VMEM),
             ],
             [],
             *args,
         )
 
-    act, partial, index = by_pair(pairs, decode, parts, inverse, decoder[0], index)
+    act, mine, sent, index = by_pair(pairs, decode, parts, inverse, decoder[0], index)
     step = 1
     while 2 * step < slabs:
-        partial = (partial.astype(F32) + across(partial, "lat", step).astype(F32)).astype(BF)
+        mine = mine + across(sent, "lat", step).astype(F32)
+        sent = mine.astype(BF)
         step *= 2
-    partial, act = lax.optimization_barrier((partial, act))
-    theirs = across(partial, "lat", step)
+    sent, act = lax.optimization_barrier((sent, act))
+    theirs = across(sent, "lat", step)
     act_t, x_t, targets_by_slot, decoder_t = call(
         turn_kernel,
         [VMEM] * 4,
@@ -391,7 +411,7 @@
         )
 
     z, residue = by_pair(
-        pairs, residues, partial, theirs, dec_bias[0], targets_by_slot, index, decoder_t
+        pairs, residues, mine, theirs, dec_bias[0], targets_by_slot, index, decoder_t
     )
     parts = share(z, "layer")
 
@@ -405,11 +425,11 @@
                 (enc_bias.shape, F32, HBM),
             ],
             [
-                pltpu.VMEM((tokens, LANES), F32),
+                pltpu.VMEM((tokens, LANES), BF),
                 pltpu.VMEM((layers + 1, width, feat), F32),
                 pltpu.VMEM(encoder.shape, F32),
                 pltpu.VMEM(enc_bias.shape, F32),
-                dma((PARTS * layers + layers + 2,)),
+                dma((PARTS * (2 * layers + 1) + 1,)),
             ],
             *args,
         )

time: 40.4 us -> 39.1 us (0.968)
  Pallas kernels: 9.54 us -> 8.22 us
    pallas_call x6, Pallas kernels: 9.54 us -> 8.22 us  [call(): pl.pallas_call(kernel, out_shape=tuple(((pltpu.HBM if spec is HBM else pl...]
where the time goes in v4:
time: 39.1 us; the launch traced here: 38.8 us
  waiting for transfers between devices  10.5 us (27%)
  blocking collectives  9.74 us (25%)
  starting transfers between devices  8.91 us (23%)
  Pallas kernels  8.22 us (21%)
  local copies, waits for them, and re-layouts  0.72 us (2%)
  between operations  0.71 us (2%)
    all_to_all x1, blocking collectives, share(): return lax.all_to_all(copies, axis, 0, 0, tiled=True)  9.74 us
    pallas_call x6, Pallas kernels, call(): pl.pallas_call(kernel, out_shape=tuple(((pltpu.HBM if spec is HBM else pl...  8.22 us
    all_to_all x1, starting transfers between devices, share(): return lax.all_to_all(copies, axis, 0, 0, tiled=True)  7.28 us
    all_to_all x1, waiting for transfers between devices, share(): return lax.all_to_all(copies, axis, 0, 0, tiled=True)  6.24 us
    ppermute x2, waiting for transfers between devices, across(): return lax.ppermute(value, axis, pairs)  4.25 us
    ppermute x2, starting transfers between devices, across(): return lax.ppermute(value, axis, pairs)  1.62 us
  transfers between devices with their start and end apart: 3, of which 3 were waited for; matrix products, arithmetic and copies ran while one was open for 0% of the time, Pallas kernels for 6%

profile of v4, /device:TPU:0, one launch (start us, length us, event | category | flops | bytes accessed | tf_op | source)
XLA Modules:
  0.0 38.8 jit_solution(6928748442279018941)
XLA Ops:
  0.6 0.0 copy-start
  0.6 2.0 %shard_map.94 = (bf16[64,128]{1,0:T(8,128)(2,1)S(1)}, s16[128,128]{1,0:T(8,128)(2,1)S(1)}, s32[64,128]{1,0:T(8,128)S(1)}) custom-call(bf16[128,2,256]{2,1,0:T(2,128)(2,1)} %x_ref.1, bf16[2,256,1024]{2,1,0:T(8,128)(2,1)} %encoder_hbm.1, f32[2,1024]{1,0:T(2,128)} %bias_hbm.1, s32[128,128]{1,0:T(8,128)} %bitcast.11), custom_call_target="tpu_custom_call" | custom-call | tf_op jit(solution)/shard_map/pallas_call | solution.py:298
  2.7 0.0 copy-start.1
  2.7 0.0 copy-start.2
  2.7 0.7 %broadcast_in_dim.6 = bf16[8,64,128]{2,1,0:T(8,128)(2,1)} broadcast(bf16[64,128]{1,0:T(8,128)(2,1)S(1)} %get-tuple-element.21), dimensions={1,2} | broadcast | bytes 147456 | tf_op jit(solution)/shard_map/broadcast_in_dim | solution.py:312
  3.4 7.3 %all-to-all-start = ((bf16[8,64,128]{2,1,0:T(8,128)(2,1)}), bf16[8,64,128]{2,1,0:T(8,128)(2,1)S(1)}, u32[]{:S(2)}, u32[]{:S(2)}) async-start(bf16[8,64,128]{2,1,0:T(8,128)(2,1)} %broadcast_in_dim.6), calls=%async_computation | async-start | bytes 262144 | tf_op jit(solution)/shard_map/all_to_all | solution.py:313
  10.7 1.1 %shard_map.95.inverse_ref = s16[2,128,1024]{2,1,0:T(8,128)(2,1)S(1)} custom-call(s32[64,128]{1,0:T(8,128)S(1)} %get-tuple-element.22.kept_ref), custom_call_target="tpu_custom_call" | custom-call | flops 100000000 | bytes 1000000 | tf_op jit(solution)/shard_map/pallas_call | solution.py:298
  11.8 6.2 %all-to-all-done.parts_ref = bf16[8,64,128]{2,1,0:T(8,128)(2,1)S(1)} async-done(((bf16[8,64,128]{2,1,0:T(8,128)(2,1)}), bf16[8,64,128]{2,1,0:T(8,128)(2,1)S(1)}, u32[]{:S(2)}, u32[]{:S(2)}) %all-to-all-start) | async-done | bytes 131104 | tf_op jit(solution)/shard_map/all_to_all | solution.py:313
  18.0 0.0 copy-done
  18.0 0.6 %shard_map.96 = (bf16[2,128,1024]{2,1,0:T(8,128)(2,1)S(1)}, f32[2,128,256]{2,1,0:T(8,128)S(1)}, bf16[2,128,256]{2,1,0:T(8,128)(2,1)S(1)}, s16[128,128]{1,0:T(8,128)(2,1)S(1)}) custom-call(bf16[8,64,128]{2,1,0:T(8,128)(2,1)S(1)} %all-to-all-done.parts_ref, s16[2,128,1024]{2,1,0:T(8,128)(2,1)S(1)} %shard_map.95.inverse_ref, bf16[3,1024,256]{2,1,0:T(8,128)(2,1)S(1)} %bitcast.7, ...), custom_call_target="tpu_custom_call" | custom-call | tf_op jit(solution)/shard_map/pallas_call | solution.py:298
  18.6 0.0 copy-start.3
  18.6 0.1 collective-permute-start
  18.7 1.3 %collective-permute-done = bf16[2,128,256]{2,1,0:T(8,128)(2,1)S(1)} collective-permute-done((bf16[2,128,256]{2,1,0:T(8,128)(2,1)S(1)}, bf16[2,128,256]{2,1,0:T(8,128)(2,1)S(1)}, u32[]{:S(2)}, u32[]{:S(2)}) %collective-permute-start) | collective-permute-done | bytes 131104 | tf_op jit(solution)/shard_map/ppermute | solution.py:325
  20.1 1.6 %collective-permute-start.1 = (bf16[2,128,256]{2,1,0:T(8,128)(2,1)S(1)}, bf16[2,128,256]{2,1,0:T(8,128)(2,1)S(1)}, u32[]{:S(2)}, u32[]{:S(2)}) collective-permute-start(bf16[2,128,256]{2,1,0:T(8,128)(2,1)S(1)} %get-tuple-element.27), channel_id=1, source_target_pairs={{0,2},{1,3},{2,0},{3,1},{4,6},{5,7},{6,4},{7,5},{8,10},{9,11},{10,... | collective-permute-start | bytes 393224 | tf_op jit(solution)/shard_map/ppermute | solution.py:325
  21.7 0.0 copy-done.1
  21.7 0.0 copy-done.2
  21.7 1.1 %shard_map.97 = (bf16[2,1024,128]{2,1,0:T(8,128)(2,1)S(1)}, bf16[2,256,128]{2,1,0:T(8,128)(2,1)S(1)}, bf16[2,128,256]{2,1,0:T(8,128)(2,1)S(1)}, bf16[3,256,1024]{2,1,0:T(8,128)(2,1)S(1)}) custom-call(bf16[2,128,1024]{2,1,0:T(8,128)(2,1)S(1)} %get-tuple-element.28.act_ref, bf16[128,2,256]{2,1,0:T(2,128)(2,1)S(1)} %copy-done.1, ...), custom_call_target="tpu_custom_call" | custom-call | flops 100000000 | bytes 10000000 | tf_op jit(solution)/shard_map/pallas_call | solution.py:298
  22.8 2.9 %collective-permute-done.1.theirs_ref = bf16[2,128,256]{2,1,0:T(8,128)(2,1)S(1)} collective-permute-done((bf16[2,128,256]{2,1,0:T(8,128)(2,1)S(1)}, bf16[2,128,256]{2,1,0:T(8,128)(2,1)S(1)}, u32[]{:S(2)}, u32[]{:S(2)}) %collective-permute-start.1) | collective-permute-done | bytes 131104 | tf_op jit(solution)/shard_map/ppermute | solution.py:325
  25.7 0.0 copy-done.3
  25.7 0.6 %shard_map.98 = (bf16[64,128]{1,0:T(8,128)(2,1)S(1)}, bf16[2,128,256]{2,1,0:T(8,128)(2,1)S(1)}) custom-call(f32[2,128,256]{2,1,0:T(8,128)S(1)} %get-tuple-element.40.mine_ref, bf16[2,128,256]{2,1,0:T(8,128)(2,1)S(1)} %collective-permute-done.1.theirs_ref, f32[2,256]{1,0:T(2,128)S(1)} %bitcast.10, bf16[2,128,256]{2,1,0:T(8,128)(2,1)S(1)} %get-tuple-element.29.targets_ref, ...), custom_call_target="tpu_custom_call" | custom-call | tf_op jit(solution)/shard_map/pallas_call | solution.py:298
  26.4 9.7 %all_to_all.10.parts_ref = bf16[8,64,128]{2,1,0:T(8,128)(2,1)S(1)} all-to-all(bf16[8,64,128]{2,1,0:T(8,128)(2,1)S(1)} %broadcast_in_dim.7), channel_id=1, replica_groups=mesh['layer'=8,'lat'=4] {'layer'}, dimensions={0} | all-to-all | bytes 262144 | tf_op jit(solution)/shard_map/all_to_all | solution.py:313
  36.1 2.7 %shard_map.99 = (f32[3,1024,256]{2,1,0:T(8,128)}, f32[2,256,1024]{2,1,0:T(8,128)}, f32[2,1024]{1,0:T(2,128)}) custom-call(bf16[8,64,128]{2,1,0:T(8,128)(2,1)S(1)} %all_to_all.10.parts_ref, s16[2,128,1024]{2,1,0:T(8,128)(2,1)S(1)} %shard_map.95.inverse_ref, bf16[2,256,128]{2,1,0:T(8,128)(2,1)S(1)} %get-tuple-element.33.x_t, ...), custom_call_target="tpu_custom_call" | custom-call | tf_op jit(solution)/shard_map/pallas_call | solution.py:298
  (2 shorter events, 0.1 us)
Async XLA Ops:
  0.6 17.4 %copy-start = (bf16[1,3,1024,256]{3,2,1,0:T(8,128)(2,1)S(1)}, bf16[1,3,1024,256]{3,2,1,0:T(8,128)(2,1)}, u32[]{:S(2)}) copy-start(bf16[1,3,1024,256]{3,2,1,0:T(8,128)(2,1)} %param.10) | copy-start | bytes 4718596
  2.7 19.0 %copy-start.1 = (bf16[128,2,256]{2,1,0:T(2,128)(2,1)S(1)}, bf16[128,2,256]{2,1,0:T(2,128)(2,1)}, u32[]{:S(2)}) copy-start(bf16[128,2,256]{2,1,0:T(2,128)(2,1)} %x_ref.1) | copy-start | bytes 393220
  2.7 19.0 %copy-start.2 = (bf16[1,128,2,256]{3,2,1,0:T(2,128)(2,1)S(1)}, bf16[1,128,2,256]{3,2,1,0:T(2,128)(2,1)}, u32[]{:S(2)}) copy-start(bf16[1,128,2,256]{3,2,1,0:T(2,128)(2,1)} %param.12) | copy-start | bytes 393220
  3.4 14.6 %all-to-all-start = ((bf16[8,64,128]{2,1,0:T(8,128)(2,1)}), bf16[8,64,128]{2,1,0:T(8,128)(2,1)S(1)}, u32[]{:S(2)}, u32[]{:S(2)}) async-start(bf16[8,64,128]{2,1,0:T(8,128)(2,1)} %broadcast_in_dim.6), calls=%async_computation | async-start | bytes 262144 | tf_op jit(solution)/shard_map/all_to_all | solution.py:313
  18.6 7.1 %copy-start.3 = (f32[1,2,256]{2,1,0:T(2,128)S(1)}, f32[1,2,256]{2,1,0:T(2,128)}, u32[]{:S(2)}) copy-start(f32[1,2,256]{2,1,0:T(2,128)} %param.11) | copy-start | bytes 6148
  18.6 1.4 %collective-permute-start = (bf16[2,128,256]{2,1,0:T(8,128)(2,1)S(1)}, bf16[2,128,256]{2,1,0:T(8,128)(2,1)S(1)}, u32[]{:S(2)}, u32[]{:S(2)}) collective-permute-start(bf16[2,128,256]{2,1,0:T(8,128)(2,1)S(1)} %get-tuple-element.25), channel_id=1, source_target_pairs={{0,1},{1,0},{2,3},{3,2},{4,5},{5,4},{6,7},{7,6},{8,9},{9,8},{10,11... | collective-permute-start | bytes 393224 | tf_op jit(solution)/shard_map/ppermute | solution.py:325
  20.1 5.6 %collective-permute-start.1 = (bf16[2,128,256]{2,1,0:T(8,128)(2,1)S(1)}, bf16[2,128,256]{2,1,0:T(8,128)(2,1)S(1)}, u32[]{:S(2)}, u32[]{:S(2)}) collective-permute-start(bf16[2,128,256]{2,1,0:T(8,128)(2,1)S(1)} %get-tuple-element.27), channel_id=1, source_target_pairs={{0,2},{1,3},{2,0},{3,1},{4,6},{5,7},{6,4},{7,5},{8,10},{9,11},{10,... | collective-permute-start | bytes 393224 | tf_op jit(solution)/shard_map/ppermute | solution.py:325

commit v5 on v4

--- a/solution.py
+++ b/solution.py
@@ -205,7 +205,7 @@
 
 def decode_kernel(
     plan, pair, parts_ref, inverse_ref, decoder_ref, index_ref,
-    act_ref, partial_ref, rounded_ref, index_out
+    act_ref, first_ref, second_ref, first_rounded, second_rounded, index_out
 ):
     layers, width, top_count, slab_most = plan
     index_out[...] = index_ref[...]
@@ -216,9 +216,10 @@
     for k, (source, slot) in enumerate(block_places(layers, pair)):
         term = matmul(act_ref[source], decoder_ref[k])
         sums[slot] = term if sums[slot] is None else sums[slot] + term
-    for slot in range(2):
-        partial_ref[slot] = sums[slot]
-        rounded_ref[slot] = sums[slot].astype(BF)
+    first_ref[...] = sums[0]
+    second_ref[...] = sums[1]
+    first_rounded[...] = sums[0].astype(BF)
+    second_rounded[...] = sums[1].astype(BF)
 
 
 def turn_kernel(act_ref, x_ref, targets_ref, decoder_ref, act_t, x_t, targets_out, decoder_t):
@@ -232,12 +233,12 @@
 
 
 def residue_kernel(
-    plan, pair, mine_ref, theirs_ref, dec_bias_ref, targets_ref, index_ref, decoder_t,
+    plan, pair, mine_a, mine_b, theirs_a, theirs_b, dec_bias_ref, targets_ref, index_ref, decoder_t,
     z_ref, residue
 ):
     layers, width, top_count, slab_most = plan
-    for slot in range(2):
-        rebuilt = mine_ref[slot] + theirs_ref[slot].astype(F32)
+    for slot, (mine, theirs) in enumerate([(mine_a, theirs_a), (mine_b, theirs_b)]):
+        rebuilt = mine[...] + theirs[...].astype(F32)
         rebuilt = rebuilt + dec_bias_ref[slot : slot + 1, :]
         residue[slot] = (rebuilt - targets_ref[slot].astype(F32)).astype(BF)
     places = block_places(layers, pair)
@@ -371,22 +372,28 @@
             [VMEM] * 4,
             [
                 ((layers, tokens, width), BF, VMEM),
-                ((2, tokens, feat), F32, VMEM),
-                ((2, tokens, feat), BF, VMEM),
+                ((tokens, feat), F32, VMEM),
+                ((tokens, feat), F32, VMEM),
+                ((tokens, feat), BF, VMEM),
+                ((tokens, feat), BF, VMEM),
                 ((tokens, LANES), i16, VMEM),
             ],
             [],
             *args,
         )
 
-    act, mine, sent, index = by_pair(pairs, decode, parts, inverse, decoder[0], index)
-    step = 1
-    while 2 * step < slabs:
-        mine = mine + across(sent, "lat", step).astype(F32)
-        sent = mine.astype(BF)
-        step *= 2
-    sent, act = lax.optimization_barrier((sent, act))
-    theirs = across(sent, "lat", step)
+    act, mine_a, mine_b, sent_a, sent_b, index = by_pair(
+        pairs, decode, parts, inverse, decoder[0], index
+    )
+    steps = [1 << i for i in range(slabs.bit_length() - 1)]
+    for i, step in enumerate(steps):
+        theirs_a = across(sent_a, "lat", step)
+        theirs_b = across(sent_b, "lat", steps[-1 - i])
+        if i + 1 < len(steps):
+            mine_a = mine_a + theirs_a.astype(F32)
+            mine_b = mine_b + theirs_b.astype(F32)
+            sent_a, sent_b = mine_a.astype(BF), mine_b.astype(BF)
+            sent_a, act = lax.optimization_barrier((sent_a, act))
     act_t, x_t, targets_by_slot, decoder_t = call(
         turn_kernel,
         [VMEM] * 4,
@@ -404,14 +411,14 @@
     def residues(pair, *args):
         return call(
             functools.partial(residue_kernel, plan, pair),
-            [VMEM] * 6,
+            [VMEM] * 8,
             [((packed, LANES), BF, VMEM), ((2, tokens, feat), BF, VMEM)],
             [],
             *args,
         )
 
     z, residue = by_pair(
-        pairs, residues, mine, theirs, dec_bias[0], targets_by_slot, index, decoder_t
+        pairs, residues, mine_a, mine_b, theirs_a, theirs_b, dec_bias[0], targets_by_slot, index, decoder_t
     )
     parts = share(z, "layer")
 

time: 39.1 us -> 38.6 us (0.987)
  waiting for transfers between devices: 10.5 us -> 8.14 us
  starting transfers between devices: 8.91 us -> 10.2 us
  blocking collectives: 9.74 us -> 10.3 us
    ppermute x2 -> x4, waiting for transfers between devices: 4.25 us -> 1.9 us  [across(): return lax.ppermute(value, axis, pairs)]
    ppermute x2 -> x4, starting transfers between devices: 1.62 us -> 2.93 us  [across(): return lax.ppermute(value, axis, pairs)]
    all_to_all x1, blocking collectives: 9.74 us -> 10.3 us  [share(): return lax.all_to_all(copies, axis, 0, 0, tiled=True)]
  transfers between devices with their start and end apart: 3 -> 5, of which waited for: 3 -> 3; matrix products, arithmetic and copies ran while one was open for 0% -> 0% of each run, Pallas kernels for 6% -> 6%
where the time goes in v5:
time: 38.6 us; the launch traced here: 38.3 us
  blocking collectives  10.3 us (27%)
  starting transfers between devices  10.2 us (26%)
  Pallas kernels  8.22 us (21%)
  waiting for transfers between devices  8.14 us (21%)
  between operations  0.75 us (2%)
  local copies, waits for them, and re-layouts  0.72 us (2%)
    all_to_all x1, blocking collectives, share(): return lax.all_to_all(copies, axis, 0, 0, tiled=True)  10.3 us
    pallas_call x6, Pallas kernels, call(): pl.pallas_call(kernel, out_shape=tuple(((pltpu.HBM if spec is HBM else pl...  8.22 us
    all_to_all x1, starting transfers between devices, share(): return lax.all_to_all(copies, axis, 0, 0, tiled=True)  7.28 us
    all_to_all x1, waiting for transfers between devices, share(): return lax.all_to_all(copies, axis, 0, 0, tiled=True)  6.24 us
    ppermute x4, starting transfers between devices, across(): return lax.ppermute(value, axis, pairs)  2.93 us
    ppermute x4, waiting for transfers between devices, across(): return lax.ppermute(value, axis, pairs)  1.9 us
  transfers between devices with their start and end apart: 5, of which 3 were waited for; matrix products, arithmetic and copies ran while one was open for 0% of the time, Pallas kernels for 6%

profile of v5, /device:TPU:0, one launch (start us, length us, event | category | flops | bytes accessed | tf_op | source)
XLA Modules:
  0.0 38.3 jit_solution(5700056078545525531)
XLA Ops:
  0.6 0.0 copy-start
  0.6 2.0 %shard_map.94 = (bf16[64,128]{1,0:T(8,128)(2,1)S(1)}, s16[128,128]{1,0:T(8,128)(2,1)S(1)}, s32[64,128]{1,0:T(8,128)S(1)}) custom-call(bf16[128,2,256]{2,1,0:T(2,128)(2,1)} %x_ref.1, bf16[2,256,1024]{2,1,0:T(8,128)(2,1)} %encoder_hbm.1, f32[2,1024]{1,0:T(2,128)} %bias_hbm.1, s32[128,128]{1,0:T(8,128)} %bitcast.11), custom_call_target="tpu_custom_call" | custom-call | tf_op jit(solution)/shard_map/pallas_call | solution.py:299
  2.7 0.0 copy-start.1
  2.7 0.0 copy-start.2
  2.7 0.7 %broadcast_in_dim.6 = bf16[8,64,128]{2,1,0:T(8,128)(2,1)} broadcast(bf16[64,128]{1,0:T(8,128)(2,1)S(1)} %get-tuple-element.23), dimensions={1,2} | broadcast | bytes 147456 | tf_op jit(solution)/shard_map/broadcast_in_dim | solution.py:313
  3.4 7.3 %all-to-all-start = ((bf16[8,64,128]{2,1,0:T(8,128)(2,1)}), bf16[8,64,128]{2,1,0:T(8,128)(2,1)S(1)}, u32[]{:S(2)}, u32[]{:S(2)}) async-start(bf16[8,64,128]{2,1,0:T(8,128)(2,1)} %broadcast_in_dim.6), calls=%async_computation | async-start | bytes 262144 | tf_op jit(solution)/shard_map/all_to_all | solution.py:314
  10.7 1.1 %shard_map.95.inverse_ref = s16[2,128,1024]{2,1,0:T(8,128)(2,1)S(1)} custom-call(s32[64,128]{1,0:T(8,128)S(1)} %get-tuple-element.24.kept_ref), custom_call_target="tpu_custom_call" | custom-call | flops 100000000 | bytes 1000000 | tf_op jit(solution)/shard_map/pallas_call | solution.py:299
  11.8 6.2 %all-to-all-done.parts_ref = bf16[8,64,128]{2,1,0:T(8,128)(2,1)S(1)} async-done(((bf16[8,64,128]{2,1,0:T(8,128)(2,1)}), bf16[8,64,128]{2,1,0:T(8,128)(2,1)S(1)}, u32[]{:S(2)}, u32[]{:S(2)}) %all-to-all-start) | async-done | bytes 131104 | tf_op jit(solution)/shard_map/all_to_all | solution.py:314
  18.0 0.0 copy-done
  18.0 0.6 %shard_map.96 = (bf16[2,128,1024]{2,1,0:T(8,128)(2,1)S(1)}, f32[128,256]{1,0:T(8,128)S(1)}, f32[128,256]{1,0:T(8,128)S(1)}, bf16[128,256]{1,0:T(8,128)(2,1)S(1)}...) custom-call(bf16[8,64,128]{2,1,0:T(8,128)(2,1)S(1)} %all-to-all-done.parts_ref, ...), custom_call_target="tpu_custom_call" | custom-call | tf_op jit(solution)/shard_map/pallas_call | solution.py:299
  18.6 0.0 copy-start.3
  18.6 0.1 collective-permute-start
  18.7 1.6 %collective-permute-start.1 = (bf16[128,256]{1,0:T(8,128)(2,1)S(1)}, bf16[128,256]{1,0:T(8,128)(2,1)S(1)}, u32[]{:S(2)}, u32[]{:S(2)}) collective-permute-start(bf16[128,256]{1,0:T(8,128)(2,1)S(1)} %get-tuple-element.29), channel_id=1, source_target_pairs={{0,2},{1,3},{2,0},{3,1},{4,6},{5,7},{6,4},{7,5},{8,10},{9,11},{10,... | collective-permute-start | bytes 196616 | tf_op jit(solution)/shard_map/ppermute | solution.py:326
  20.3 0.0 collective-permute-done
  20.3 1.2 %collective-permute-start.2 = (bf16[128,256]{1,0:T(8,128)(2,1)S(1)}, bf16[128,256]{1,0:T(8,128)(2,1)S(1)}, u32[]{:S(2)}, u32[]{:S(2)}) collective-permute-start(bf16[128,256]{1,0:T(8,128)(2,1)S(1)} %get-tuple-element.31), channel_id=1, source_target_pairs={{0,2},{1,3},{2,0},{3,1},{4,6},{5,7},{6,4},{7,5},{8,10},{9,11},{10,... | collective-permute-start | bytes 196616 | tf_op jit(solution)/shard_map/ppermute | solution.py:326
  21.5 1.8 %collective-permute-done.1 = bf16[128,256]{1,0:T(8,128)(2,1)S(1)} collective-permute-done((bf16[128,256]{1,0:T(8,128)(2,1)S(1)}, bf16[128,256]{1,0:T(8,128)(2,1)S(1)}, u32[]{:S(2)}, u32[]{:S(2)}) %collective-permute-start.1) | collective-permute-done | bytes 65568 | tf_op jit(solution)/shard_map/ppermute | solution.py:326
  23.4 0.1 collective-permute-start.3
  23.5 0.0 copy-done.1
  23.5 1.1 %shard_map.97 = (bf16[2,1024,128]{2,1,0:T(8,128)(2,1)S(1)}, bf16[2,256,128]{2,1,0:T(8,128)(2,1)S(1)}, bf16[2,128,256]{2,1,0:T(8,128)(2,1)S(1)}, bf16[3,256,1024]{2,1,0:T(8,128)(2,1)S(1)}) custom-call(bf16[2,128,1024]{2,1,0:T(8,128)(2,1)S(1)} %get-tuple-element.32.act_ref, bf16[128,2,256]{2,1,0:T(2,128)(2,1)S(1)} %copy-done.1, ...), custom_call_target="tpu_custom_call" | custom-call | flops 100000000 | bytes 10000000 | tf_op jit(solution)/shard_map/pallas_call | solution.py:299
  24.6 0.0 collective-permute-done.2.theirs_a
  24.6 0.1 collective-permute-done.3.theirs_b
  24.7 0.6 %shard_map.98 = (bf16[64,128]{1,0:T(8,128)(2,1)S(1)}, bf16[2,128,256]{2,1,0:T(8,128)(2,1)S(1)}) custom-call(f32[128,256]{1,0:T(8,128)S(1)} %get-tuple-element.46.mine_a, f32[128,256]{1,0:T(8,128)S(1)} %get-tuple-element.44.mine_b, bf16[128,256]{1,0:T(8,128)(2,1)S(1)} %collective-permute-done.2.theirs_a, ...), custom_call_target="tpu_custom_call" | custom-call | tf_op jit(solution)/shard_map/pallas_call | solution.py:299
  25.4 10.3 %all_to_all.10.parts_ref = bf16[8,64,128]{2,1,0:T(8,128)(2,1)S(1)} all-to-all(bf16[8,64,128]{2,1,0:T(8,128)(2,1)S(1)} %broadcast_in_dim.7), channel_id=1, replica_groups=mesh['layer'=8,'lat'=4] {'layer'}, dimensions={0} | all-to-all | bytes 262144 | tf_op jit(solution)/shard_map/all_to_all | solution.py:314
  35.6 2.7 %shard_map.99 = (f32[3,1024,256]{2,1,0:T(8,128)}, f32[2,256,1024]{2,1,0:T(8,128)}, f32[2,1024]{1,0:T(2,128)}) custom-call(bf16[8,64,128]{2,1,0:T(8,128)(2,1)S(1)} %all_to_all.10.parts_ref, s16[2,128,1024]{2,1,0:T(8,128)(2,1)S(1)} %shard_map.95.inverse_ref, bf16[2,256,128]{2,1,0:T(8,128)(2,1)S(1)} %get-tuple-element.37.x_t, ...), custom_call_target="tpu_custom_call" | custom-call | tf_op jit(solution)/shard_map/pallas_call | solution.py:299
  (5 shorter events, 0.1 us)
Async XLA Ops:
  0.6 17.4 %copy-start = (bf16[1,3,1024,256]{3,2,1,0:T(8,128)(2,1)S(1)}, bf16[1,3,1024,256]{3,2,1,0:T(8,128)(2,1)}, u32[]{:S(2)}) copy-start(bf16[1,3,1024,256]{3,2,1,0:T(8,128)(2,1)} %param.10) | copy-start | bytes 4718596
  2.7 20.8 %copy-start.1 = (bf16[128,2,256]{2,1,0:T(2,128)(2,1)S(1)}, bf16[128,2,256]{2,1,0:T(2,128)(2,1)}, u32[]{:S(2)}) copy-start(bf16[128,2,256]{2,1,0:T(2,128)(2,1)} %x_ref.1) | copy-start | bytes 393220
  2.7 20.8 %copy-start.2 = (bf16[1,128,2,256]{3,2,1,0:T(2,128)(2,1)S(1)}, bf16[1,128,2,256]{3,2,1,0:T(2,128)(2,1)}, u32[]{:S(2)}) copy-start(bf16[1,128,2,256]{3,2,1,0:T(2,128)(2,1)} %param.12) | copy-start | bytes 393220
  3.4 14.6 %all-to-all-start = ((bf16[8,64,128]{2,1,0:T(8,128)(2,1)}), bf16[8,64,128]{2,1,0:T(8,128)(2,1)S(1)}, u32[]{:S(2)}, u32[]{:S(2)}) async-start(bf16[8,64,128]{2,1,0:T(8,128)(2,1)} %broadcast_in_dim.6), calls=%async_computation | async-start | bytes 262144 | tf_op jit(solution)/shard_map/all_to_all | solution.py:314
  18.6 6.1 %copy-start.3 = (f32[1,2,256]{2,1,0:T(2,128)S(1)}, f32[1,2,256]{2,1,0:T(2,128)}, u32[]{:S(2)}) copy-start(f32[1,2,256]{2,1,0:T(2,128)} %param.11) | copy-start | bytes 6148
  18.6 1.6 %collective-permute-start = (bf16[128,256]{1,0:T(8,128)(2,1)S(1)}, bf16[128,256]{1,0:T(8,128)(2,1)S(1)}, u32[]{:S(2)}, u32[]{:S(2)}) collective-permute-start(bf16[128,256]{1,0:T(8,128)(2,1)S(1)} %get-tuple-element.27), channel_id=1, source_target_pairs={{0,1},{1,0},{2,3},{3,2},{4,5},{5,4},{6,7},{7,6},{8,9},{9,8},{10,11... | collective-permute-start | bytes 196616 | tf_op jit(solution)/shard_map/ppermute | solution.py:326
  18.7 4.6 %collective-permute-start.1 = (bf16[128,256]{1,0:T(8,128)(2,1)S(1)}, bf16[128,256]{1,0:T(8,128)(2,1)S(1)}, u32[]{:S(2)}, u32[]{:S(2)}) collective-permute-start(bf16[128,256]{1,0:T(8,128)(2,1)S(1)} %get-tuple-element.29), channel_id=1, source_target_pairs={{0,2},{1,3},{2,0},{3,1},{4,6},{5,7},{6,4},{7,5},{8,10},{9,11},{10,... | collective-permute-start | bytes 196616 | tf_op jit(solution)/shard_map/ppermute | solution.py:326
  20.3 4.3 %collective-permute-start.2 = (bf16[128,256]{1,0:T(8,128)(2,1)S(1)}, bf16[128,256]{1,0:T(8,128)(2,1)S(1)}, u32[]{:S(2)}, u32[]{:S(2)}) collective-permute-start(bf16[128,256]{1,0:T(8,128)(2,1)S(1)} %get-tuple-element.31), channel_id=1, source_target_pairs={{0,2},{1,3},{2,0},{3,1},{4,6},{5,7},{6,4},{7,5},{8,10},{9,11},{10,... | collective-permute-start | bytes 196616 | tf_op jit(solution)/shard_map/ppermute | solution.py:326
  23.4 1.3 %collective-permute-start.3 = (bf16[128,256]{1,0:T(8,128)(2,1)S(1)}, bf16[128,256]{1,0:T(8,128)(2,1)S(1)}, u32[]{:S(2)}, u32[]{:S(2)}) collective-permute-start(bf16[128,256]{1,0:T(8,128)(2,1)S(1)} %get-tuple-element.43), channel_id=1, source_target_pairs={{0,1},{1,0},{2,3},{3,2},{4,5},{5,4},{6,7},{7,6},{8,9},{9,8},{10,11... | collective-permute-start | bytes 196616 | tf_op jit(solution)/shard_map/ppermute | solution.py:326

commit v6 on v5

--- a/solution.py
+++ b/solution.py
@@ -74,26 +74,23 @@
 
 def join_layers(picked, index, width):
     total = choose(picked, index, LANES * stride(width))
-    return jnp.where(index < 0, jnp.zeros_like(total), total).astype(F32)
+    return jnp.where(index < 0, jnp.zeros_like(total), total)
 
 
 def fold_slots(values, used):
-    folds = LANES // used
-    rows = values.shape[0] // folds
+    rows = values.shape[0] * used // LANES
     total = values[:rows]
-    for f in range(1, folds):
-        total = total + pltpu.roll(values[f * rows : (f + 1) * rows], f * used, 1)
+    for first in range(rows, values.shape[0], rows):
+        total = total + values[first : first + rows]
     return total
 
 
 def sum_parts(parts_ref, used):
     total = jnp.sum(parts_ref[...].astype(F32), axis=0)
-    folds = LANES // used
-    total = jnp.concatenate(
-        [pltpu.roll(total, (1 - f * used) % LANES, 1) for f in range(folds)], axis=0
-    )
-    lane = iota(total.shape, 1)
-    return jnp.where((lane > 0) & (lane <= used), total, 0.0).astype(BF)
+    part = iota(total.shape, 1) // used
+    return jnp.concatenate(
+        [jnp.where(part == f, total, 0.0).astype(BF) for f in range(LANES // used)], axis=0
+    )
 
 
 def place_slots(values, lane):
@@ -128,8 +125,12 @@
 
 
 def by_token(kept):
-    spare = jnp.full((LANES - kept.shape[0], kept.shape[1]), -1, jnp.int32)
-    return jnp.transpose(jnp.concatenate([kept, spare], axis=0), (1, 0))
+    used, tokens = kept.shape
+    folds = LANES // used
+    part = iota(kept.shape, 1) // (tokens // folds)
+    return jnp.transpose(
+        jnp.concatenate([jnp.where(part == f, kept, -1) for f in range(folds)], axis=0), (1, 0)
+    )
 
 
 def inverse_kernel(plan, kept_ref, inverse_ref, rows_ref):
@@ -137,6 +138,9 @@
     tokens = kept_ref.shape[1]
     blocks = width // LANES
     words = -(-blocks // WORD_BLOCKS)
+    used = layers * slab_most
+    part = iota((tokens, LANES), 0) // (tokens * used // LANES)
+    unused = (part + 1) % (LANES // used) * used
     for layer in range(layers):
         own = kept_ref[layer * slab_most : (layer + 1) * slab_most, :]
         block = lax.shift_right_arithmetic(own, 7) - layer * stride(width)
@@ -159,9 +163,9 @@
             word = jnp.transpose(jnp.concatenate(pieces[w], axis=0), (1, 0))
             for b in range(w * WORD_BLOCKS, min((w + 1) * WORD_BLOCKS, blocks)):
                 numbers = lax.shift_right_logical(word, NUMBER_BITS * (b % WORD_BLOCKS))
-                inverse_ref[layer, :, b * LANES : (b + 1) * LANES] = jnp.bitwise_and(
-                    numbers, LANES - 1
-                ).astype(jnp.int16)
+                numbers = jnp.bitwise_and(numbers, LANES - 1)
+                lanes = jnp.where(numbers > 0, numbers - 1 + part * used, unused)
+                inverse_ref[layer, :, b * LANES : (b + 1) * LANES] = lanes.astype(jnp.int16)
 
 
 def encode_kernel(
@@ -196,7 +200,7 @@
         dense = matmul(x_layer[layer], encoder_ref[layer])
         dense = dense + bias_ref[layer : layer + 1, :] * with_bias
         picked.append(gather_slots(dense, index))
-    z_ref[...] = fold_slots(join_layers(picked, index, width), layers * slab_most).astype(BF)
+    z_ref[...] = fold_slots(join_layers(picked, index, width), layers * slab_most)
 
 
 def block_places(layers, pair):
@@ -251,7 +255,7 @@
                 term = matmul(residue[slot], decoder_t[k])
                 dense = term if dense is None else dense + term
         picked.append(jnp.zeros(index.shape, BF) if dense is None else gather_slots(dense, index))
-    z_ref[...] = fold_slots(join_layers(picked, index, width), layers * slab_most).astype(BF)
+    z_ref[...] = fold_slots(join_layers(picked, index, width), layers * slab_most)
 
 
 def grads_kernel(
@@ -385,7 +389,7 @@
     act, mine_a, mine_b, sent_a, sent_b, index = by_pair(
         pairs, decode, parts, inverse, decoder[0], index
     )
-    steps = [1 << i for i in range(slabs.bit_length() - 1)]
+    steps = [1 << i | 1 for i in range(slabs.bit_length() - 1)]
     for i, step in enumerate(steps):
         theirs_a = across(sent_a, "lat", step)
         theirs_b = across(sent_b, "lat", steps[-1 - i])

time: 38.6 us -> 38 us (0.984)
  waiting for transfers between devices: 8.14 us -> 7.73 us
where the time goes in v6:
time: 38 us; the launch traced here: 37.7 us
  starting transfers between devices  10.4 us (27%)
  blocking collectives  9.93 us (26%)
  Pallas kernels  8.23 us (22%)
  waiting for transfers between devices  7.73 us (20%)
  local copies, waits for them, and re-layouts  0.72 us (2%)
  between operations  0.72 us (2%)
    all_to_all x1, blocking collectives, share(): return lax.all_to_all(copies, axis, 0, 0, tiled=True)  9.93 us
    pallas_call x6, Pallas kernels, call(): pl.pallas_call(kernel, out_shape=tuple(((pltpu.HBM if spec is HBM else pl...  8.23 us
    all_to_all x1, starting transfers between devices, share(): return lax.all_to_all(copies, axis, 0, 0, tiled=True)  7.29 us
    all_to_all x1, waiting for transfers between devices, share(): return lax.all_to_all(copies, axis, 0, 0, tiled=True)  6.09 us
    ppermute x4, starting transfers between devices, across(): return lax.ppermute(value, axis, pairs)  3.08 us
    ppermute x4, waiting for transfers between devices, across(): return lax.ppermute(value, axis, pairs)  1.64 us
  transfers between devices with their start and end apart: 5, of which 3 were waited for; matrix products, arithmetic and copies ran while one was open for 0% of the time, Pallas kernels for 6%

profile of v6, /device:TPU:0, one launch (start us, length us, event | category | flops | bytes accessed | tf_op | source)
XLA Modules:
  0.0 37.7 jit_solution(12210575288736120042)
XLA Ops:
  0.6 0.0 copy-start
  0.6 2.0 %shard_map.94 = (bf16[64,128]{1,0:T(8,128)(2,1)S(1)}, s16[128,128]{1,0:T(8,128)(2,1)S(1)}, s32[64,128]{1,0:T(8,128)S(1)}) custom-call(bf16[128,2,256]{2,1,0:T(2,128)(2,1)} %x_ref.1, bf16[2,256,1024]{2,1,0:T(8,128)(2,1)} %encoder_hbm.1, f32[2,1024]{1,0:T(2,128)} %bias_hbm.1, s32[128,128]{1,0:T(8,128)} %bitcast.11), custom_call_target="tpu_custom_call" | custom-call | tf_op jit(solution)/shard_map/pallas_call | solution.py:303
  2.6 0.0 copy-start.1
  2.7 0.0 copy-start.2
  2.7 0.7 %broadcast_in_dim.6 = bf16[8,64,128]{2,1,0:T(8,128)(2,1)} broadcast(bf16[64,128]{1,0:T(8,128)(2,1)S(1)} %get-tuple-element.23), dimensions={1,2} | broadcast | bytes 147456 | tf_op jit(solution)/shard_map/broadcast_in_dim | solution.py:317
  3.3 7.3 %all-to-all-start = ((bf16[8,64,128]{2,1,0:T(8,128)(2,1)}), bf16[8,64,128]{2,1,0:T(8,128)(2,1)S(1)}, u32[]{:S(2)}, u32[]{:S(2)}) async-start(bf16[8,64,128]{2,1,0:T(8,128)(2,1)} %broadcast_in_dim.6), calls=%async_computation | async-start | bytes 262144 | tf_op jit(solution)/shard_map/all_to_all | solution.py:318
  10.6 1.3 %shard_map.95.inverse_ref = s16[2,128,1024]{2,1,0:T(8,128)(2,1)S(1)} custom-call(s32[64,128]{1,0:T(8,128)S(1)} %get-tuple-element.24.kept_ref), custom_call_target="tpu_custom_call" | custom-call | flops 100000000 | bytes 1000000 | tf_op jit(solution)/shard_map/pallas_call | solution.py:303
  11.9 6.1 %all-to-all-done.parts_ref = bf16[8,64,128]{2,1,0:T(8,128)(2,1)S(1)} async-done(((bf16[8,64,128]{2,1,0:T(8,128)(2,1)}), bf16[8,64,128]{2,1,0:T(8,128)(2,1)S(1)}, u32[]{:S(2)}, u32[]{:S(2)}) %all-to-all-start) | async-done | bytes 131104 | tf_op jit(solution)/shard_map/all_to_all | solution.py:318
  18.0 0.0 copy-done
  18.0 0.6 %shard_map.96 = (bf16[2,128,1024]{2,1,0:T(8,128)(2,1)S(1)}, f32[128,256]{1,0:T(8,128)S(1)}, f32[128,256]{1,0:T(8,128)S(1)}, bf16[128,256]{1,0:T(8,128)(2,1)S(1)}...) custom-call(bf16[8,64,128]{2,1,0:T(8,128)(2,1)S(1)} %all-to-all-done.parts_ref, ...), custom_call_target="tpu_custom_call" | custom-call | tf_op jit(solution)/shard_map/pallas_call | solution.py:303
  18.5 0.0 copy-start.3
  18.6 0.1 collective-permute-start
  18.6 1.6 %collective-permute-start.1 = (bf16[128,256]{1,0:T(8,128)(2,1)S(1)}, bf16[128,256]{1,0:T(8,128)(2,1)S(1)}, u32[]{:S(2)}, u32[]{:S(2)}) collective-permute-start(bf16[128,256]{1,0:T(8,128)(2,1)S(1)} %get-tuple-element.29), channel_id=1, source_target_pairs={{0,3},{1,2},{2,1},{3,0},{4,7},{5,6},{6,5},{7,4},{8,11},{9,10},{10,... | collective-permute-start | bytes 196616 | tf_op jit(solution)/shard_map/ppermute | solution.py:330
  20.2 0.0 collective-permute-done
  20.3 0.9 %collective-permute-start.2 = (bf16[128,256]{1,0:T(8,128)(2,1)S(1)}, bf16[128,256]{1,0:T(8,128)(2,1)S(1)}, u32[]{:S(2)}, u32[]{:S(2)}) collective-permute-start(bf16[128,256]{1,0:T(8,128)(2,1)S(1)} %get-tuple-element.31), channel_id=1, source_target_pairs={{0,3},{1,2},{2,1},{3,0},{4,7},{5,6},{6,5},{7,4},{8,11},{9,10},{10,... | collective-permute-start | bytes 196616 | tf_op jit(solution)/shard_map/ppermute | solution.py:330
  21.2 1.3 %collective-permute-done.1 = bf16[128,256]{1,0:T(8,128)(2,1)S(1)} collective-permute-done((bf16[128,256]{1,0:T(8,128)(2,1)S(1)}, bf16[128,256]{1,0:T(8,128)(2,1)S(1)}, u32[]{:S(2)}, u32[]{:S(2)}) %collective-permute-start.1) | collective-permute-done | bytes 65568 | tf_op jit(solution)/shard_map/ppermute | solution.py:330
  22.5 0.5 %collective-permute-start.3 = (bf16[128,256]{1,0:T(8,128)(2,1)S(1)}, bf16[128,256]{1,0:T(8,128)(2,1)S(1)}, u32[]{:S(2)}, u32[]{:S(2)}) collective-permute-start(bf16[128,256]{1,0:T(8,128)(2,1)S(1)} %get-tuple-element.43), channel_id=1, source_target_pairs={{0,1},{1,0},{2,3},{3,2},{4,5},{5,4},{6,7},{7,6},{8,9},{9,8},{10,11... | collective-permute-start | bytes 196616 | tf_op jit(solution)/shard_map/ppermute | solution.py:330
  23.0 1.1 %shard_map.97 = (bf16[2,1024,128]{2,1,0:T(8,128)(2,1)S(1)}, bf16[2,256,128]{2,1,0:T(8,128)(2,1)S(1)}, bf16[2,128,256]{2,1,0:T(8,128)(2,1)S(1)}, bf16[3,256,1024]{2,1,0:T(8,128)(2,1)S(1)}) custom-call(bf16[2,128,1024]{2,1,0:T(8,128)(2,1)S(1)} %get-tuple-element.32.act_ref, bf16[128,2,256]{2,1,0:T(2,128)(2,1)S(1)} %copy-done.1, ...), custom_call_target="tpu_custom_call" | custom-call | flops 100000000 | bytes 10000000 | tf_op jit(solution)/shard_map/pallas_call | solution.py:303
  24.1 0.3 collective-permute-done.2.theirs_a
  24.5 0.0 collective-permute-done.3.theirs_b
  24.5 0.0 copy-done.3
  24.5 0.6 %shard_map.98 = (bf16[64,128]{1,0:T(8,128)(2,1)S(1)}, bf16[2,128,256]{2,1,0:T(8,128)(2,1)S(1)}) custom-call(f32[128,256]{1,0:T(8,128)S(1)} %get-tuple-element.46.mine_a, f32[128,256]{1,0:T(8,128)S(1)} %get-tuple-element.44.mine_b, bf16[128,256]{1,0:T(8,128)(2,1)S(1)} %collective-permute-done.2.theirs_a, ...), custom_call_target="tpu_custom_call" | custom-call | tf_op jit(solution)/shard_map/pallas_call | solution.py:303
  25.1 9.9 %all_to_all.10.parts_ref = bf16[8,64,128]{2,1,0:T(8,128)(2,1)S(1)} all-to-all(bf16[8,64,128]{2,1,0:T(8,128)(2,1)S(1)} %broadcast_in_dim.7), channel_id=1, replica_groups=mesh['layer'=8,'lat'=4] {'layer'}, dimensions={0} | all-to-all | bytes 262144 | tf_op jit(solution)/shard_map/all_to_all | solution.py:318
  35.0 2.7 %shard_map.99 = (f32[3,1024,256]{2,1,0:T(8,128)}, f32[2,256,1024]{2,1,0:T(8,128)}, f32[2,1024]{1,0:T(2,128)}) custom-call(bf16[8,64,128]{2,1,0:T(8,128)(2,1)S(1)} %all_to_all.10.parts_ref, s16[2,128,1024]{2,1,0:T(8,128)(2,1)S(1)} %shard_map.95.inverse_ref, bf16[2,256,128]{2,1,0:T(8,128)(2,1)S(1)} %get-tuple-element.37.x_t, ...), custom_call_target="tpu_custom_call" | custom-call | tf_op jit(solution)/shard_map/pallas_call | solution.py:303
  (5 shorter events, 0.1 us)
Async XLA Ops:
  0.6 17.3 %copy-start = (bf16[1,3,1024,256]{3,2,1,0:T(8,128)(2,1)S(1)}, bf16[1,3,1024,256]{3,2,1,0:T(8,128)(2,1)}, u32[]{:S(2)}) copy-start(bf16[1,3,1024,256]{3,2,1,0:T(8,128)(2,1)} %param.10) | copy-start | bytes 4718596
  2.6 20.4 %copy-start.1 = (bf16[128,2,256]{2,1,0:T(2,128)(2,1)S(1)}, bf16[128,2,256]{2,1,0:T(2,128)(2,1)}, u32[]{:S(2)}) copy-start(bf16[128,2,256]{2,1,0:T(2,128)(2,1)} %x_ref.1) | copy-start | bytes 393220
  2.7 20.3 %copy-start.2 = (bf16[1,128,2,256]{3,2,1,0:T(2,128)(2,1)S(1)}, bf16[1,128,2,256]{3,2,1,0:T(2,128)(2,1)}, u32[]{:S(2)}) copy-start(bf16[1,128,2,256]{3,2,1,0:T(2,128)(2,1)} %param.12) | copy-start | bytes 393220
  3.3 14.6 %all-to-all-start = ((bf16[8,64,128]{2,1,0:T(8,128)(2,1)}), bf16[8,64,128]{2,1,0:T(8,128)(2,1)S(1)}, u32[]{:S(2)}, u32[]{:S(2)}) async-start(bf16[8,64,128]{2,1,0:T(8,128)(2,1)} %broadcast_in_dim.6), calls=%async_computation | async-start | bytes 262144 | tf_op jit(solution)/shard_map/all_to_all | solution.py:318
  18.5 5.9 %copy-start.3 = (f32[1,2,256]{2,1,0:T(2,128)S(1)}, f32[1,2,256]{2,1,0:T(2,128)}, u32[]{:S(2)}) copy-start(f32[1,2,256]{2,1,0:T(2,128)} %param.11) | copy-start | bytes 6148
  18.6 1.7 %collective-permute-start = (bf16[128,256]{1,0:T(8,128)(2,1)S(1)}, bf16[128,256]{1,0:T(8,128)(2,1)S(1)}, u32[]{:S(2)}, u32[]{:S(2)}) collective-permute-start(bf16[128,256]{1,0:T(8,128)(2,1)S(1)} %get-tuple-element.27), channel_id=1, source_target_pairs={{0,1},{1,0},{2,3},{3,2},{4,5},{5,4},{6,7},{7,6},{8,9},{9,8},{10,11... | collective-permute-start | bytes 196616 | tf_op jit(solution)/shard_map/ppermute | solution.py:330
  18.6 3.9 %collective-permute-start.1 = (bf16[128,256]{1,0:T(8,128)(2,1)S(1)}, bf16[128,256]{1,0:T(8,128)(2,1)S(1)}, u32[]{:S(2)}, u32[]{:S(2)}) collective-permute-start(bf16[128,256]{1,0:T(8,128)(2,1)S(1)} %get-tuple-element.29), channel_id=1, source_target_pairs={{0,3},{1,2},{2,1},{3,0},{4,7},{5,6},{6,5},{7,4},{8,11},{9,10},{10,... | collective-permute-start | bytes 196616 | tf_op jit(solution)/shard_map/ppermute | solution.py:330
  20.3 4.2 %collective-permute-start.2 = (bf16[128,256]{1,0:T(8,128)(2,1)S(1)}, bf16[128,256]{1,0:T(8,128)(2,1)S(1)}, u32[]{:S(2)}, u32[]{:S(2)}) collective-permute-start(bf16[128,256]{1,0:T(8,128)(2,1)S(1)} %get-tuple-element.31), channel_id=1, source_target_pairs={{0,3},{1,2},{2,1},{3,0},{4,7},{5,6},{6,5},{7,4},{8,11},{9,10},{10,... | collective-permute-start | bytes 196616 | tf_op jit(solution)/shard_map/ppermute | solution.py:330
  22.5 1.9 %collective-permute-start.3 = (bf16[128,256]{1,0:T(8,128)(2,1)S(1)}, bf16[128,256]{1,0:T(8,128)(2,1)S(1)}, u32[]{:S(2)}, u32[]{:S(2)}) collective-permute-start(bf16[128,256]{1,0:T(8,128)(2,1)S(1)} %get-tuple-element.43), channel_id=1, source_target_pairs={{0,1},{1,0},{2,3},{3,2},{4,5},{5,4},{6,7},{7,6},{8,9},{9,8},{10,11... | collective-permute-start | bytes 196616 | tf_op jit(solution)/shard_map/ppermute | solution.py:330

commit v7 on v6

--- a/solution.py
+++ b/solution.py
@@ -238,7 +238,7 @@
 
 def residue_kernel(
     plan, pair, mine_a, mine_b, theirs_a, theirs_b, dec_bias_ref, targets_ref, index_ref, decoder_t,
-    z_ref, residue
+    act_t, z_ref, residue, head_ref
 ):
     layers, width, top_count, slab_most = plan
     for slot, (mine, theirs) in enumerate([(mine_a, theirs_a), (mine_b, theirs_b)]):
@@ -256,10 +256,11 @@
                 dense = term if dense is None else dense + term
         picked.append(jnp.zeros(index.shape, BF) if dense is None else gather_slots(dense, index))
     z_ref[...] = fold_slots(join_layers(picked, index, width), layers * slab_most)
+    head_ref[...] = matmul(act_t[places[0][0]], residue[places[0][1]])
 
 
 def grads_kernel(
-    plan, pair, parts_ref, inverse_ref, x_t, act_t, residue_ref,
+    plan, pair, parts_ref, inverse_ref, x_t, act_t, residue_ref, head_ref,
     decoder_hbm, encoder_hbm, bias_hbm, values, decoder_grad, encoder_grad, bias, sems
 ):
     layers, width, top_count, slab_most = plan
@@ -271,11 +272,7 @@
         copies.append(pltpu.make_async_copy(source, target, sems.at[len(copies)]))
         copies[-1].start()
 
-    for k, (source, slot) in enumerate(block_places(layers, pair)):
-        for i in range(PARTS):
-            rows = pl.ds(i * part, part)
-            decoder_grad[k, rows] = matmul(act_t[source, rows], residue_ref[slot])
-            send(decoder_grad.at[k, rows], decoder_hbm.at[k, rows])
+    send(head_ref, decoder_hbm.at[0])
     values[...] = sum_parts(parts_ref, layers * slab_most)
     ones = jnp.ones((8, tokens), BF)
     for layer in range(layers):
@@ -285,6 +282,11 @@
             encoder_grad[at] = matmul(x_t[layer], dense)
             send(encoder_grad.at[at], encoder_hbm.at[at])
             bias[layer : layer + 1, i * part : (i + 1) * part] = matmul(ones, dense)[:1]
+    for k, (source, slot) in list(enumerate(block_places(layers, pair)))[1:]:
+        for i in range(PARTS):
+            rows = pl.ds(i * part, part)
+            decoder_grad[k - 1, rows] = matmul(act_t[source, rows], residue_ref[slot])
+            send(decoder_grad.at[k - 1, rows], decoder_hbm.at[k, rows])
     send(bias, bias_hbm)
     for copy in copies:
         copy.wait()
@@ -390,8 +392,8 @@
         pairs, decode, parts, inverse, decoder[0], index
     )
     steps = [1 << i | 1 for i in range(slabs.bit_length() - 1)]
-    for i, step in enumerate(steps):
-        theirs_a = across(sent_a, "lat", step)
+    for i in range(len(steps)):
+        theirs_a = across(sent_a, "lat", 1 << i)
         theirs_b = across(sent_b, "lat", steps[-1 - i])
         if i + 1 < len(steps):
             mine_a = mine_a + theirs_a.astype(F32)
@@ -415,21 +417,25 @@
     def residues(pair, *args):
         return call(
             functools.partial(residue_kernel, plan, pair),
-            [VMEM] * 8,
-            [((packed, LANES), BF, VMEM), ((2, tokens, feat), BF, VMEM)],
+            [VMEM] * 9,
+            [
+                ((packed, LANES), BF, VMEM),
+                ((2, tokens, feat), BF, VMEM),
+                ((width, feat), F32, VMEM),
+            ],
             [],
             *args,
         )
 
-    z, residue = by_pair(
-        pairs, residues, mine_a, mine_b, theirs_a, theirs_b, dec_bias[0], targets_by_slot, index, decoder_t
+    z, residue, head = by_pair(
+        pairs, residues, mine_a, mine_b, theirs_a, theirs_b, dec_bias[0], targets_by_slot, index, decoder_t, act_t
     )
     parts = share(z, "layer")
 
     def grads(pair, *args):
         return call(
             functools.partial(grads_kernel, plan, pair),
-            [VMEM] * 5,
+            [VMEM] * 6,
             [
                 ((layers + 1, width, feat), F32, HBM),
                 (encoder.shape, F32, HBM),
@@ -437,16 +443,16 @@
             ],
             [
                 pltpu.VMEM((tokens, LANES), BF),
-                pltpu.VMEM((layers + 1, width, feat), F32),
+                pltpu.VMEM((layers, width, feat), F32),
                 pltpu.VMEM(encoder.shape, F32),
                 pltpu.VMEM(enc_bias.shape, F32),
-                dma((PARTS * (2 * layers + 1) + 1,)),
+                dma((PARTS * 2 * layers + 2,)),
             ],
             *args,
         )
 
     decoder_grad, encoder_grad, bias_grad = by_pair(
-        pairs, grads, parts, inverse, x_t, act_t, residue
+        pairs, grads, parts, inverse, x_t, act_t, residue, head
     )
     return decoder_grad[None], encoder_grad, bias_grad
 

time: 38 us -> 37.7 us (level)
  starting transfers between devices: 10.4 us -> 10.8 us
    ppermute x4, starting transfers between devices: 3.08 us -> 3.47 us  [across(): return lax.ppermute(value, axis, pairs)]
where the time goes in v7:
time: 37.7 us; the launch traced here: 37.4 us
  starting transfers between devices  10.8 us (29%)
  blocking collectives  9.74 us (26%)
  Pallas kernels  7.99 us (21%)
  waiting for transfers between devices  7.46 us (20%)
  local copies, waits for them, and re-layouts  0.72 us (2%)
  between operations  0.72 us (2%)
    all_to_all x1, blocking collectives, share(): return lax.all_to_all(copies, axis, 0, 0, tiled=True)  9.74 us
    pallas_call x6, Pallas kernels, call(): pl.pallas_call(kernel, out_shape=tuple(((pltpu.HBM if spec is HBM else pl...  7.99 us
    all_to_all x1, starting transfers between devices, share(): return lax.all_to_all(copies, axis, 0, 0, tiled=True)  7.29 us
    all_to_all x1, waiting for transfers between devices, share(): return lax.all_to_all(copies, axis, 0, 0, tiled=True)  6.09 us
    ppermute x4, starting transfers between devices, across(): return lax.ppermute(value, axis, pairs)  3.47 us
    ppermute x4, waiting for transfers between devices, across(): return lax.ppermute(value, axis, pairs)  1.37 us
  transfers between devices with their start and end apart: 5, of which 3 were waited for; matrix products, arithmetic and copies ran while one was open for 0% of the time, Pallas kernels for 6%

profile of v7, /device:TPU:0, one launch (start us, length us, event | category | flops | bytes accessed | tf_op | source)
XLA Modules:
  0.0 37.4 jit_solution(2216739048122823349)
XLA Ops:
  0.6 0.0 copy-start
  0.6 2.0 %shard_map.94 = (bf16[64,128]{1,0:T(8,128)(2,1)S(1)}, s16[128,128]{1,0:T(8,128)(2,1)S(1)}, s32[64,128]{1,0:T(8,128)S(1)}) custom-call(bf16[128,2,256]{2,1,0:T(2,128)(2,1)} %x_ref.1, bf16[2,256,1024]{2,1,0:T(8,128)(2,1)} %encoder_hbm.1, f32[2,1024]{1,0:T(2,128)} %bias_hbm.1, s32[128,128]{1,0:T(8,128)} %bitcast.11), custom_call_target="tpu_custom_call" | custom-call | tf_op jit(solution)/shard_map/pallas_call | solution.py:305
  2.6 0.0 copy-start.1
  2.7 0.0 copy-start.2
  2.7 0.7 %broadcast_in_dim.6 = bf16[8,64,128]{2,1,0:T(8,128)(2,1)} broadcast(bf16[64,128]{1,0:T(8,128)(2,1)S(1)} %get-tuple-element.24), dimensions={1,2} | broadcast | bytes 147456 | tf_op jit(solution)/shard_map/broadcast_in_dim | solution.py:319
  3.3 7.3 %all-to-all-start = ((bf16[8,64,128]{2,1,0:T(8,128)(2,1)}), bf16[8,64,128]{2,1,0:T(8,128)(2,1)S(1)}, u32[]{:S(2)}, u32[]{:S(2)}) async-start(bf16[8,64,128]{2,1,0:T(8,128)(2,1)} %broadcast_in_dim.6), calls=%async_computation | async-start | bytes 262144 | tf_op jit(solution)/shard_map/all_to_all | solution.py:320
  10.6 1.3 %shard_map.95.inverse_ref = s16[2,128,1024]{2,1,0:T(8,128)(2,1)S(1)} custom-call(s32[64,128]{1,0:T(8,128)S(1)} %get-tuple-element.25.kept_ref), custom_call_target="tpu_custom_call" | custom-call | flops 100000000 | bytes 1000000 | tf_op jit(solution)/shard_map/pallas_call | solution.py:305
  11.9 6.1 %all-to-all-done.parts_ref = bf16[8,64,128]{2,1,0:T(8,128)(2,1)S(1)} async-done(((bf16[8,64,128]{2,1,0:T(8,128)(2,1)}), bf16[8,64,128]{2,1,0:T(8,128)(2,1)S(1)}, u32[]{:S(2)}, u32[]{:S(2)}) %all-to-all-start) | async-done | bytes 131104 | tf_op jit(solution)/shard_map/all_to_all | solution.py:320
  18.0 0.0 copy-done
  18.0 0.6 %shard_map.96 = (bf16[2,128,1024]{2,1,0:T(8,128)(2,1)S(1)}, f32[128,256]{1,0:T(8,128)S(1)}, f32[128,256]{1,0:T(8,128)S(1)}, bf16[128,256]{1,0:T(8,128)(2,1)S(1)}...) custom-call(bf16[8,64,128]{2,1,0:T(8,128)(2,1)S(1)} %all-to-all-done.parts_ref, ...), custom_call_target="tpu_custom_call" | custom-call | tf_op jit(solution)/shard_map/pallas_call | solution.py:305
  18.5 0.0 copy-start.3
  18.6 0.1 collective-permute-start
  18.6 1.6 %collective-permute-start.1 = (bf16[128,256]{1,0:T(8,128)(2,1)S(1)}, bf16[128,256]{1,0:T(8,128)(2,1)S(1)}, u32[]{:S(2)}, u32[]{:S(2)}) collective-permute-start(bf16[128,256]{1,0:T(8,128)(2,1)S(1)} %get-tuple-element.30), channel_id=1, source_target_pairs={{0,3},{1,2},{2,1},{3,0},{4,7},{5,6},{6,5},{7,4},{8,11},{9,10},{10,... | collective-permute-start | bytes 196616 | tf_op jit(solution)/shard_map/ppermute | solution.py:332
  20.2 0.0 collective-permute-done
  20.3 1.2 %collective-permute-start.2 = (bf16[128,256]{1,0:T(8,128)(2,1)S(1)}, bf16[128,256]{1,0:T(8,128)(2,1)S(1)}, u32[]{:S(2)}, u32[]{:S(2)}) collective-permute-start(bf16[128,256]{1,0:T(8,128)(2,1)S(1)} %get-tuple-element.32), channel_id=1, source_target_pairs={{0,2},{1,3},{2,0},{3,1},{4,6},{5,7},{6,4},{7,5},{8,10},{9,11},{10,... | collective-permute-start | bytes 196616 | tf_op jit(solution)/shard_map/ppermute | solution.py:332
  21.4 1.1 %collective-permute-done.1 = bf16[128,256]{1,0:T(8,128)(2,1)S(1)} collective-permute-done((bf16[128,256]{1,0:T(8,128)(2,1)S(1)}, bf16[128,256]{1,0:T(8,128)(2,1)S(1)}, u32[]{:S(2)}, u32[]{:S(2)}) %collective-permute-start.1) | collective-permute-done | bytes 65568 | tf_op jit(solution)/shard_map/ppermute | solution.py:332
  22.5 0.6 %collective-permute-start.3 = (bf16[128,256]{1,0:T(8,128)(2,1)S(1)}, bf16[128,256]{1,0:T(8,128)(2,1)S(1)}, u32[]{:S(2)}, u32[]{:S(2)}) collective-permute-start(bf16[128,256]{1,0:T(8,128)(2,1)S(1)} %get-tuple-element.45), channel_id=1, source_target_pairs={{0,1},{1,0},{2,3},{3,2},{4,5},{5,4},{6,7},{7,6},{8,9},{9,8},{10,11... | collective-permute-start | bytes 196616 | tf_op jit(solution)/shard_map/ppermute | solution.py:332
  23.2 1.1 %shard_map.97 = (bf16[2,1024,128]{2,1,0:T(8,128)(2,1)S(1)}, bf16[2,256,128]{2,1,0:T(8,128)(2,1)S(1)}, bf16[2,128,256]{2,1,0:T(8,128)(2,1)S(1)}, bf16[3,256,1024]{2,1,0:T(8,128)(2,1)S(1)}) custom-call(bf16[2,128,1024]{2,1,0:T(8,128)(2,1)S(1)} %get-tuple-element.33.act_ref, bf16[128,2,256]{2,1,0:T(2,128)(2,1)S(1)} %copy-done.1, ...), custom_call_target="tpu_custom_call" | custom-call | flops 100000000 | bytes 10000000 | tf_op jit(solution)/shard_map/pallas_call | solution.py:305
  24.3 0.3 collective-permute-done.2.theirs_a
  24.6 0.0 collective-permute-done.3.theirs_b
  24.6 0.0 copy-done.3
  24.6 0.6 %shard_map.98 = (bf16[64,128]{1,0:T(8,128)(2,1)S(1)}, bf16[2,128,256]{2,1,0:T(8,128)(2,1)S(1)}, f32[1024,256]{1,0:T(8,128)S(1)}) custom-call(f32[128,256]{1,0:T(8,128)S(1)} %get-tuple-element.48.mine_a, f32[128,256]{1,0:T(8,128)S(1)} %get-tuple-element.46.mine_b, bf16[128,256]{1,0:T(8,128)(2,1)S(1)} %collective-permute-done.2.theirs_a, ...), custom_call_target="tpu_custom_call" | custom-call | tf_op jit(solution)/shard_map/pallas_call | solution.py:305
  25.2 9.7 %all_to_all.10.parts_ref = bf16[8,64,128]{2,1,0:T(8,128)(2,1)S(1)} all-to-all(bf16[8,64,128]{2,1,0:T(8,128)(2,1)S(1)} %broadcast_in_dim.7), channel_id=1, replica_groups=mesh['layer'=8,'lat'=4] {'layer'}, dimensions={0} | all-to-all | bytes 262144 | tf_op jit(solution)/shard_map/all_to_all | solution.py:320
  34.9 2.5 %shard_map.99 = (f32[3,1024,256]{2,1,0:T(8,128)}, f32[2,256,1024]{2,1,0:T(8,128)}, f32[2,1024]{1,0:T(2,128)}) custom-call(bf16[8,64,128]{2,1,0:T(8,128)(2,1)S(1)} %all_to_all.10.parts_ref, s16[2,128,1024]{2,1,0:T(8,128)(2,1)S(1)} %shard_map.95.inverse_ref, bf16[2,256,128]{2,1,0:T(8,128)(2,1)S(1)} %get-tuple-element.39.x_t, ...), custom_call_target="tpu_custom_call" | custom-call | tf_op jit(solution)/shard_map/pallas_call | solution.py:305
  (5 shorter events, 0.1 us)
Async XLA Ops:
  0.6 17.3 %copy-start = (bf16[1,3,1024,256]{3,2,1,0:T(8,128)(2,1)S(1)}, bf16[1,3,1024,256]{3,2,1,0:T(8,128)(2,1)}, u32[]{:S(2)}) copy-start(bf16[1,3,1024,256]{3,2,1,0:T(8,128)(2,1)} %param.10) | copy-start | bytes 4718596
  2.6 20.5 %copy-start.1 = (bf16[128,2,256]{2,1,0:T(2,128)(2,1)S(1)}, bf16[128,2,256]{2,1,0:T(2,128)(2,1)}, u32[]{:S(2)}) copy-start(bf16[128,2,256]{2,1,0:T(2,128)(2,1)} %x_ref.1) | copy-start | bytes 393220
  2.7 20.5 %copy-start.2 = (bf16[1,128,2,256]{3,2,1,0:T(2,128)(2,1)S(1)}, bf16[1,128,2,256]{3,2,1,0:T(2,128)(2,1)}, u32[]{:S(2)}) copy-start(bf16[1,128,2,256]{3,2,1,0:T(2,128)(2,1)} %param.12) | copy-start | bytes 393220
  3.3 14.6 %all-to-all-start = ((bf16[8,64,128]{2,1,0:T(8,128)(2,1)}), bf16[8,64,128]{2,1,0:T(8,128)(2,1)S(1)}, u32[]{:S(2)}, u32[]{:S(2)}) async-start(bf16[8,64,128]{2,1,0:T(8,128)(2,1)} %broadcast_in_dim.6), calls=%async_computation | async-start | bytes 262144 | tf_op jit(solution)/shard_map/all_to_all | solution.py:320
  18.5 6.1 %copy-start.3 = (f32[1,2,256]{2,1,0:T(2,128)S(1)}, f32[1,2,256]{2,1,0:T(2,128)}, u32[]{:S(2)}) copy-start(f32[1,2,256]{2,1,0:T(2,128)} %param.11) | copy-start | bytes 6148
  18.6 1.7 %collective-permute-start = (bf16[128,256]{1,0:T(8,128)(2,1)S(1)}, bf16[128,256]{1,0:T(8,128)(2,1)S(1)}, u32[]{:S(2)}, u32[]{:S(2)}) collective-permute-start(bf16[128,256]{1,0:T(8,128)(2,1)S(1)} %get-tuple-element.28), channel_id=1, source_target_pairs={{0,1},{1,0},{2,3},{3,2},{4,5},{5,4},{6,7},{7,6},{8,9},{9,8},{10,11... | collective-permute-start | bytes 196616 | tf_op jit(solution)/shard_map/ppermute | solution.py:332
  18.6 3.9 %collective-permute-start.1 = (bf16[128,256]{1,0:T(8,128)(2,1)S(1)}, bf16[128,256]{1,0:T(8,128)(2,1)S(1)}, u32[]{:S(2)}, u32[]{:S(2)}) collective-permute-start(bf16[128,256]{1,0:T(8,128)(2,1)S(1)} %get-tuple-element.30), channel_id=1, source_target_pairs={{0,3},{1,2},{2,1},{3,0},{4,7},{5,6},{6,5},{7,4},{8,11},{9,10},{10,... | collective-permute-start | bytes 196616 | tf_op jit(solution)/shard_map/ppermute | solution.py:332
  20.3 4.3 %collective-permute-start.2 = (bf16[128,256]{1,0:T(8,128)(2,1)S(1)}, bf16[128,256]{1,0:T(8,128)(2,1)S(1)}, u32[]{:S(2)}, u32[]{:S(2)}) collective-permute-start(bf16[128,256]{1,0:T(8,128)(2,1)S(1)} %get-tuple-element.32), channel_id=1, source_target_pairs={{0,2},{1,3},{2,0},{3,1},{4,6},{5,7},{6,4},{7,5},{8,10},{9,11},{10,... | collective-permute-start | bytes 196616 | tf_op jit(solution)/shard_map/ppermute | solution.py:332
  22.5 2.1 %collective-permute-start.3 = (bf16[128,256]{1,0:T(8,128)(2,1)S(1)}, bf16[128,256]{1,0:T(8,128)(2,1)S(1)}, u32[]{:S(2)}, u32[]{:S(2)}) collective-permute-start(bf16[128,256]{1,0:T(8,128)(2,1)S(1)} %get-tuple-element.45), channel_id=1, source_target_pairs={{0,1},{1,0},{2,3},{3,2},{4,5},{5,4},{6,7},{7,6},{8,9},{9,8},{10,11... | collective-permute-start | bytes 196616 | tf_op jit(solution)/shard_map/ppermute | solution.py:332

commit v8 on v7

--- a/solution.py
+++ b/solution.py
@@ -393,7 +393,7 @@
     )
     steps = [1 << i | 1 for i in range(slabs.bit_length() - 1)]
     for i in range(len(steps)):
-        theirs_a = across(sent_a, "lat", 1 << i)
+        theirs_a = across(sent_a, "lat", steps[i])
         theirs_b = across(sent_b, "lat", steps[-1 - i])
         if i + 1 < len(steps):
             mine_a = mine_a + theirs_a.astype(F32)

time: 37.7 us -> 37.8 us (level)
  starting transfers between devices: 10.8 us -> 10.4 us
    ppermute x4, starting transfers between devices: 3.47 us -> 3.08 us  [across(): return lax.ppermute(value, axis, pairs)]
where the time goes in v8:
time: 37.8 us; the launch traced here: 37.5 us
  starting transfers between devices  10.4 us (28%)
  blocking collectives  9.94 us (26%)
  Pallas kernels  7.99 us (21%)
  waiting for transfers between devices  7.73 us (20%)
  local copies, waits for them, and re-layouts  0.72 us (2%)
  between operations  0.72 us (2%)
    all_to_all x1, blocking collectives, share(): return lax.all_to_all(copies, axis, 0, 0, tiled=True)  9.94 us
    pallas_call x6, Pallas kernels, call(): pl.pallas_call(kernel, out_shape=tuple(((pltpu.HBM if spec is HBM else pl...  7.99 us
    all_to_all x1, starting transfers between devices, share(): return lax.all_to_all(copies, axis, 0, 0, tiled=True)  7.29 us
    all_to_all x1, waiting for transfers between devices, share(): return lax.all_to_all(copies, axis, 0, 0, tiled=True)  6.09 us
    ppermute x4, starting transfers between devices, across(): return lax.ppermute(value, axis, pairs)  3.08 us
    ppermute x4, waiting for transfers between devices, across(): return lax.ppermute(value, axis, pairs)  1.64 us
  transfers between devices with their start and end apart: 5, of which 3 were waited for; matrix products, arithmetic and copies ran while one was open for 0% of the time, Pallas kernels for 6%

profile of v8, /device:TPU:0, one launch (start us, length us, event | category | flops | bytes accessed | tf_op | source)
XLA Modules:
  0.0 37.5 jit_solution(7333586492003648780)
XLA Ops:
  0.6 0.0 copy-start
  0.6 2.0 %shard_map.94 = (bf16[64,128]{1,0:T(8,128)(2,1)S(1)}, s16[128,128]{1,0:T(8,128)(2,1)S(1)}, s32[64,128]{1,0:T(8,128)S(1)}) custom-call(bf16[128,2,256]{2,1,0:T(2,128)(2,1)} %x_ref.1, bf16[2,256,1024]{2,1,0:T(8,128)(2,1)} %encoder_hbm.1, f32[2,1024]{1,0:T(2,128)} %bias_hbm.1, s32[128,128]{1,0:T(8,128)} %bitcast.11), custom_call_target="tpu_custom_call" | custom-call | tf_op jit(solution)/shard_map/pallas_call | solution.py:305
  2.6 0.0 copy-start.1
  2.7 0.0 copy-start.2
  2.7 0.7 %broadcast_in_dim.6 = bf16[8,64,128]{2,1,0:T(8,128)(2,1)} broadcast(bf16[64,128]{1,0:T(8,128)(2,1)S(1)} %get-tuple-element.24), dimensions={1,2} | broadcast | bytes 147456 | tf_op jit(solution)/shard_map/broadcast_in_dim | solution.py:319
  3.3 7.3 %all-to-all-start = ((bf16[8,64,128]{2,1,0:T(8,128)(2,1)}), bf16[8,64,128]{2,1,0:T(8,128)(2,1)S(1)}, u32[]{:S(2)}, u32[]{:S(2)}) async-start(bf16[8,64,128]{2,1,0:T(8,128)(2,1)} %broadcast_in_dim.6), calls=%async_computation | async-start | bytes 262144 | tf_op jit(solution)/shard_map/all_to_all | solution.py:320
  10.6 1.3 %shard_map.95.inverse_ref = s16[2,128,1024]{2,1,0:T(8,128)(2,1)S(1)} custom-call(s32[64,128]{1,0:T(8,128)S(1)} %get-tuple-element.25.kept_ref), custom_call_target="tpu_custom_call" | custom-call | flops 100000000 | bytes 1000000 | tf_op jit(solution)/shard_map/pallas_call | solution.py:305
  11.9 6.1 %all-to-all-done.parts_ref = bf16[8,64,128]{2,1,0:T(8,128)(2,1)S(1)} async-done(((bf16[8,64,128]{2,1,0:T(8,128)(2,1)}), bf16[8,64,128]{2,1,0:T(8,128)(2,1)S(1)}, u32[]{:S(2)}, u32[]{:S(2)}) %all-to-all-start) | async-done | bytes 131104 | tf_op jit(solution)/shard_map/all_to_all | solution.py:320
  18.0 0.0 copy-done
  18.0 0.6 %shard_map.96 = (bf16[2,128,1024]{2,1,0:T(8,128)(2,1)S(1)}, f32[128,256]{1,0:T(8,128)S(1)}, f32[128,256]{1,0:T(8,128)S(1)}, bf16[128,256]{1,0:T(8,128)(2,1)S(1)}...) custom-call(bf16[8,64,128]{2,1,0:T(8,128)(2,1)S(1)} %all-to-all-done.parts_ref, ...), custom_call_target="tpu_custom_call" | custom-call | tf_op jit(solution)/shard_map/pallas_call | solution.py:305
  18.5 0.0 copy-start.3
  18.6 0.1 collective-permute-start
  18.6 1.6 %collective-permute-start.1 = (bf16[128,256]{1,0:T(8,128)(2,1)S(1)}, bf16[128,256]{1,0:T(8,128)(2,1)S(1)}, u32[]{:S(2)}, u32[]{:S(2)}) collective-permute-start(bf16[128,256]{1,0:T(8,128)(2,1)S(1)} %get-tuple-element.30), channel_id=1, source_target_pairs={{0,3},{1,2},{2,1},{3,0},{4,7},{5,6},{6,5},{7,4},{8,11},{9,10},{10,... | collective-permute-start | bytes 196616 | tf_op jit(solution)/shard_map/ppermute | solution.py:332
  20.2 0.0 collective-permute-done
  20.3 0.9 %collective-permute-start.2 = (bf16[128,256]{1,0:T(8,128)(2,1)S(1)}, bf16[128,256]{1,0:T(8,128)(2,1)S(1)}, u32[]{:S(2)}, u32[]{:S(2)}) collective-permute-start(bf16[128,256]{1,0:T(8,128)(2,1)S(1)} %get-tuple-element.32), channel_id=1, source_target_pairs={{0,3},{1,2},{2,1},{3,0},{4,7},{5,6},{6,5},{7,4},{8,11},{9,10},{10,... | collective-permute-start | bytes 196616 | tf_op jit(solution)/shard_map/ppermute | solution.py:332
  21.2 1.3 %collective-permute-done.1 = bf16[128,256]{1,0:T(8,128)(2,1)S(1)} collective-permute-done((bf16[128,256]{1,0:T(8,128)(2,1)S(1)}, bf16[128,256]{1,0:T(8,128)(2,1)S(1)}, u32[]{:S(2)}, u32[]{:S(2)}) %collective-permute-start.1) | collective-permute-done | bytes 65568 | tf_op jit(solution)/shard_map/ppermute | solution.py:332
  22.5 0.5 %collective-permute-start.3 = (bf16[128,256]{1,0:T(8,128)(2,1)S(1)}, bf16[128,256]{1,0:T(8,128)(2,1)S(1)}, u32[]{:S(2)}, u32[]{:S(2)}) collective-permute-start(bf16[128,256]{1,0:T(8,128)(2,1)S(1)} %get-tuple-element.45), channel_id=1, source_target_pairs={{0,1},{1,0},{2,3},{3,2},{4,5},{5,4},{6,7},{7,6},{8,9},{9,8},{10,11... | collective-permute-start | bytes 196616 | tf_op jit(solution)/shard_map/ppermute | solution.py:332
  23.0 0.0 copy-done.1
  23.0 1.1 %shard_map.97 = (bf16[2,1024,128]{2,1,0:T(8,128)(2,1)S(1)}, bf16[2,256,128]{2,1,0:T(8,128)(2,1)S(1)}, bf16[2,128,256]{2,1,0:T(8,128)(2,1)S(1)}, bf16[3,256,1024]{2,1,0:T(8,128)(2,1)S(1)}) custom-call(bf16[2,128,1024]{2,1,0:T(8,128)(2,1)S(1)} %get-tuple-element.33.act_ref, bf16[128,2,256]{2,1,0:T(2,128)(2,1)S(1)} %copy-done.1, ...), custom_call_target="tpu_custom_call" | custom-call | flops 100000000 | bytes 10000000 | tf_op jit(solution)/shard_map/pallas_call | solution.py:305
  24.1 0.3 collective-permute-done.2.theirs_a
  24.5 0.0 collective-permute-done.3.theirs_b
  24.5 0.6 %shard_map.98 = (bf16[64,128]{1,0:T(8,128)(2,1)S(1)}, bf16[2,128,256]{2,1,0:T(8,128)(2,1)S(1)}, f32[1024,256]{1,0:T(8,128)S(1)}) custom-call(f32[128,256]{1,0:T(8,128)S(1)} %get-tuple-element.48.mine_a, f32[128,256]{1,0:T(8,128)S(1)} %get-tuple-element.46.mine_b, bf16[128,256]{1,0:T(8,128)(2,1)S(1)} %collective-permute-done.2.theirs_a, ...), custom_call_target="tpu_custom_call" | custom-call | tf_op jit(solution)/shard_map/pallas_call | solution.py:305
  25.1 9.9 %all_to_all.10.parts_ref = bf16[8,64,128]{2,1,0:T(8,128)(2,1)S(1)} all-to-all(bf16[8,64,128]{2,1,0:T(8,128)(2,1)S(1)} %broadcast_in_dim.7), channel_id=1, replica_groups=mesh['layer'=8,'lat'=4] {'layer'}, dimensions={0} | all-to-all | bytes 262144 | tf_op jit(solution)/shard_map/all_to_all | solution.py:320
  35.0 2.5 %shard_map.99 = (f32[3,1024,256]{2,1,0:T(8,128)}, f32[2,256,1024]{2,1,0:T(8,128)}, f32[2,1024]{1,0:T(2,128)}) custom-call(bf16[8,64,128]{2,1,0:T(8,128)(2,1)S(1)} %all_to_all.10.parts_ref, s16[2,128,1024]{2,1,0:T(8,128)(2,1)S(1)} %shard_map.95.inverse_ref, bf16[2,256,128]{2,1,0:T(8,128)(2,1)S(1)} %get-tuple-element.39.x_t, ...), custom_call_target="tpu_custom_call" | custom-call | tf_op jit(solution)/shard_map/pallas_call | solution.py:305
  (5 shorter events, 0.1 us)
Async XLA Ops:
  0.6 17.3 %copy-start = (bf16[1,3,1024,256]{3,2,1,0:T(8,128)(2,1)S(1)}, bf16[1,3,1024,256]{3,2,1,0:T(8,128)(2,1)}, u32[]{:S(2)}) copy-start(bf16[1,3,1024,256]{3,2,1,0:T(8,128)(2,1)} %param.10) | copy-start | bytes 4718596
  2.6 20.4 %copy-start.1 = (bf16[128,2,256]{2,1,0:T(2,128)(2,1)S(1)}, bf16[128,2,256]{2,1,0:T(2,128)(2,1)}, u32[]{:S(2)}) copy-start(bf16[128,2,256]{2,1,0:T(2,128)(2,1)} %x_ref.1) | copy-start | bytes 393220
  2.7 20.3 %copy-start.2 = (bf16[1,128,2,256]{3,2,1,0:T(2,128)(2,1)S(1)}, bf16[1,128,2,256]{3,2,1,0:T(2,128)(2,1)}, u32[]{:S(2)}) copy-start(bf16[1,128,2,256]{3,2,1,0:T(2,128)(2,1)} %param.12) | copy-start | bytes 393220
  3.3 14.6 %all-to-all-start = ((bf16[8,64,128]{2,1,0:T(8,128)(2,1)}), bf16[8,64,128]{2,1,0:T(8,128)(2,1)S(1)}, u32[]{:S(2)}, u32[]{:S(2)}) async-start(bf16[8,64,128]{2,1,0:T(8,128)(2,1)} %broadcast_in_dim.6), calls=%async_computation | async-start | bytes 262144 | tf_op jit(solution)/shard_map/all_to_all | solution.py:320
  18.5 5.9 %copy-start.3 = (f32[1,2,256]{2,1,0:T(2,128)S(1)}, f32[1,2,256]{2,1,0:T(2,128)}, u32[]{:S(2)}) copy-start(f32[1,2,256]{2,1,0:T(2,128)} %param.11) | copy-start | bytes 6148
  18.6 1.7 %collective-permute-start = (bf16[128,256]{1,0:T(8,128)(2,1)S(1)}, bf16[128,256]{1,0:T(8,128)(2,1)S(1)}, u32[]{:S(2)}, u32[]{:S(2)}) collective-permute-start(bf16[128,256]{1,0:T(8,128)(2,1)S(1)} %get-tuple-element.28), channel_id=1, source_target_pairs={{0,1},{1,0},{2,3},{3,2},{4,5},{5,4},{6,7},{7,6},{8,9},{9,8},{10,11... | collective-permute-start | bytes 196616 | tf_op jit(solution)/shard_map/ppermute | solution.py:332
  18.6 3.9 %collective-permute-start.1 = (bf16[128,256]{1,0:T(8,128)(2,1)S(1)}, bf16[128,256]{1,0:T(8,128)(2,1)S(1)}, u32[]{:S(2)}, u32[]{:S(2)}) collective-permute-start(bf16[128,256]{1,0:T(8,128)(2,1)S(1)} %get-tuple-element.30), channel_id=1, source_target_pairs={{0,3},{1,2},{2,1},{3,0},{4,7},{5,6},{6,5},{7,4},{8,11},{9,10},{10,... | collective-permute-start | bytes 196616 | tf_op jit(solution)/shard_map/ppermute | solution.py:332
  20.3 4.2 %collective-permute-start.2 = (bf16[128,256]{1,0:T(8,128)(2,1)S(1)}, bf16[128,256]{1,0:T(8,128)(2,1)S(1)}, u32[]{:S(2)}, u32[]{:S(2)}) collective-permute-start(bf16[128,256]{1,0:T(8,128)(2,1)S(1)} %get-tuple-element.32), channel_id=1, source_target_pairs={{0,3},{1,2},{2,1},{3,0},{4,7},{5,6},{6,5},{7,4},{8,11},{9,10},{10,... | collective-permute-start | bytes 196616 | tf_op jit(solution)/shard_map/ppermute | solution.py:332
  22.5 1.9 %collective-permute-start.3 = (bf16[128,256]{1,0:T(8,128)(2,1)S(1)}, bf16[128,256]{1,0:T(8,128)(2,1)S(1)}, u32[]{:S(2)}, u32[]{:S(2)}) collective-permute-start(bf16[128,256]{1,0:T(8,128)(2,1)S(1)} %get-tuple-element.45), channel_id=1, source_target_pairs={{0,1},{1,0},{2,3},{3,2},{4,5},{5,4},{6,7},{7,6},{8,9},{9,8},{10,11... | collective-permute-start | bytes 196616 | tf_op jit(solution)/shard_map/ppermute | solution.py:332

commit v9 on v7

--- a/solution.py
+++ b/solution.py
@@ -391,28 +391,37 @@
     act, mine_a, mine_b, sent_a, sent_b, index = by_pair(
         pairs, decode, parts, inverse, decoder[0], index
     )
+    def turn(act):
+        return call(
+            turn_kernel,
+            [VMEM] * 4,
+            [
+                ((layers, width, tokens), BF, VMEM),
+                ((layers, depth, tokens), BF, VMEM),
+                ((2, tokens, feat), BF, VMEM),
+                ((layers + 1, feat, width), BF, VMEM),
+            ],
+            [],
+            act, inputs, targets[0], decoder[0],
+            cost=pl.CostEstimate(flops=10**8, bytes_accessed=10**7, transcendentals=0),
+        )
+
     steps = [1 << i | 1 for i in range(slabs.bit_length() - 1)]
+    turned = None
     for i in range(len(steps)):
         theirs_a = across(sent_a, "lat", 1 << i)
         theirs_b = across(sent_b, "lat", steps[-1 - i])
         if i + 1 < len(steps):
             mine_a = mine_a + theirs_a.astype(F32)
+            sent_a = mine_a.astype(BF)
+            if i + 2 == len(steps):
+                sent_a, act = lax.optimization_barrier((sent_a, act))
+                turned = turn(act)
             mine_b = mine_b + theirs_b.astype(F32)
-            sent_a, sent_b = mine_a.astype(BF), mine_b.astype(BF)
-            sent_a, act = lax.optimization_barrier((sent_a, act))
-    act_t, x_t, targets_by_slot, decoder_t = call(
-        turn_kernel,
-        [VMEM] * 4,
-        [
-            ((layers, width, tokens), BF, VMEM),
-            ((layers, depth, tokens), BF, VMEM),
-            ((2, tokens, feat), BF, VMEM),
-            ((layers + 1, feat, width), BF, VMEM),
-        ],
-        [],
-        act, inputs, targets[0], decoder[0],
-        cost=pl.CostEstimate(flops=10**8, bytes_accessed=10**7, transcendentals=0),
-    )
+            sent_b = mine_b.astype(BF)
+            if turned is not None:
+                sent_b, turned = lax.optimization_barrier((sent_b, turned))
+    act_t, x_t, targets_by_slot, decoder_t = turn(act) if turned is None else turned
 
     def residues(pair, *args):
         return call(

time: 37.7 us -> 37.7 us (level)
  transfers between devices with their start and end apart: 5 -> 5, of which waited for: 3 -> 2; matrix products, arithmetic and copies ran while one was open for 0% -> 0% of each run, Pallas kernels for 6% -> 6%
where the time goes in v9:
time: 37.7 us; the launch traced here: 37.4 us
  starting transfers between devices  10.7 us (28%)
  blocking collectives  9.74 us (26%)
  Pallas kernels  7.99 us (21%)
  waiting for transfers between devices  7.53 us (20%)
  between operations  0.73 us (2%)
  local copies, waits for them, and re-layouts  0.72 us (2%)
    all_to_all x1, blocking collectives, share(): return lax.all_to_all(copies, axis, 0, 0, tiled=True)  9.74 us
    pallas_call x6, Pallas kernels, call(): pl.pallas_call(kernel, out_shape=tuple(((pltpu.HBM if spec is HBM else pl...  7.99 us
    all_to_all x1, starting transfers between devices, share(): return lax.all_to_all(copies, axis, 0, 0, tiled=True)  7.29 us
    all_to_all x1, waiting for transfers between devices, share(): return lax.all_to_all(copies, axis, 0, 0, tiled=True)  6.09 us
    ppermute x4, starting transfers between devices, across(): return lax.ppermute(value, axis, pairs)  3.38 us
    ppermute x4, waiting for transfers between devices, across(): return lax.ppermute(value, axis, pairs)  1.44 us
  transfers between devices with their start and end apart: 5, of which 2 were waited for; matrix products, arithmetic and copies ran while one was open for 0% of the time, Pallas kernels for 6%

profile of v9, /device:TPU:0, one launch (start us, length us, event | category | flops | bytes accessed | tf_op | source)
XLA Modules:
  0.0 37.4 jit_solution(14374523329992656332)
XLA Ops:
  0.6 0.0 copy-start
  0.6 2.0 %shard_map.94 = (bf16[64,128]{1,0:T(8,128)(2,1)S(1)}, s16[128,128]{1,0:T(8,128)(2,1)S(1)}, s32[64,128]{1,0:T(8,128)S(1)}) custom-call(bf16[128,2,256]{2,1,0:T(2,128)(2,1)} %x_ref.1, bf16[2,256,1024]{2,1,0:T(8,128)(2,1)} %encoder_hbm.1, f32[2,1024]{1,0:T(2,128)} %bias_hbm.1, s32[128,128]{1,0:T(8,128)} %bitcast.11), custom_call_target="tpu_custom_call" | custom-call | tf_op jit(solution)/shard_map/pallas_call | solution.py:305
  2.6 0.0 copy-start.1
  2.7 0.0 copy-start.2
  2.7 0.7 %broadcast_in_dim.6 = bf16[8,64,128]{2,1,0:T(8,128)(2,1)} broadcast(bf16[64,128]{1,0:T(8,128)(2,1)S(1)} %get-tuple-element.29), dimensions={1,2} | broadcast | bytes 147456 | tf_op jit(solution)/shard_map/broadcast_in_dim | solution.py:319
  3.3 7.3 %all-to-all-start = ((bf16[8,64,128]{2,1,0:T(8,128)(2,1)}), bf16[8,64,128]{2,1,0:T(8,128)(2,1)S(1)}, u32[]{:S(2)}, u32[]{:S(2)}) async-start(bf16[8,64,128]{2,1,0:T(8,128)(2,1)} %broadcast_in_dim.6), calls=%async_computation | async-start | bytes 262144 | tf_op jit(solution)/shard_map/all_to_all | solution.py:320
  10.6 1.3 %shard_map.95.inverse_ref = s16[2,128,1024]{2,1,0:T(8,128)(2,1)S(1)} custom-call(s32[64,128]{1,0:T(8,128)S(1)} %get-tuple-element.30.kept_ref), custom_call_target="tpu_custom_call" | custom-call | flops 100000000 | bytes 1000000 | tf_op jit(solution)/shard_map/pallas_call | solution.py:305
  11.9 6.1 %all-to-all-done.parts_ref = bf16[8,64,128]{2,1,0:T(8,128)(2,1)S(1)} async-done(((bf16[8,64,128]{2,1,0:T(8,128)(2,1)}), bf16[8,64,128]{2,1,0:T(8,128)(2,1)S(1)}, u32[]{:S(2)}, u32[]{:S(2)}) %all-to-all-start) | async-done | bytes 131104 | tf_op jit(solution)/shard_map/all_to_all | solution.py:320
  18.0 0.0 copy-done
  18.0 0.6 %shard_map.96 = (bf16[2,128,1024]{2,1,0:T(8,128)(2,1)S(1)}, f32[128,256]{1,0:T(8,128)S(1)}, f32[128,256]{1,0:T(8,128)S(1)}, bf16[128,256]{1,0:T(8,128)(2,1)S(1)}...) custom-call(bf16[8,64,128]{2,1,0:T(8,128)(2,1)S(1)} %all-to-all-done.parts_ref, ...), custom_call_target="tpu_custom_call" | custom-call | tf_op jit(solution)/shard_map/pallas_call | solution.py:305
  18.5 0.0 copy-start.3
  18.6 0.1 collective-permute-start
  18.6 1.6 %collective-permute-start.1 = (bf16[128,256]{1,0:T(8,128)(2,1)S(1)}, bf16[128,256]{1,0:T(8,128)(2,1)S(1)}, u32[]{:S(2)}, u32[]{:S(2)}) collective-permute-start(bf16[128,256]{1,0:T(8,128)(2,1)S(1)} %get-tuple-element.35), channel_id=1, source_target_pairs={{0,3},{1,2},{2,1},{3,0},{4,7},{5,6},{6,5},{7,4},{8,11},{9,10},{10,... | collective-permute-start | bytes 196616 | tf_op jit(solution)/shard_map/ppermute | solution.py:332
  20.2 0.0 collective-permute-done
  20.3 1.2 %collective-permute-start.2 = (bf16[128,256]{1,0:T(8,128)(2,1)S(1)}, bf16[128,256]{1,0:T(8,128)(2,1)S(1)}, u32[]{:S(2)}, u32[]{:S(2)}) collective-permute-start(bf16[128,256]{1,0:T(8,128)(2,1)S(1)} %get-tuple-element.37), channel_id=1, source_target_pairs={{0,2},{1,3},{2,0},{3,1},{4,6},{5,7},{6,4},{7,5},{8,10},{9,11},{10,... | collective-permute-start | bytes 196616 | tf_op jit(solution)/shard_map/ppermute | solution.py:332
  21.4 0.0 copy-done.1
  21.4 1.1 %shard_map.97 = (bf16[2,1024,128]{2,1,0:T(8,128)(2,1)S(1)}, bf16[2,256,128]{2,1,0:T(8,128)(2,1)S(1)}, bf16[2,128,256]{2,1,0:T(8,128)(2,1)S(1)}, bf16[3,256,1024]{2,1,0:T(8,128)(2,1)S(1)}) custom-call(bf16[2,128,1024]{2,1,0:T(8,128)(2,1)S(1)} %get-tuple-element.38.act_ref, bf16[128,2,256]{2,1,0:T(2,128)(2,1)S(1)} %copy-done.1, ...), custom_call_target="tpu_custom_call" | custom-call | flops 100000000 | bytes 10000000 | tf_op jit(solution)/shard_map/pallas_call | solution.py:305
  22.6 0.0 collective-permute-done.1
  22.6 0.5 %collective-permute-start.3 = (bf16[128,256]{1,0:T(8,128)(2,1)S(1)}, bf16[128,256]{1,0:T(8,128)(2,1)S(1)}, u32[]{:S(2)}, u32[]{:S(2)}) collective-permute-start(bf16[128,256]{1,0:T(8,128)(2,1)S(1)} %get-tuple-element.43), channel_id=1, source_target_pairs={{0,1},{1,0},{2,3},{3,2},{4,5},{5,4},{6,7},{7,6},{8,9},{9,8},{10,11... | collective-permute-start | bytes 196616 | tf_op jit(solution)/shard_map/ppermute | solution.py:332
  23.1 1.4 %collective-permute-done.2.theirs_a = bf16[128,256]{1,0:T(8,128)(2,1)S(1)} collective-permute-done((bf16[128,256]{1,0:T(8,128)(2,1)S(1)}, bf16[128,256]{1,0:T(8,128)(2,1)S(1)}, u32[]{:S(2)}, u32[]{:S(2)}) %collective-permute-start.2) | collective-permute-done | bytes 65568 | tf_op jit(solution)/shard_map/ppermute | solution.py:332
  24.6 0.0 collective-permute-done.3.theirs_b
  24.6 0.6 %shard_map.98 = (bf16[64,128]{1,0:T(8,128)(2,1)S(1)}, bf16[2,128,256]{2,1,0:T(8,128)(2,1)S(1)}, f32[1024,256]{1,0:T(8,128)S(1)}) custom-call(f32[128,256]{1,0:T(8,128)S(1)} %get-tuple-element.58.mine_a, f32[128,256]{1,0:T(8,128)S(1)} %get-tuple-element.56.mine_b, bf16[128,256]{1,0:T(8,128)(2,1)S(1)} %collective-permute-done.2.theirs_a, ...), custom_call_target="tpu_custom_call" | custom-call | tf_op jit(solution)/shard_map/pallas_call | solution.py:305
  25.2 9.7 %all_to_all.10.parts_ref = bf16[8,64,128]{2,1,0:T(8,128)(2,1)S(1)} all-to-all(bf16[8,64,128]{2,1,0:T(8,128)(2,1)S(1)} %broadcast_in_dim.7), channel_id=1, replica_groups=mesh['layer'=8,'lat'=4] {'layer'}, dimensions={0} | all-to-all | bytes 262144 | tf_op jit(solution)/shard_map/all_to_all | solution.py:320
  34.9 2.5 %shard_map.99 = (f32[3,1024,256]{2,1,0:T(8,128)}, f32[2,256,1024]{2,1,0:T(8,128)}, f32[2,1024]{1,0:T(2,128)}) custom-call(bf16[8,64,128]{2,1,0:T(8,128)(2,1)S(1)} %all_to_all.10.parts_ref, s16[2,128,1024]{2,1,0:T(8,128)(2,1)S(1)} %shard_map.95.inverse_ref, bf16[2,256,128]{2,1,0:T(8,128)(2,1)S(1)} %get-tuple-element.49.x_t, ...), custom_call_target="tpu_custom_call" | custom-call | tf_op jit(solution)/shard_map/pallas_call | solution.py:305
  (5 shorter events, 0.1 us)
Async XLA Ops:
  0.6 17.3 %copy-start = (bf16[1,3,1024,256]{3,2,1,0:T(8,128)(2,1)S(1)}, bf16[1,3,1024,256]{3,2,1,0:T(8,128)(2,1)}, u32[]{:S(2)}) copy-start(bf16[1,3,1024,256]{3,2,1,0:T(8,128)(2,1)} %param.10) | copy-start | bytes 4718596
  2.6 18.8 %copy-start.1 = (bf16[128,2,256]{2,1,0:T(2,128)(2,1)S(1)}, bf16[128,2,256]{2,1,0:T(2,128)(2,1)}, u32[]{:S(2)}) copy-start(bf16[128,2,256]{2,1,0:T(2,128)(2,1)} %x_ref.1) | copy-start | bytes 393220
  2.7 18.8 %copy-start.2 = (bf16[1,128,2,256]{3,2,1,0:T(2,128)(2,1)S(1)}, bf16[1,128,2,256]{3,2,1,0:T(2,128)(2,1)}, u32[]{:S(2)}) copy-start(bf16[1,128,2,256]{3,2,1,0:T(2,128)(2,1)} %param.12) | copy-start | bytes 393220
  3.3 14.6 %all-to-all-start = ((bf16[8,64,128]{2,1,0:T(8,128)(2,1)}), bf16[8,64,128]{2,1,0:T(8,128)(2,1)S(1)}, u32[]{:S(2)}, u32[]{:S(2)}) async-start(bf16[8,64,128]{2,1,0:T(8,128)(2,1)} %broadcast_in_dim.6), calls=%async_computation | async-start | bytes 262144 | tf_op jit(solution)/shard_map/all_to_all | solution.py:320
  18.5 6.1 %copy-start.3 = (f32[1,2,256]{2,1,0:T(2,128)S(1)}, f32[1,2,256]{2,1,0:T(2,128)}, u32[]{:S(2)}) copy-start(f32[1,2,256]{2,1,0:T(2,128)} %param.11) | copy-start | bytes 6148
  18.6 1.7 %collective-permute-start = (bf16[128,256]{1,0:T(8,128)(2,1)S(1)}, bf16[128,256]{1,0:T(8,128)(2,1)S(1)}, u32[]{:S(2)}, u32[]{:S(2)}) collective-permute-start(bf16[128,256]{1,0:T(8,128)(2,1)S(1)} %get-tuple-element.33), channel_id=1, source_target_pairs={{0,1},{1,0},{2,3},{3,2},{4,5},{5,4},{6,7},{7,6},{8,9},{9,8},{10,11... | collective-permute-start | bytes 196616 | tf_op jit(solution)/shard_map/ppermute | solution.py:332
  18.6 4.0 %collective-permute-start.1 = (bf16[128,256]{1,0:T(8,128)(2,1)S(1)}, bf16[128,256]{1,0:T(8,128)(2,1)S(1)}, u32[]{:S(2)}, u32[]{:S(2)}) collective-permute-start(bf16[128,256]{1,0:T(8,128)(2,1)S(1)} %get-tuple-element.35), channel_id=1, source_target_pairs={{0,3},{1,2},{2,1},{3,0},{4,7},{5,6},{6,5},{7,4},{8,11},{9,10},{10,... | collective-permute-start | bytes 196616 | tf_op jit(solution)/shard_map/ppermute | solution.py:332
  20.3 4.3 %collective-permute-start.2 = (bf16[128,256]{1,0:T(8,128)(2,1)S(1)}, bf16[128,256]{1,0:T(8,128)(2,1)S(1)}, u32[]{:S(2)}, u32[]{:S(2)}) collective-permute-start(bf16[128,256]{1,0:T(8,128)(2,1)S(1)} %get-tuple-element.37), channel_id=1, source_target_pairs={{0,2},{1,3},{2,0},{3,1},{4,6},{5,7},{6,4},{7,5},{8,10},{9,11},{10,... | collective-permute-start | bytes 196616 | tf_op jit(solution)/shard_map/ppermute | solution.py:332
  22.6 2.0 %collective-permute-start.3 = (bf16[128,256]{1,0:T(8,128)(2,1)S(1)}, bf16[128,256]{1,0:T(8,128)(2,1)S(1)}, u32[]{:S(2)}, u32[]{:S(2)}) collective-permute-start(bf16[128,256]{1,0:T(8,128)(2,1)S(1)} %get-tuple-element.43), channel_id=1, source_target_pairs={{0,1},{1,0},{2,3},{3,2},{4,5},{5,4},{6,7},{7,6},{8,9},{9,8},{10,11... | collective-permute-start | bytes 196616 | tf_op jit(solution)/shard_map/ppermute | solution.py:332

commit v10 on v9

--- a/solution.py
+++ b/solution.py
@@ -214,12 +214,17 @@
     layers, width, top_count, slab_most = plan
     index_out[...] = index_ref[...]
     total = sum_parts(parts_ref, layers * slab_most)
-    for layer in range(layers):
-        act_ref[layer] = place_slots(total, inverse_ref[layer])
     sums = [None, None]
-    for k, (source, slot) in enumerate(block_places(layers, pair)):
-        term = matmul(act_ref[source], decoder_ref[k])
-        sums[slot] = term if sums[slot] is None else sums[slot] + term
+    places = block_places(layers, pair)
+    for layer in range(layers):
+        for first in range(0, width, 2 * LANES):
+            columns = slice(first, first + 2 * LANES)
+            piece = place_slots(total, inverse_ref[layer, :, columns])
+            act_ref[layer, :, columns] = piece
+            for k, (source, slot) in enumerate(places):
+                if source == layer:
+                    term = matmul(piece, decoder_ref[k, columns, :])
+                    sums[slot] = term if sums[slot] is None else sums[slot] + term
     first_ref[...] = sums[0]
     second_ref[...] = sums[1]
     first_rounded[...] = sums[0].astype(BF)
@@ -249,12 +254,13 @@
     index = index_ref[...]
     picked = []
     for layer in range(layers):
-        dense = None
-        for k, (source, slot) in enumerate(places):
-            if source == layer:
-                term = matmul(residue[slot], decoder_t[k])
-                dense = term if dense is None else dense + term
-        picked.append(jnp.zeros(index.shape, BF) if dense is None else gather_slots(dense, index))
+        own = [(k, slot) for k, (source, slot) in enumerate(places) if source == layer]
+        if own:
+            left = jnp.concatenate([residue[slot] for k, slot in own], axis=1)
+            right = jnp.concatenate([decoder_t[k] for k, slot in own], axis=0)
+            picked.append(gather_slots(matmul(left, right), index))
+        else:
+            picked.append(jnp.zeros(index.shape, BF))
     z_ref[...] = fold_slots(join_layers(picked, index, width), layers * slab_most)
     head_ref[...] = matmul(act_t[places[0][0]], residue[places[0][1]])
 

time: 37.7 us -> 37.7 us (level)
  no operation moved by 1% of the time
where the time goes in v10:
time: 37.7 us; the launch traced here: 37.4 us
  starting transfers between devices  10.7 us (28%)
  blocking collectives  9.74 us (26%)
  Pallas kernels  7.96 us (21%)
  waiting for transfers between devices  7.53 us (20%)
  between operations  0.74 us (2%)
  local copies, waits for them, and re-layouts  0.72 us (2%)
    all_to_all x1, blocking collectives, share(): return lax.all_to_all(copies, axis, 0, 0, tiled=True)  9.74 us
    pallas_call x6, Pallas kernels, call(): pl.pallas_call(kernel, out_shape=tuple(((pltpu.HBM if spec is HBM else pl...  7.96 us
    all_to_all x1, starting transfers between devices, share(): return lax.all_to_all(copies, axis, 0, 0, tiled=True)  7.29 us
    all_to_all x1, waiting for transfers between devices, share(): return lax.all_to_all(copies, axis, 0, 0, tiled=True)  6.09 us
    ppermute x4, starting transfers between devices, across(): return lax.ppermute(value, axis, pairs)  3.38 us
    ppermute x4, waiting for transfers between devices, across(): return lax.ppermute(value, axis, pairs)  1.45 us
  transfers between devices with their start and end apart: 5, of which 2 were waited for; matrix products, arithmetic and copies ran while one was open for 0% of the time, Pallas kernels for 6%

profile of v10, /device:TPU:0, one launch (start us, length us, event | category | flops | bytes accessed | tf_op | source)
XLA Modules:
  0.0 37.4 jit_solution(17093961833767428899)
XLA Ops:
  0.6 0.0 copy-start
  0.6 2.0 %shard_map.94 = (bf16[64,128]{1,0:T(8,128)(2,1)S(1)}, s16[128,128]{1,0:T(8,128)(2,1)S(1)}, s32[64,128]{1,0:T(8,128)S(1)}) custom-call(bf16[128,2,256]{2,1,0:T(2,128)(2,1)} %x_ref.1, bf16[2,256,1024]{2,1,0:T(8,128)(2,1)} %encoder_hbm.1, f32[2,1024]{1,0:T(2,128)} %bias_hbm.1, s32[128,128]{1,0:T(8,128)} %bitcast.11), custom_call_target="tpu_custom_call" | custom-call | tf_op jit(solution)/shard_map/pallas_call | solution.py:311
  2.6 0.0 copy-start.1
  2.7 0.0 copy-start.2
  2.7 0.7 %broadcast_in_dim.6 = bf16[8,64,128]{2,1,0:T(8,128)(2,1)} broadcast(bf16[64,128]{1,0:T(8,128)(2,1)S(1)} %get-tuple-element.29), dimensions={1,2} | broadcast | bytes 147456 | tf_op jit(solution)/shard_map/broadcast_in_dim | solution.py:325
  3.3 7.3 %all-to-all-start = ((bf16[8,64,128]{2,1,0:T(8,128)(2,1)}), bf16[8,64,128]{2,1,0:T(8,128)(2,1)S(1)}, u32[]{:S(2)}, u32[]{:S(2)}) async-start(bf16[8,64,128]{2,1,0:T(8,128)(2,1)} %broadcast_in_dim.6), calls=%async_computation | async-start | bytes 262144 | tf_op jit(solution)/shard_map/all_to_all | solution.py:326
  10.6 1.3 %shard_map.95.inverse_ref = s16[2,128,1024]{2,1,0:T(8,128)(2,1)S(1)} custom-call(s32[64,128]{1,0:T(8,128)S(1)} %get-tuple-element.30.kept_ref), custom_call_target="tpu_custom_call" | custom-call | flops 100000000 | bytes 1000000 | tf_op jit(solution)/shard_map/pallas_call | solution.py:311
  11.9 6.1 %all-to-all-done.parts_ref = bf16[8,64,128]{2,1,0:T(8,128)(2,1)S(1)} async-done(((bf16[8,64,128]{2,1,0:T(8,128)(2,1)}), bf16[8,64,128]{2,1,0:T(8,128)(2,1)S(1)}, u32[]{:S(2)}, u32[]{:S(2)}) %all-to-all-start) | async-done | bytes 131104 | tf_op jit(solution)/shard_map/all_to_all | solution.py:326
  18.0 0.0 copy-done
  18.0 0.6 %shard_map.96 = (bf16[2,128,1024]{2,1,0:T(8,128)(2,1)S(1)}, f32[128,256]{1,0:T(8,128)S(1)}, f32[128,256]{1,0:T(8,128)S(1)}, bf16[128,256]{1,0:T(8,128)(2,1)S(1)}...) custom-call(bf16[8,64,128]{2,1,0:T(8,128)(2,1)S(1)} %all-to-all-done.parts_ref, ...), custom_call_target="tpu_custom_call" | custom-call | tf_op jit(solution)/shard_map/pallas_call | solution.py:311
  18.5 0.0 copy-start.3
  18.5 0.1 collective-permute-start
  18.6 1.6 %collective-permute-start.1 = (bf16[128,256]{1,0:T(8,128)(2,1)S(1)}, bf16[128,256]{1,0:T(8,128)(2,1)S(1)}, u32[]{:S(2)}, u32[]{:S(2)}) collective-permute-start(bf16[128,256]{1,0:T(8,128)(2,1)S(1)} %get-tuple-element.35), channel_id=1, source_target_pairs={{0,3},{1,2},{2,1},{3,0},{4,7},{5,6},{6,5},{7,4},{8,11},{9,10},{10,... | collective-permute-start | bytes 196616 | tf_op jit(solution)/shard_map/ppermute | solution.py:338
  20.2 0.0 collective-permute-done
  20.3 1.2 %collective-permute-start.2 = (bf16[128,256]{1,0:T(8,128)(2,1)S(1)}, bf16[128,256]{1,0:T(8,128)(2,1)S(1)}, u32[]{:S(2)}, u32[]{:S(2)}) collective-permute-start(bf16[128,256]{1,0:T(8,128)(2,1)S(1)} %get-tuple-element.37), channel_id=1, source_target_pairs={{0,2},{1,3},{2,0},{3,1},{4,6},{5,7},{6,4},{7,5},{8,10},{9,11},{10,... | collective-permute-start | bytes 196616 | tf_op jit(solution)/shard_map/ppermute | solution.py:338
  21.4 0.0 copy-done.1
  21.4 1.1 %shard_map.97 = (bf16[2,1024,128]{2,1,0:T(8,128)(2,1)S(1)}, bf16[2,256,128]{2,1,0:T(8,128)(2,1)S(1)}, bf16[2,128,256]{2,1,0:T(8,128)(2,1)S(1)}, bf16[3,256,1024]{2,1,0:T(8,128)(2,1)S(1)}) custom-call(bf16[2,128,1024]{2,1,0:T(8,128)(2,1)S(1)} %get-tuple-element.38.act_ref, bf16[128,2,256]{2,1,0:T(2,128)(2,1)S(1)} %copy-done.1, ...), custom_call_target="tpu_custom_call" | custom-call | flops 100000000 | bytes 10000000 | tf_op jit(solution)/shard_map/pallas_call | solution.py:311
  22.6 0.0 collective-permute-done.1
  22.6 0.5 %collective-permute-start.3 = (bf16[128,256]{1,0:T(8,128)(2,1)S(1)}, bf16[128,256]{1,0:T(8,128)(2,1)S(1)}, u32[]{:S(2)}, u32[]{:S(2)}) collective-permute-start(bf16[128,256]{1,0:T(8,128)(2,1)S(1)} %get-tuple-element.43), channel_id=1, source_target_pairs={{0,1},{1,0},{2,3},{3,2},{4,5},{5,4},{6,7},{7,6},{8,9},{9,8},{10,11... | collective-permute-start | bytes 196616 | tf_op jit(solution)/shard_map/ppermute | solution.py:338
  23.1 1.4 %collective-permute-done.2.theirs_a = bf16[128,256]{1,0:T(8,128)(2,1)S(1)} collective-permute-done((bf16[128,256]{1,0:T(8,128)(2,1)S(1)}, bf16[128,256]{1,0:T(8,128)(2,1)S(1)}, u32[]{:S(2)}, u32[]{:S(2)}) %collective-permute-start.2) | collective-permute-done | bytes 65568 | tf_op jit(solution)/shard_map/ppermute | solution.py:338
  24.6 0.0 collective-permute-done.3.theirs_b
  24.6 0.5 %shard_map.98 = (bf16[64,128]{1,0:T(8,128)(2,1)S(1)}, bf16[2,128,256]{2,1,0:T(8,128)(2,1)S(1)}, f32[1024,256]{1,0:T(8,128)S(1)}) custom-call(f32[128,256]{1,0:T(8,128)S(1)} %get-tuple-element.58.mine_a, f32[128,256]{1,0:T(8,128)S(1)} %get-tuple-element.56.mine_b, bf16[128,256]{1,0:T(8,128)(2,1)S(1)} %collective-permute-done.2.theirs_a, ...), custom_call_target="tpu_custom_call" | custom-call | tf_op jit(solution)/shard_map/pallas_call | solution.py:311
  25.2 9.7 %all_to_all.10.parts_ref = bf16[8,64,128]{2,1,0:T(8,128)(2,1)S(1)} all-to-all(bf16[8,64,128]{2,1,0:T(8,128)(2,1)S(1)} %broadcast_in_dim.7), channel_id=1, replica_groups=mesh['layer'=8,'lat'=4] {'layer'}, dimensions={0} | all-to-all | bytes 262144 | tf_op jit(solution)/shard_map/all_to_all | solution.py:326
  34.9 2.5 %shard_map.99 = (f32[3,1024,256]{2,1,0:T(8,128)}, f32[2,256,1024]{2,1,0:T(8,128)}, f32[2,1024]{1,0:T(2,128)}) custom-call(bf16[8,64,128]{2,1,0:T(8,128)(2,1)S(1)} %all_to_all.10.parts_ref, s16[2,128,1024]{2,1,0:T(8,128)(2,1)S(1)} %shard_map.95.inverse_ref, bf16[2,256,128]{2,1,0:T(8,128)(2,1)S(1)} %get-tuple-element.49.x_t, ...), custom_call_target="tpu_custom_call" | custom-call | tf_op jit(solution)/shard_map/pallas_call | solution.py:311
  (5 shorter events, 0.1 us)
Async XLA Ops:
  0.6 17.3 %copy-start = (bf16[1,3,1024,256]{3,2,1,0:T(8,128)(2,1)S(1)}, bf16[1,3,1024,256]{3,2,1,0:T(8,128)(2,1)}, u32[]{:S(2)}) copy-start(bf16[1,3,1024,256]{3,2,1,0:T(8,128)(2,1)} %param.10) | copy-start | bytes 4718596
  2.6 18.8 %copy-start.1 = (bf16[128,2,256]{2,1,0:T(2,128)(2,1)S(1)}, bf16[128,2,256]{2,1,0:T(2,128)(2,1)}, u32[]{:S(2)}) copy-start(bf16[128,2,256]{2,1,0:T(2,128)(2,1)} %x_ref.1) | copy-start | bytes 393220
  2.7 18.8 %copy-start.2 = (bf16[1,128,2,256]{3,2,1,0:T(2,128)(2,1)S(1)}, bf16[1,128,2,256]{3,2,1,0:T(2,128)(2,1)}, u32[]{:S(2)}) copy-start(bf16[1,128,2,256]{3,2,1,0:T(2,128)(2,1)} %param.12) | copy-start | bytes 393220
  3.3 14.6 %all-to-all-start = ((bf16[8,64,128]{2,1,0:T(8,128)(2,1)}), bf16[8,64,128]{2,1,0:T(8,128)(2,1)S(1)}, u32[]{:S(2)}, u32[]{:S(2)}) async-start(bf16[8,64,128]{2,1,0:T(8,128)(2,1)} %broadcast_in_dim.6), calls=%async_computation | async-start | bytes 262144 | tf_op jit(solution)/shard_map/all_to_all | solution.py:326
  18.5 6.1 %copy-start.3 = (f32[1,2,256]{2,1,0:T(2,128)S(1)}, f32[1,2,256]{2,1,0:T(2,128)}, u32[]{:S(2)}) copy-start(f32[1,2,256]{2,1,0:T(2,128)} %param.11) | copy-start | bytes 6148
  18.5 1.7 %collective-permute-start = (bf16[128,256]{1,0:T(8,128)(2,1)S(1)}, bf16[128,256]{1,0:T(8,128)(2,1)S(1)}, u32[]{:S(2)}, u32[]{:S(2)}) collective-permute-start(bf16[128,256]{1,0:T(8,128)(2,1)S(1)} %get-tuple-element.33), channel_id=1, source_target_pairs={{0,1},{1,0},{2,3},{3,2},{4,5},{5,4},{6,7},{7,6},{8,9},{9,8},{10,11... | collective-permute-start | bytes 196616 | tf_op jit(solution)/shard_map/ppermute | solution.py:338
  18.6 4.0 %collective-permute-start.1 = (bf16[128,256]{1,0:T(8,128)(2,1)S(1)}, bf16[128,256]{1,0:T(8,128)(2,1)S(1)}, u32[]{:S(2)}, u32[]{:S(2)}) collective-permute-start(bf16[128,256]{1,0:T(8,128)(2,1)S(1)} %get-tuple-element.35), channel_id=1, source_target_pairs={{0,3},{1,2},{2,1},{3,0},{4,7},{5,6},{6,5},{7,4},{8,11},{9,10},{10,... | collective-permute-start | bytes 196616 | tf_op jit(solution)/shard_map/ppermute | solution.py:338
  20.3 4.3 %collective-permute-start.2 = (bf16[128,256]{1,0:T(8,128)(2,1)S(1)}, bf16[128,256]{1,0:T(8,128)(2,1)S(1)}, u32[]{:S(2)}, u32[]{:S(2)}) collective-permute-start(bf16[128,256]{1,0:T(8,128)(2,1)S(1)} %get-tuple-element.37), channel_id=1, source_target_pairs={{0,2},{1,3},{2,0},{3,1},{4,6},{5,7},{6,4},{7,5},{8,10},{9,11},{10,... | collective-permute-start | bytes 196616 | tf_op jit(solution)/shard_map/ppermute | solution.py:338
  22.6 2.0 %collective-permute-start.3 = (bf16[128,256]{1,0:T(8,128)(2,1)S(1)}, bf16[128,256]{1,0:T(8,128)(2,1)S(1)}, u32[]{:S(2)}, u32[]{:S(2)}) collective-permute-start(bf16[128,256]{1,0:T(8,128)(2,1)S(1)} %get-tuple-element.43), channel_id=1, source_target_pairs={{0,1},{1,0},{2,3},{3,2},{4,5},{5,4},{6,7},{7,6},{8,9},{9,8},{10,11... | collective-permute-start | bytes 196616 | tf_op jit(solution)/shard_map/ppermute | solution.py:338

commit v11 on v9

--- a/solution.py
+++ b/solution.py
@@ -249,12 +249,13 @@
     index = index_ref[...]
     picked = []
     for layer in range(layers):
-        dense = None
-        for k, (source, slot) in enumerate(places):
-            if source == layer:
-                term = matmul(residue[slot], decoder_t[k])
-                dense = term if dense is None else dense + term
-        picked.append(jnp.zeros(index.shape, BF) if dense is None else gather_slots(dense, index))
+        own = [(k, slot) for k, (source, slot) in enumerate(places) if source == layer]
+        if own:
+            left = jnp.concatenate([residue[slot] for k, slot in own], axis=1)
+            right = jnp.concatenate([decoder_t[k] for k, slot in own], axis=0)
+            picked.append(gather_slots(matmul(left, right), index))
+        else:
+            picked.append(jnp.zeros(index.shape, BF))
     z_ref[...] = fold_slots(join_layers(picked, index, width), layers * slab_most)
     head_ref[...] = matmul(act_t[places[0][0]], residue[places[0][1]])
 

time: 37.7 us -> 37.7 us (level)
  no operation moved by 1% of the time
where the time goes in v11:
time: 37.7 us; the launch traced here: 37.4 us
  starting transfers between devices  10.7 us (28%)
  blocking collectives  9.74 us (26%)
  Pallas kernels  7.96 us (21%)
  waiting for transfers between devices  7.53 us (20%)
  between operations  0.73 us (2%)
  local copies, waits for them, and re-layouts  0.72 us (2%)
    all_to_all x1, blocking collectives, share(): return lax.all_to_all(copies, axis, 0, 0, tiled=True)  9.74 us
    pallas_call x6, Pallas kernels, call(): pl.pallas_call(kernel, out_shape=tuple(((pltpu.HBM if spec is HBM else pl...  7.96 us
    all_to_all x1, starting transfers between devices, share(): return lax.all_to_all(copies, axis, 0, 0, tiled=True)  7.29 us
    all_to_all x1, waiting for transfers between devices, share(): return lax.all_to_all(copies, axis, 0, 0, tiled=True)  6.09 us
    ppermute x4, starting transfers between devices, across(): return lax.ppermute(value, axis, pairs)  3.38 us
    ppermute x4, waiting for transfers between devices, across(): return lax.ppermute(value, axis, pairs)  1.44 us
  transfers between devices with their start and end apart: 5, of which 2 were waited for; matrix products, arithmetic and copies ran while one was open for 0% of the time, Pallas kernels for 6%

profile of v11, /device:TPU:0, one launch (start us, length us, event | category | flops | bytes accessed | tf_op | source)
XLA Modules:
  0.0 37.4 jit_solution(17845901886927642393)
XLA Ops:
  0.6 0.0 copy-start
  0.6 2.0 %shard_map.94 = (bf16[64,128]{1,0:T(8,128)(2,1)S(1)}, s16[128,128]{1,0:T(8,128)(2,1)S(1)}, s32[64,128]{1,0:T(8,128)S(1)}) custom-call(bf16[128,2,256]{2,1,0:T(2,128)(2,1)} %x_ref.1, bf16[2,256,1024]{2,1,0:T(8,128)(2,1)} %encoder_hbm.1, f32[2,1024]{1,0:T(2,128)} %bias_hbm.1, s32[128,128]{1,0:T(8,128)} %bitcast.11), custom_call_target="tpu_custom_call" | custom-call | tf_op jit(solution)/shard_map/pallas_call | solution.py:306
  2.6 0.0 copy-start.1
  2.7 0.0 copy-start.2
  2.7 0.7 %broadcast_in_dim.6 = bf16[8,64,128]{2,1,0:T(8,128)(2,1)} broadcast(bf16[64,128]{1,0:T(8,128)(2,1)S(1)} %get-tuple-element.29), dimensions={1,2} | broadcast | bytes 147456 | tf_op jit(solution)/shard_map/broadcast_in_dim | solution.py:320
  3.3 7.3 %all-to-all-start = ((bf16[8,64,128]{2,1,0:T(8,128)(2,1)}), bf16[8,64,128]{2,1,0:T(8,128)(2,1)S(1)}, u32[]{:S(2)}, u32[]{:S(2)}) async-start(bf16[8,64,128]{2,1,0:T(8,128)(2,1)} %broadcast_in_dim.6), calls=%async_computation | async-start | bytes 262144 | tf_op jit(solution)/shard_map/all_to_all | solution.py:321
  10.6 1.3 %shard_map.95.inverse_ref = s16[2,128,1024]{2,1,0:T(8,128)(2,1)S(1)} custom-call(s32[64,128]{1,0:T(8,128)S(1)} %get-tuple-element.30.kept_ref), custom_call_target="tpu_custom_call" | custom-call | flops 100000000 | bytes 1000000 | tf_op jit(solution)/shard_map/pallas_call | solution.py:306
  11.9 6.1 %all-to-all-done.parts_ref = bf16[8,64,128]{2,1,0:T(8,128)(2,1)S(1)} async-done(((bf16[8,64,128]{2,1,0:T(8,128)(2,1)}), bf16[8,64,128]{2,1,0:T(8,128)(2,1)S(1)}, u32[]{:S(2)}, u32[]{:S(2)}) %all-to-all-start) | async-done | bytes 131104 | tf_op jit(solution)/shard_map/all_to_all | solution.py:321
  18.0 0.0 copy-done
  18.0 0.6 %shard_map.96 = (bf16[2,128,1024]{2,1,0:T(8,128)(2,1)S(1)}, f32[128,256]{1,0:T(8,128)S(1)}, f32[128,256]{1,0:T(8,128)S(1)}, bf16[128,256]{1,0:T(8,128)(2,1)S(1)}...) custom-call(bf16[8,64,128]{2,1,0:T(8,128)(2,1)S(1)} %all-to-all-done.parts_ref, ...), custom_call_target="tpu_custom_call" | custom-call | tf_op jit(solution)/shard_map/pallas_call | solution.py:306
  18.5 0.0 copy-start.3
  18.6 0.1 collective-permute-start
  18.6 1.6 %collective-permute-start.1 = (bf16[128,256]{1,0:T(8,128)(2,1)S(1)}, bf16[128,256]{1,0:T(8,128)(2,1)S(1)}, u32[]{:S(2)}, u32[]{:S(2)}) collective-permute-start(bf16[128,256]{1,0:T(8,128)(2,1)S(1)} %get-tuple-element.35), channel_id=1, source_target_pairs={{0,3},{1,2},{2,1},{3,0},{4,7},{5,6},{6,5},{7,4},{8,11},{9,10},{10,... | collective-permute-start | bytes 196616 | tf_op jit(solution)/shard_map/ppermute | solution.py:333
  20.2 0.0 collective-permute-done
  20.3 1.2 %collective-permute-start.2 = (bf16[128,256]{1,0:T(8,128)(2,1)S(1)}, bf16[128,256]{1,0:T(8,128)(2,1)S(1)}, u32[]{:S(2)}, u32[]{:S(2)}) collective-permute-start(bf16[128,256]{1,0:T(8,128)(2,1)S(1)} %get-tuple-element.37), channel_id=1, source_target_pairs={{0,2},{1,3},{2,0},{3,1},{4,6},{5,7},{6,4},{7,5},{8,10},{9,11},{10,... | collective-permute-start | bytes 196616 | tf_op jit(solution)/shard_map/ppermute | solution.py:333
  21.4 0.0 copy-done.1
  21.4 1.1 %shard_map.97 = (bf16[2,1024,128]{2,1,0:T(8,128)(2,1)S(1)}, bf16[2,256,128]{2,1,0:T(8,128)(2,1)S(1)}, bf16[2,128,256]{2,1,0:T(8,128)(2,1)S(1)}, bf16[3,256,1024]{2,1,0:T(8,128)(2,1)S(1)}) custom-call(bf16[2,128,1024]{2,1,0:T(8,128)(2,1)S(1)} %get-tuple-element.38.act_ref, bf16[128,2,256]{2,1,0:T(2,128)(2,1)S(1)} %copy-done.1, ...), custom_call_target="tpu_custom_call" | custom-call | flops 100000000 | bytes 10000000 | tf_op jit(solution)/shard_map/pallas_call | solution.py:306
  22.6 0.0 collective-permute-done.1
  22.6 0.5 %collective-permute-start.3 = (bf16[128,256]{1,0:T(8,128)(2,1)S(1)}, bf16[128,256]{1,0:T(8,128)(2,1)S(1)}, u32[]{:S(2)}, u32[]{:S(2)}) collective-permute-start(bf16[128,256]{1,0:T(8,128)(2,1)S(1)} %get-tuple-element.43), channel_id=1, source_target_pairs={{0,1},{1,0},{2,3},{3,2},{4,5},{5,4},{6,7},{7,6},{8,9},{9,8},{10,11... | collective-permute-start | bytes 196616 | tf_op jit(solution)/shard_map/ppermute | solution.py:333
  23.1 1.4 %collective-permute-done.2.theirs_a = bf16[128,256]{1,0:T(8,128)(2,1)S(1)} collective-permute-done((bf16[128,256]{1,0:T(8,128)(2,1)S(1)}, bf16[128,256]{1,0:T(8,128)(2,1)S(1)}, u32[]{:S(2)}, u32[]{:S(2)}) %collective-permute-start.2) | collective-permute-done | bytes 65568 | tf_op jit(solution)/shard_map/ppermute | solution.py:333
  24.6 0.0 collective-permute-done.3.theirs_b
  24.6 0.5 %shard_map.98 = (bf16[64,128]{1,0:T(8,128)(2,1)S(1)}, bf16[2,128,256]{2,1,0:T(8,128)(2,1)S(1)}, f32[1024,256]{1,0:T(8,128)S(1)}) custom-call(f32[128,256]{1,0:T(8,128)S(1)} %get-tuple-element.58.mine_a, f32[128,256]{1,0:T(8,128)S(1)} %get-tuple-element.56.mine_b, bf16[128,256]{1,0:T(8,128)(2,1)S(1)} %collective-permute-done.2.theirs_a, ...), custom_call_target="tpu_custom_call" | custom-call | tf_op jit(solution)/shard_map/pallas_call | solution.py:306
  25.2 9.7 %all_to_all.10.parts_ref = bf16[8,64,128]{2,1,0:T(8,128)(2,1)S(1)} all-to-all(bf16[8,64,128]{2,1,0:T(8,128)(2,1)S(1)} %broadcast_in_dim.7), channel_id=1, replica_groups=mesh['layer'=8,'lat'=4] {'layer'}, dimensions={0} | all-to-all | bytes 262144 | tf_op jit(solution)/shard_map/all_to_all | solution.py:321
  34.9 2.5 %shard_map.99 = (f32[3,1024,256]{2,1,0:T(8,128)}, f32[2,256,1024]{2,1,0:T(8,128)}, f32[2,1024]{1,0:T(2,128)}) custom-call(bf16[8,64,128]{2,1,0:T(8,128)(2,1)S(1)} %all_to_all.10.parts_ref, s16[2,128,1024]{2,1,0:T(8,128)(2,1)S(1)} %shard_map.95.inverse_ref, bf16[2,256,128]{2,1,0:T(8,128)(2,1)S(1)} %get-tuple-element.49.x_t, ...), custom_call_target="tpu_custom_call" | custom-call | tf_op jit(solution)/shard_map/pallas_call | solution.py:306
  (5 shorter events, 0.1 us)
Async XLA Ops:
  0.6 17.3 %copy-start = (bf16[1,3,1024,256]{3,2,1,0:T(8,128)(2,1)S(1)}, bf16[1,3,1024,256]{3,2,1,0:T(8,128)(2,1)}, u32[]{:S(2)}) copy-start(bf16[1,3,1024,256]{3,2,1,0:T(8,128)(2,1)} %param.10) | copy-start | bytes 4718596
  2.6 18.8 %copy-start.1 = (bf16[128,2,256]{2,1,0:T(2,128)(2,1)S(1)}, bf16[128,2,256]{2,1,0:T(2,128)(2,1)}, u32[]{:S(2)}) copy-start(bf16[128,2,256]{2,1,0:T(2,128)(2,1)} %x_ref.1) | copy-start | bytes 393220
  2.7 18.8 %copy-start.2 = (bf16[1,128,2,256]{3,2,1,0:T(2,128)(2,1)S(1)}, bf16[1,128,2,256]{3,2,1,0:T(2,128)(2,1)}, u32[]{:S(2)}) copy-start(bf16[1,128,2,256]{3,2,1,0:T(2,128)(2,1)} %param.12) | copy-start | bytes 393220
  3.3 14.6 %all-to-all-start = ((bf16[8,64,128]{2,1,0:T(8,128)(2,1)}), bf16[8,64,128]{2,1,0:T(8,128)(2,1)S(1)}, u32[]{:S(2)}, u32[]{:S(2)}) async-start(bf16[8,64,128]{2,1,0:T(8,128)(2,1)} %broadcast_in_dim.6), calls=%async_computation | async-start | bytes 262144 | tf_op jit(solution)/shard_map/all_to_all | solution.py:321
  18.5 6.1 %copy-start.3 = (f32[1,2,256]{2,1,0:T(2,128)S(1)}, f32[1,2,256]{2,1,0:T(2,128)}, u32[]{:S(2)}) copy-start(f32[1,2,256]{2,1,0:T(2,128)} %param.11) | copy-start | bytes 6148
  18.6 1.7 %collective-permute-start = (bf16[128,256]{1,0:T(8,128)(2,1)S(1)}, bf16[128,256]{1,0:T(8,128)(2,1)S(1)}, u32[]{:S(2)}, u32[]{:S(2)}) collective-permute-start(bf16[128,256]{1,0:T(8,128)(2,1)S(1)} %get-tuple-element.33), channel_id=1, source_target_pairs={{0,1},{1,0},{2,3},{3,2},{4,5},{5,4},{6,7},{7,6},{8,9},{9,8},{10,11... | collective-permute-start | bytes 196616 | tf_op jit(solution)/shard_map/ppermute | solution.py:333
  18.6 4.0 %collective-permute-start.1 = (bf16[128,256]{1,0:T(8,128)(2,1)S(1)}, bf16[128,256]{1,0:T(8,128)(2,1)S(1)}, u32[]{:S(2)}, u32[]{:S(2)}) collective-permute-start(bf16[128,256]{1,0:T(8,128)(2,1)S(1)} %get-tuple-element.35), channel_id=1, source_target_pairs={{0,3},{1,2},{2,1},{3,0},{4,7},{5,6},{6,5},{7,4},{8,11},{9,10},{10,... | collective-permute-start | bytes 196616 | tf_op jit(solution)/shard_map/ppermute | solution.py:333
  20.3 4.3 %collective-permute-start.2 = (bf16[128,256]{1,0:T(8,128)(2,1)S(1)}, bf16[128,256]{1,0:T(8,128)(2,1)S(1)}, u32[]{:S(2)}, u32[]{:S(2)}) collective-permute-start(bf16[128,256]{1,0:T(8,128)(2,1)S(1)} %get-tuple-element.37), channel_id=1, source_target_pairs={{0,2},{1,3},{2,0},{3,1},{4,6},{5,7},{6,4},{7,5},{8,10},{9,11},{10,... | collective-permute-start | bytes 196616 | tf_op jit(solution)/shard_map/ppermute | solution.py:333
  22.6 2.0 %collective-permute-start.3 = (bf16[128,256]{1,0:T(8,128)(2,1)S(1)}, bf16[128,256]{1,0:T(8,128)(2,1)S(1)}, u32[]{:S(2)}, u32[]{:S(2)}) collective-permute-start(bf16[128,256]{1,0:T(8,128)(2,1)S(1)} %get-tuple-element.43), channel_id=1, source_target_pairs={{0,1},{1,0},{2,3},{3,2},{4,5},{5,4},{6,7},{7,6},{8,9},{9,8},{10,11... | collective-permute-start | bytes 196616 | tf_op jit(solution)/shard_map/ppermute | solution.py:333
